TPU v7x, 128 devices: a whole 4x4x4 slice. The times are simulated.
128 devices in a mesh: seq: 32 (over x, z, core), head: 4 (over y).
Axes of the slice: x: 4, y: 4, z: 4, core: 2. Of those that a mesh axis runs over, the one named last changes fastest.
Arguments:
- queries: bfloat16 [24576, 8192], P('seq', 'head'), may hold values from -3 to 3
- keys: bfloat16 [24576, 8192], P('seq', 'head'), may hold values from -3 to 3
- values: bfloat16 [24576, 8192], P('seq', 'head'), may hold values from -13 to 13
- log_decay: float32 [64, 24576], P('head', 'seq'), may hold values from -1 to 0, as said below
- gain: float32 [8192], P('head'), may hold values from 0.25 to 1.75
- grad_out: bfloat16 [24576, 8192], P('seq', 'head'), may hold values from -5 to 5
Outputs:
- output: bfloat16 [24576, 8192], P('seq', 'head')
- grad_queries: bfloat16 [24576, 8192], P('seq', 'head')
- grad_keys: bfloat16 [24576, 8192], P('seq', 'head')
- grad_values: bfloat16 [24576, 8192], P('seq', 'head')
- grad_gain: float32 [8192], P('head')
Inputs may be any that keep to these rules, and one draw needn't show every extreme that they name: `log_decay`: every entry is negative.
All inputs are finite; a program needn't handle non-finite values.
Results may differ from a plain program's by a relative error of at most 0.012.
Values sent between devices are 32-bit elements; how exact they have to be, the bound alone decides.
No kernel may reach another device: no remote copies, remote signals or barrier semaphores. Data moves between devices by JAX's collectives and lax.ppermute only.
A program may use at most 192 MiB of HBM per device.

v0:
```python
import jax
import jax.numpy as jnp
from jax import lax
from jax.sharding import PartitionSpec as P

HEAD_TOTAL = 64
DH = 128
SPAN = 128


def entering_2(part, axis, combine, identity, reverse):
    count = lax.axis_size(axis)
    place = lax.axis_index(axis)
    ahead = count - 1 - place if reverse else place
    gathered = jax.tree.map(lambda a: lax.all_gather(a, axis), part)
    state = jax.tree.map(lambda a, e: jnp.zeros_like(a) + jnp.asarray(e, a.dtype), part, identity)

    def one(lap, state):
        source = count - 1 - lap if reverse else lap
        return combine(
            state, jax.tree.map(lambda a: lax.dynamic_index_in_dim(a, source, 0, False), gathered)
        )

    return lax.fori_loop(0, ahead, one, state)


def combine_states(earlier, later):
    return (earlier[0] * later[0], later[0][:, None, None] * earlier[1] + later[1])


def per_device(queries, keys, values, log_decay, gain, grad_out):
    rows_here, width_here = queries.shape
    heads_here = log_decay.shape[0]
    head_size = width_here // heads_here
    block_count = rows_here // SPAN
    query_blocks = queries.reshape(block_count, SPAN, heads_here, head_size)
    key_blocks = keys.reshape(block_count, SPAN, heads_here, head_size)
    value_blocks = values.reshape(block_count, SPAN, heads_here, head_size)
    cumulative = jnp.cumsum(log_decay.reshape(heads_here, block_count, SPAN), axis=2)
    block_logs = cumulative[:, :, -1]
    places = jnp.arange(SPAN)
    triangle = places[:, None] >= places[None, :]
    diffs = cumulative[:, :, :, None] - cumulative[:, :, None, :]
    decays = jnp.where(triangle, jnp.exp(jnp.minimum(diffs, 0.0)), 0.0)
    query_scale = jnp.exp(cumulative).transpose(1, 2, 0)[..., None]
    key_scale = jnp.exp(block_logs[:, :, None] - cumulative).transpose(1, 2, 0)[..., None]
    scores = jnp.einsum(
        "nihd,njhd->hnij", query_blocks, key_blocks, preferred_element_type=jnp.float32
    )
    weights = (scores * decays).astype(jnp.bfloat16)
    query_decayed = (query_blocks * query_scale).astype(jnp.bfloat16)
    key_decayed = (key_blocks * key_scale).astype(jnp.bfloat16)
    updates = jnp.einsum(
        "nihd,nihe->nhde", key_decayed, value_blocks, preferred_element_type=jnp.float32
    )
    state_now = jnp.zeros((heads_here, head_size, head_size), jnp.float32)
    local_in = []
    for number in range(block_count):
        local_in.append(state_now)
        state_now = jnp.exp(block_logs[:, number])[:, None, None] * state_now + updates[number]
    local_in = jnp.stack(local_in)
    total_log = jnp.sum(block_logs, axis=1)
    carry_factor = jnp.exp(total_log)
    identity = (jnp.ones_like(carry_factor), jnp.zeros_like(state_now))
    _, entering = entering_2((carry_factor, state_now), "seq", combine_states, identity, False)
    before = jnp.cumsum(block_logs, axis=1) - block_logs
    state_in = local_in + jnp.exp(before).T[:, :, None, None] * entering[None]
    state_low = state_in.astype(jnp.bfloat16)
    attn_sum = jnp.einsum(
        "hnij,njhe->nihe", weights, value_blocks, preferred_element_type=jnp.float32
    )
    attn_sum = attn_sum + jnp.einsum(
        "nihd,nhde->nihe", query_decayed, state_low, preferred_element_type=jnp.float32
    )
    attention = attn_sum.astype(jnp.bfloat16).reshape(rows_here, width_here)
    attn_float = attention.astype(jnp.float32)
    square_sum = lax.psum(jnp.sum(attn_float * attn_float, axis=1), "head")
    inverse = lax.rsqrt(square_sum / (HEAD_TOTAL * DH) + 1e-06)[:, None]
    normed = attn_float * inverse
    output = (normed * gain).astype(jnp.bfloat16)
    grad_float = grad_out.astype(jnp.float32)
    grad_normed = grad_float * gain
    grad_gain = lax.psum(jnp.sum(grad_float * normed, axis=0), "seq")
    inner_sum = lax.psum(jnp.sum(grad_normed * normed, axis=1), "head")
    grad_attn = (
        inverse * (grad_normed - normed * (inner_sum / (HEAD_TOTAL * DH))[:, None])
    ).astype(jnp.bfloat16)
    grad_blocks = grad_attn.reshape(block_count, SPAN, heads_here, head_size)
    qgrad_terms = jnp.einsum(
        "nihd,nihe->nhde", query_decayed, grad_blocks, preferred_element_type=jnp.float32
    )
    state_back = jnp.zeros_like(state_now)
    local_out = [None] * block_count
    for number in reversed(range(block_count)):
        local_out[number] = state_back
        state_back = (
            jnp.exp(block_logs[:, number])[:, None, None] * state_back + qgrad_terms[number]
        )
    local_out = jnp.stack(local_out)
    _, leaving = entering_2((carry_factor, state_back), "seq", combine_states, identity, True)
    later_logs = total_log[:, None] - jnp.cumsum(block_logs, axis=1)
    state_grad = (local_out + jnp.exp(later_logs).T[:, :, None, None] * leaving[None]).astype(
        jnp.bfloat16
    )
    grad_weights = jnp.einsum(
        "nihe,njhe->hnij", grad_blocks, value_blocks, preferred_element_type=jnp.float32
    )
    grad_weights = (grad_weights * decays).astype(jnp.bfloat16)
    grad_query = jnp.einsum(
        "hnij,njhd->nihd", grad_weights, key_blocks, preferred_element_type=jnp.float32
    )
    grad_query = grad_query + query_scale * jnp.einsum(
        "nihe,nhde->nihd", grad_blocks, state_low, preferred_element_type=jnp.float32
    )
    grad_key = jnp.einsum(
        "hnij,nihd->njhd", grad_weights, query_blocks, preferred_element_type=jnp.float32
    )
    grad_key = grad_key + key_scale * jnp.einsum(
        "njhe,nhde->njhd", value_blocks, state_grad, preferred_element_type=jnp.float32
    )
    grad_value = jnp.einsum(
        "hnij,nihe->njhe", weights, grad_blocks, preferred_element_type=jnp.float32
    )
    grad_value = grad_value + jnp.einsum(
        "njhd,nhde->njhe", key_decayed, state_grad, preferred_element_type=jnp.float32
    )
    return (
        output,
        grad_query.astype(jnp.bfloat16).reshape(rows_here, width_here),
        grad_key.astype(jnp.bfloat16).reshape(rows_here, width_here),
        grad_value.astype(jnp.bfloat16).reshape(rows_here, width_here),
        grad_gain,
    )


def solution(mesh):
    placed = (
        P("seq", "head"),
        P("seq", "head"),
        P("seq", "head"),
        P("head", "seq"),
        P("head"),
        P("seq", "head"),
    )
    return jax.shard_map(
        per_device,
        mesh=mesh,
        in_specs=placed,
        out_specs=(
            P("seq", "head"),
            P("seq", "head"),
            P("seq", "head"),
            P("seq", "head"),
            P("head"),
        ),
        check_vma=False,
    )
```

profile of v0, /device:TPU:1, one launch (start us, length us, event | category | flops | bytes accessed | tf_op | source)
XLA Modules:
  0.0 530.4 jit_solution(11531480908536895590)
XLA Ops:
  10.1 3.1 copy.107
  14.3 6.6 %fusion.34 = f32[6,16,128,128]{3,2,1,0:T(8,128)S(1)} fusion(bf16[6,128,16,128]{3,2,1,0:T(8,128)(2,1)S(1)} %bitcast.120, f32[6,128,16]{1,2,0:T(8,128)S(1)} %get-tuple-element.168, bf16[6,128,16,128]{3,2,1,0:T(8,128)(2,1)S(1)} %bitcast.124), kind=kOutput, calls=%fused_computation.55 | convolution fusion | flops 407371776 | bytes 12632064 | tf_op jit(solution)/shard_map/nihd,nihe->nhde/dot_general | solution.py:53
  28.5 4.6 copy.105
  34.4 65.9 %all-reduce = f32[512]{0:T(512)S(1)} all-reduce(f32[512]{0:T(512)S(1)} %exponential_dynamic-update-slice_fusion), channel_id=2, replica_groups=mesh['seq'=32,'head'=4] {'seq'}, use_global_device_ids=true, to_apply=%add | all-reduce | flops 512 | bytes 4096
  103.0 3.1 fusion.48
  111.0 5.2 multiply_convert_fusion.4
  116.2 30.5 %all-gather.4.cloned.1.call-done = f32[32,16,128,128]{3,2,1,0:T(8,128)} async-done(((f32[1,16,128,128]{3,2,1,0:T(8,128)}), f32[32,16,128,128]{3,2,1,0:T(8,128)}) %all-gather.4.cloned.1.call-update) | async-done | bytes 33554448 | tf_op jit(solution)/shard_map/all_gather | solution.py:15
  150.6 6.5 %fusion.37 = f32[6,16,128,128]{3,2,1,0:T(8,128)S(1)} fusion(f32[6,128,16]{1,2,0:T(8,128)S(1)} %get-tuple-element.169, bf16[6,128,16,128]{3,2,1,0:T(8,128)(2,1)} %bitcast.130, f32[6,16,128,128]{3,2,1,0:T(8,128)} %fusion.49, f32[16,128,128]{2,1,0:T(8,128)} %get-tuple-element.133, f32[6,16]{1,0:T(8,128)S(1)} %get-tuple-element.171), kind=kOutput, calls=%fused_computation.58 | convolution fusion | flops 412090368 | bytes 16826752 | tf_op jit(solution)/shard_map/nihd,nhde->nihe/dot_general | solution.py:72
  157.1 5.0 multiply_reduce_fusion
  162.1 6.7 %copy.77 = f32[6,128,16,128]{3,2,1,0:T(8,128)} copy(f32[6,128,16,128]{1,3,2,0:T(8,128)} %get-tuple-element.181) | data formatting | bytes 12582912 | tf_op jit(solution)/shard_map/convert_element_type | solution.py:76
  168.9 8.9 %psum.21 = f32[768]{0:T(1024)S(1)} all-reduce(f32[768]{0:T(1024)S(1)} %bitcast.144), channel_id=1, replica_groups=mesh['seq'=32,'head'=4] {'head'}, use_global_device_ids=true, to_apply=%region_6.7 | all-reduce | flops 768 | bytes 6144 | tf_op jit(solution)/shard_map/psum | solution.py:77
  177.8 6.6 %fusion.5 = (f32[2048]{0:T(1024)S(1)}, f32[768]{0:T(1024)S(1)}) fusion(bf16[768,2048]{1,0:T(8,128)(2,1)S(1)} %copy-done.17, f32[96,8,16,128]{3,2,1,0:T(8,128)} %bitcast.128, f32[768]{0:T(1024)S(1)} %add_rsqrt_fusion, f32[2048]{0:T(1024)S(1)} %copy-done.23), kind=kLoop, calls=%fused_computation.11 | loop fusion | flops 11007232 | bytes 9459712 | tf_op jit(solution)/shard_map/reduce_sum | solution.py:83
  184.3 6.1 %psum.22 = f32[768]{0:T(1024)S(1)} all-reduce(f32[768]{0:T(1024)S(1)} %get-tuple-element.136), channel_id=1, replica_groups=mesh['seq'=32,'head'=4] {'head'}, use_global_device_ids=true, to_apply=%region_8.9 | all-reduce | flops 768 | bytes 6144 | tf_op jit(solution)/shard_map/psum | solution.py:84
  190.4 8.0 %fusion.13 = (bf16[96,8,16,128]{3,1,2,0:T(8,128)(2,1)S(1)}, bf16[768,2048]{1,0:T(8,128)(2,1)}) fusion(f32[96,8,16,128]{3,2,1,0:T(8,128)} %bitcast.129, bf16[768,2048]{1,0:T(8,128)(2,1)} %param.15, f32[768]{0:T(1024)S(1)} %broadcast_multiply_fusion, f32[2048]{0:T(1024)S(1)} %copy-done.23, f32[768]{0:T(1024)S(1)} %add_rsqrt_fusion), kind=kLoop, calls=%fused_computation.33 | loop fusion | flops 14155776 | bytes 15742976
  201.2 3.8 copy.92
  204.9 5.6 %fusion.36 = f32[6,16,128,128]{3,2,1,0:T(8,128)S(1)} fusion(bf16[6,128,16,128]{1,3,2,0:T(8,128)(2,1)S(1)} %copy.92, f32[6,128,16]{1,2,0:T(8,128)S(1)} %get-tuple-element.169, bf16[6,128,16,128]{3,2,1,0:T(8,128)(2,1)} %bitcast.131), kind=kOutput, calls=%fused_computation.57 | convolution fusion | flops 407371776 | bytes 12632064 | tf_op jit(solution)/shard_map/nihd,nihe->nhde/dot_general | solution.py:89
  215.3 5.4 %multiply_convert_fusion = bf16[16,6,128,128]{3,2,1,0:T(8,128)(2,1)S(1)} fusion(f32[16,6,128]{2,1,0:T(8,128)S(1)} %copy.68, pred[128,128]{1,0:T(8,128)(4,1)S(1)} %iota_compare_fusion, bf16[6,128,16,128]{3,2,1,0:T(8,128)(2,1)} %bitcast.122, bf16[6,128,16,128]{3,2,1,0:T(8,128)(2,1)} %bitcast.135), kind=kOutput, calls=%fused_computation.23 | convolution fusion | flops 410517504 | bytes 9502720 | tf_op jit(solution)/shard_map/nihe,njhe->hnij/dot_general | solution.py:105
  223.5 5.8 %fusion.9 = bf16[6,128,16,128]{3,1,2,0:T(8,128)(2,1)S(1)} fusion(f32[6,16,128,128]{3,2,1,0:T(8,128)S(1)} %fusion.22, f32[6,128,16]{1,2,0:T(8,128)S(1)} %get-tuple-element.169, bf16[6,128,16,128]{1,3,2,0:T(8,128)(2,1)S(1)} %copy.92, f32[6,16,128,128]{3,2,1,0:T(8,128)} %fusion.49, f32[16,128,128]{2,1,0:T(8,128)S(1)} %copy-done.8, ...), kind=kOutput, calls=%fused_computation.18 | convolution fusion | flops 412090368 | bytes 19972480 | tf_op jit(solution)/shard_map/nihe,nhde->nihd/dot_general | solution.py:112
  231.4 3.0 copy.174
  234.4 146.6 %psum.23 = f32[2048]{0:T(1024)} all-reduce(f32[2048]{0:T(1024)S(1)} %get-tuple-element.135), channel_id=1, replica_groups=mesh['seq'=32,'head'=4] {'seq'}, use_global_device_ids=true, to_apply=%region_12.13 | all-reduce | flops 2048 | bytes 16384 | tf_op jit(solution)/shard_map/psum | solution.py:83
  380.9 2.9 fusion.51
  386.2 2.8 fusion.50
  393.6 4.2 fusion.26
  398.7 3.9 fusion.20
  402.5 8.6 %all-gather.6.cloned.1.call-done = f32[32,16,128,128]{3,2,1,0:T(8,128)} async-done(((f32[1,16,128,128]{3,2,1,0:T(8,128)}), f32[32,16,128,128]{3,2,1,0:T(8,128)}) %all-gather.6.cloned.1.call-update) | async-done | bytes 33554448 | tf_op jit(solution)/shard_map/all_gather | solution.py:15
  412.3 82.9 %while.27 = (s32[]{:T(128)}, f32[16,128,128]{2,1,0:T(8,128)}, s32[]{:T(128)}, f32[32,16]{1,0:T(8,128)S(1)}, f32[32,16,128,128]{3,2,1,0:T(8,128)}, /*index=5*/s32[]{:T(128)}, s32[]{:T(128)}, s32[]{:T(128)}, s32[]{:T(128)}) while((s32[]{:T(128)}, f32[16,128,128]{2,1,0:T(8,128)}, s32[]{:T(128)}, f32[32,16]{1,0:T(8,128)S(1)}, ...), condition=%wide.region_10.11_spmd, body=%wide.region_9.10_spmd.sunk | while | flops 524294 | bytes 3146075 | solution.py:24
  412.3 2.9 bitcast_add_fusion.6
  415.2 2.8 bitcast_add_fusion.6
  417.9 2.8 bitcast_add_fusion.6
  420.7 2.8 bitcast_add_fusion.6
  423.5 2.8 bitcast_add_fusion.6
  426.2 2.8 bitcast_add_fusion.6
  429.0 2.8 bitcast_add_fusion.6
  434.5 2.8 bitcast_add_fusion.6
  437.2 2.8 bitcast_add_fusion.6
  440.0 2.8 bitcast_add_fusion.6
  442.8 2.8 bitcast_add_fusion.6
  445.5 2.8 bitcast_add_fusion.6
  448.3 2.8 bitcast_add_fusion.6
  451.0 2.8 bitcast_add_fusion.6
  453.8 2.8 bitcast_add_fusion.6
  456.6 2.8 bitcast_add_fusion.6
  459.3 2.8 bitcast_add_fusion.6
  462.1 2.8 bitcast_add_fusion.6
  495.2 8.3 %fusion.11 = bf16[6,128,16,128]{1,3,2,0:T(8,128)(2,1)} fusion(f32[6,16,128,128]{3,2,1,0:T(8,128)} %fusion.26, f32[6,128,16]{1,2,0:T(8,128)S(1)} %get-tuple-element.168, bf16[6,128,16,128]{3,2,1,0:T(8,128)(2,1)S(1)} %bitcast.127, f32[6,16,128,128]{3,2,1,0:T(8,128)} %broadcast_dynamic-update-slice_fusion, f32[16,128,128]{2,1,0:T(8,128)} %get-tuple-element.134, ...), kind=kOutput, calls=%fused_computation.31 | convolution fusion | flops 415236096 | bytes 19972480 | tf_op jit(solution)/shard_map/njhd,nhde->njhe/dot_general | solution.py:124
  503.5 5.0 copy.95
  508.5 6.7 %fusion.7 = bf16[6,128,16,128]{3,1,2,0:T(8,128)(2,1)S(1)} fusion(f32[6,16,128,128]{3,2,1,0:T(8,128)} %fusion.20, f32[6,128,16]{1,2,0:T(8,128)S(1)} %get-tuple-element.168, bf16[6,128,16,128]{3,2,1,0:T(8,128)(2,1)S(1)} %bitcast.123, f32[6,16,128,128]{3,2,1,0:T(8,128)} %broadcast_dynamic-update-slice_fusion, f32[16,128,128]{2,1,0:T(8,128)} %get-tuple-element.134, ...), kind=kOutput, calls=%fused_computation.15 | convolution fusion | flops 412090368 | bytes 19972480 | tf_op jit(solution)/shard_map/njhe,nhde->njhd/dot_general | solution.py:118
  517.3 6.0 %copy_bitcast_fusion = (bf16[768,2048]{1,0:T(8,128)(2,1)}, bf16[768,2048]{1,0:T(8,128)(2,1)}) fusion(bf16[96,8,16,128]{3,2,1,0:T(8,128)(2,1)S(1)} %bitcast.137, bf16[96,8,16,128]{3,2,1,0:T(8,128)(2,1)S(1)} %bitcast.138), kind=kLoop, calls=%fused_computation.34 | loop fusion | bytes 12582912 | tf_op jit(solution)/shard_map/reshape | solution.py:131
  (132 shorter events, 82.9 us)
Async XLA Ops:
  7.2 0.8 copy-start
  7.2 139.5 %all-gather.4.cloned.1.call-start = ((), (), s32[]{:S(2)}) async-start(), calls=%async_computation | async-start | bytes 34603008 | tf_op jit(solution)/shard_map/all_gather | solution.py:15
  9.7 3.6 copy-start.22
  13.3 143.8 %copy-start.2 = (bf16[96,8,16,128]{3,2,1,0:T(8,128)(2,1)}, bf16[96,8,16,128]{3,2,1,0:T(8,128)(2,1)S(1)}, u32[]{:S(2)}) copy-start(bf16[96,8,16,128]{3,2,1,0:T(8,128)(2,1)S(1)} %copy.107) | copy-start | bytes 9437188
  14.3 6.6 %copy-start.4 = (bf16[96,8,16,128]{3,2,1,0:T(8,128)(2,1)}, bf16[96,8,16,128]{3,2,1,0:T(8,128)(2,1)S(1)}, u32[]{:S(2)}) copy-start(bf16[96,8,16,128]{3,2,1,0:T(8,128)(2,1)S(1)} %copy.106) | copy-start | bytes 9437188
  20.9 2.6 copy-start.9
  25.7 2.7 copy-start.13
  28.4 4.7 copy-start.24
  28.4 382.7 %all-gather.6.cloned.1.call-start = ((), (), s32[]{:S(2)}) async-start(), calls=%async_computation.1 | async-start | bytes 34603008 | tf_op jit(solution)/shard_map/all_gather | solution.py:15
  100.4 8.1 %copy-start.20 = (f32[1,16,128,128]{3,2,1,0:T(8,128)S(1)}, f32[1,16,128,128]{3,2,1,0:T(8,128)}, u32[]{:S(2)}) copy-start(f32[1,16,128,128]{3,2,1,0:T(8,128)} %get-tuple-element.163) | copy-start | bytes 3145732
  100.4 10.6 %copy-start.5 = (bf16[96,8,16,128]{3,2,1,0:T(8,128)(2,1)S(1)}, bf16[96,8,16,128]{3,2,1,0:T(8,128)(2,1)}, u32[]{:S(2)}) copy-start(bf16[96,8,16,128]{3,2,1,0:T(8,128)(2,1)} %copy-done.4) | copy-start | bytes 9437188
  100.4 10.6 %copy-start.10 = (bf16[96,8,16,128]{3,2,1,0:T(8,128)(2,1)S(1)}, bf16[96,8,16,128]{3,2,1,0:T(8,128)(2,1)}, u32[]{:S(2)}) copy-start(bf16[96,8,16,128]{3,2,1,0:T(8,128)(2,1)} %copy.105) | copy-start | bytes 9437188
  150.6 6.5 %copy-start.14 = (bf16[16,6,128,128]{3,2,1,0:T(8,128)(2,1)S(1)}, bf16[16,6,128,128]{3,2,1,0:T(8,128)(2,1)}, u32[]{:S(2)}) copy-start(bf16[16,6,128,128]{3,2,1,0:T(8,128)(2,1)} %multiply_convert_fusion.4) | copy-start | bytes 9437188
  162.1 15.6 %copy-start.17 = (bf16[768,2048]{1,0:T(8,128)(2,1)S(1)}, bf16[768,2048]{1,0:T(8,128)(2,1)}, u32[]{:S(2)}) copy-start(bf16[768,2048]{1,0:T(8,128)(2,1)} %param.15) | copy-start | bytes 9437188
  162.1 15.6 %copy-start.23 = (f32[2048]{0:T(1024)S(1)}, f32[2048]{0:T(1024)}, u32[]{:S(2)}) copy-start(f32[2048]{0:T(1024)} %param.14) | copy-start | bytes 24580
  210.5 2.7 copy-start.12
  215.3 7.0 %copy-start.6 = (bf16[96,8,16,128]{3,2,1,0:T(8,128)(2,1)S(1)}, bf16[96,8,16,128]{3,2,1,0:T(8,128)(2,1)}, u32[]{:S(2)}) copy-start(bf16[96,8,16,128]{3,2,1,0:T(8,128)(2,1)} %copy-done.4) | copy-start | bytes 9437188
  220.7 1.6 copy-start.18
  222.3 1.2 copy-start.8
  380.9 8.0 %copy-start.21 = (f32[1,16,128,128]{3,2,1,0:T(8,128)S(1)}, f32[1,16,128,128]{3,2,1,0:T(8,128)}, u32[]{:S(2)}) copy-start(f32[1,16,128,128]{3,2,1,0:T(8,128)} %get-tuple-element.161) | copy-start | bytes 3145732
  380.9 12.7 %copy-start.15 = (bf16[16,6,128,128]{3,2,1,0:T(8,128)(2,1)S(1)}, bf16[16,6,128,128]{3,2,1,0:T(8,128)(2,1)}, u32[]{:S(2)}) copy-start(bf16[16,6,128,128]{3,2,1,0:T(8,128)(2,1)} %multiply_convert_fusion.4) | copy-start | bytes 9437188
  393.6 4.2 copy-start.11
  393.6 5.0 copy-start.19
  412.3 82.9 %copy-start.7 = (bf16[96,8,16,128]{3,2,1,0:T(8,128)(2,1)S(1)}, bf16[96,8,16,128]{3,2,1,0:T(8,128)(2,1)}, u32[]{:S(2)}) copy-start(bf16[96,8,16,128]{3,2,1,0:T(8,128)(2,1)} %copy-done.4) | copy-start | bytes 9437188
  503.5 5.0 copy-start.3
  515.2 2.1 copy-start.16
  517.3 6.0 %copy-start.1 = (f32[16,768]{1,0:T(8,128)S(1)}, f32[16,768]{1,0:T(8,128)}, u32[]{:S(2)}) copy-start(f32[16,768]{1,0:T(8,128)} %param.13) | copy-start | bytes 147460
Sparse Core Ops, SparseCore 0:
  28.5 118.1 all-gather.3
  215.4 195.6 all-gather.5
where the time goes:
time: 540 us; the launch traced here: 530 us
  blocking collectives  227 us (42%)
  other arithmetic  120 us (22%)
  local copies, waits for them, and re-layouts  64.4 us (12%)
  matrix products  64.1 us (12%)
  waiting for transfers between devices  39.1 us (7%)
  between operations  15.3 us (3%)
    psum x1, blocking collectives, per_device(): grad_gain = lax.psum(jnp.sum(grad_float * normed, axis=0), 'seq')  147 us
    add x31, other arithmetic, combine_states(): later[0][:, None, None] * earlier[1] + later[1]  85.4 us
    unnamed x1, blocking collectives  65.9 us
    all_gather x2, waiting for transfers between devices, entering_2(): gathered = jax.tree.map(lambda a: lax.all_gather(a, axis), part)  39.1 us
    unnamed x63, local copies, waits for them, and re-layouts  35 us
    unnamed x5, other arithmetic  19.3 us
  transfers between devices with their start and end apart: 2, of which 2 were waited for; matrix products, arithmetic and copies ran while one was open for 11% of the time, Pallas kernels for 0%

commit v1 on v0

v1 whole, which is shorter than its diff:
```python
import functools

import jax
import jax.numpy as jnp
from jax import lax
from jax.experimental import pallas as pl
from jax.experimental.pallas import tpu as pltpu
from jax.sharding import PartitionSpec as P

HEAD_TOTAL = 64
DH = 128
SPAN = 128
HALF = DH // 2
ROWS = 8
PIECE = HALF + ROWS
GROUP = 4
F32 = jnp.float32
BF16 = jnp.bfloat16
EXACT = lax.Precision.HIGHEST
VMEM = pl.BlockSpec(memory_space=pltpu.VMEM)
SMEM = pl.BlockSpec(memory_space=pltpu.SMEM)
HBM = pl.BlockSpec(memory_space=pltpu.HBM)
ANY = pl.BlockSpec(memory_space=pl.ANY)


def dot(a, b, contract, precision=None):
    return lax.dot_general(
        a, b, ((contract[:1], contract[1:]), ((), ())), precision=precision, preferred_element_type=F32
    )


def nn(a, b):
    return dot(a, b, (1, 0))


def nt(a, b):
    return dot(a, b, (1, 1))


def params(mib):
    return pltpu.CompilerParams(vmem_limit_bytes=mib * 1024 * 1024)


def cost(flops, nbytes):
    return pl.CostEstimate(flops=int(flops), bytes_accessed=int(nbytes), transcendentals=0)


def head_rows(ref, head):
    return ref[pl.ds(pl.multiple_of(head * ROWS, ROWS), ROWS), :]


def head_lanes(head, count=1):
    return pl.ds(pl.multiple_of(head * DH, DH), count * DH)


def span(n):
    return slice(n * SPAN, (n + 1) * SPAN)


def last_lane(rows):
    return jnp.broadcast_to(rows[:, SPAN - 1 :], rows.shape)


def middle_lane(rows):
    return jnp.broadcast_to(rows[:, SPAN // 2 - 1 : SPAN // 2], rows.shape)


def masks():
    i = lax.broadcasted_iota(jnp.int32, (SPAN, SPAN), 0)
    j = lax.broadcasted_iota(jnp.int32, (SPAN, SPAN), 1)
    return i >= j, i <= j


def join_rows(rows, blocks):
    return jnp.concatenate([rows[n : n + 1] for n in range(blocks)], axis=1)


def piece_store(ref, at, state, extra):
    ref[2 * at, :HALF, :] = state[:HALF]
    ref[2 * at, HALF:, :] = extra
    ref[2 * at + 1, :HALF, :] = state[HALF:]
    ref[2 * at + 1, HALF:, :] = extra


def piece_state(keep_ref, taken_ref, at, half):
    kept = at < half
    place = 2 * jnp.where(kept, at, at - half)
    low = jnp.where(kept, keep_ref[place, :HALF, :], taken_ref[place, :HALF, :])
    high = jnp.where(kept, keep_ref[place + 1, :HALF, :], taken_ref[place + 1, :HALF, :])
    return jnp.concatenate([low, high], axis=0)


def extra_rows(decay, gain_row=None):
    place = lax.broadcasted_iota(jnp.int32, (ROWS, DH), 0)
    rest = 0.0 if gain_row is None else jnp.where(place == 1, gain_row, 0.0)
    return jnp.where(place == 0, decay, rest)


def state_body(core_ref, log_ref, k_hbm, v_hbm, send_ref, own_ref, cum_ref, before_ref, total_ref, k_ref, v_ref, sems):
    heads, rows = log_ref.shape
    blocks, half = rows // SPAN, heads // 2
    core = core_ref[0]
    copies = []
    for g in range(heads // GROUP):
        first = lax.rem((1 - core) * half + g * GROUP, heads)
        lanes = head_lanes(first, GROUP)
        pair = [
            pltpu.make_async_copy(k_hbm.at[:, lanes], k_ref.at[:, lanes], sems.at[0, g]),
            pltpu.make_async_copy(v_hbm.at[:, lanes], v_ref.at[:, lanes], sems.at[1, g]),
        ]
        for copy in pair:
            copy.start()
        copies.append((first, pair))

    _, triangle = masks()
    triangle = triangle.astype(F32)
    cum_ref[...] = jnp.zeros_like(cum_ref)
    before_ref[...] = jnp.zeros_like(before_ref)
    before = jnp.zeros((heads, SPAN), F32)
    for n in range(blocks):
        cum = dot(log_ref[:, span(n)], triangle, (1, 0), EXACT)
        for h in range(heads):
            cum_ref[h * ROWS + n : h * ROWS + n + 1, :] = cum[h : h + 1]
            before_ref[h * ROWS + n : h * ROWS + n + 1, :] = before[h : h + 1]
        before = before + last_lane(cum)
    for h in range(heads):
        total_ref[h * ROWS : (h + 1) * ROWS, :] = jnp.broadcast_to(before[h : h + 1], (ROWS, SPAN))

    for g, (first, pair) in enumerate(copies):
        for copy in pair:
            copy.wait()
        for at in range(GROUP):
            head = first + at
            lanes = head_lanes(head)
            total = head_rows(total_ref, head)
            scale = jnp.exp(total - head_rows(before_ref, head) - head_rows(cum_ref, head))
            decayed = (k_ref[:, lanes].T.astype(F32) * join_rows(scale, blocks)).astype(BF16)
            state = nn(decayed, v_ref[:, lanes])
            place = (g * GROUP + at) % half
            piece_store(send_ref if g * GROUP < half else own_ref, place, state, extra_rows(jnp.exp(total)))


def local_state(core, log_decay, keys, values):
    heads, rows = log_decay.shape
    pieces = jax.ShapeDtypeStruct((heads, PIECE, DH), F32)
    table = jax.ShapeDtypeStruct((heads * ROWS, SPAN), F32)
    like = jax.ShapeDtypeStruct(keys.shape, BF16)
    return pl.pallas_call(
        state_body,
        in_specs=[SMEM, VMEM, HBM, HBM],
        out_specs=[VMEM] * 7,
        out_shape=[pieces, pieces, table, table, table, like, like],
        scratch_shapes=[pltpu.SemaphoreType.DMA((2, heads // GROUP))],
        compiler_params=params(8),
        cost_estimate=cost(2 * heads * rows * DH * DH, 4 * rows * heads * DH),
        name="local_state",
    )(core, log_decay, keys, values)


def scan_body(reverse, in_ref, after_ref, out_ref):
    count = in_ref.shape[0]
    state = jnp.zeros((HALF, DH), F32)
    extra = jnp.zeros((ROWS, DH), F32)
    for lap in range(count):
        at = count - 1 - lap if reverse else lap
        out_ref[at, :HALF, :] = state
        state = in_ref[at, HALF : HALF + 1, :] * state + in_ref[at, :HALF, :]
        extra = extra + in_ref[at, HALF:, :]
    for at in range(count):
        out_ref[at, HALF:, :] = extra


def scan_pieces(pieces, after, reverse):
    count = pieces.shape[0]
    return pl.pallas_call(
        functools.partial(scan_body, reverse),
        in_specs=[VMEM, ANY],
        out_specs=VMEM,
        out_shape=jax.ShapeDtypeStruct(pieces.shape, F32),
        compiler_params=params(8),
        cost_estimate=cost(2 * count * HALF * DH, 8 * count * HALF * DH),
        name="scan_pieces",
    )(pieces, after)


def scan_over_seq(send, own, core, reverse, during_out, during_back):
    count = lax.axis_size("seq")
    chips = [list(range(c, count, 2)) for c in range(2)]
    pairs = [(i, i ^ 1) for i in range(count)]
    got = lax.ppermute(send, "seq", pairs)
    near_here = jnp.logical_xor(core == 0, reverse)
    near = jnp.where(near_here, own, got)
    far = jnp.where(near_here, got, own)
    row = lax.broadcasted_iota(jnp.int32, (1, PIECE, 1), 1)
    both = jnp.where(row <= HALF, far[:, HALF : HALF + 1], 1.0) * near + jnp.where(row == HALF, 0.0, far)
    shared = lax.all_to_all(both, "seq", 0, 0, axis_index_groups=chips)
    meanwhile = during_out(both)
    scanned = scan_pieces(shared, meanwhile[-1], reverse)
    entering = lax.all_to_all(scanned, "seq", 0, 0, axis_index_groups=chips)
    meanwhile = during_back(scanned, meanwhile)
    passed = jnp.where(row < HALF, near[:, HALF : HALF + 1] * entering + near, entering)
    keep = jnp.where(near_here, entering, passed)
    give = jnp.where(near_here, passed, entering)
    taken = lax.ppermute(give, "seq", pairs)
    return keep, taken, meanwhile


def attend_body(first_head, count, loads, *refs):
    _, k_ref, v_ref, cum_ref, before_ref = refs[:5]
    refs = refs[5:]
    blocks = k_ref.shape[0] // SPAN
    if loads:
        q_hbm, local_ref, low_ref, turned_ref, q_ref, q_sems = refs
        copies = []
        for g in range(q_hbm.shape[1] // (GROUP * DH)):
            lanes = slice(g * GROUP * DH, (g + 1) * GROUP * DH)
            copies.append(pltpu.make_async_copy(q_hbm.at[:, lanes], q_ref.at[:, lanes], q_sems.at[g]))
            copies[-1].start()
    else:
        q_ref, go_hbm, _, _, _, local_ref, low_ref, turned_ref, go_ref, go_sem = refs
        go_copy = pltpu.make_async_copy(go_hbm, go_ref, go_sem)
        go_copy.start()
    mask, _ = masks()

    def one(head):
        lanes = head_lanes(head)
        cum = head_rows(cum_ref, head)
        end, mid = last_lane(cum), middle_lane(cum)
        before = head_rows(before_ref, head)
        query_col = jnp.exp(cum - mid).T
        key_col = jnp.exp(mid - cum).T
        query_row = jnp.exp(cum + before)
        mid_scale, end_scale, rest_scale = jnp.exp(mid), jnp.exp(end), jnp.exp(end - mid)
        q_up = [(q_ref[span(n), lanes].astype(F32) * query_col[:, n : n + 1]).astype(BF16) for n in range(blocks)]
        k_up = [(k_ref[span(n), lanes].astype(F32) * key_col[:, n : n + 1]).astype(BF16) for n in range(blocks)]
        turned_ref[head] = (q_ref[:, lanes].T.astype(F32) * join_rows(query_row, blocks)).astype(BF16)
        weights = [jnp.where(mask, nt(q_up[n], k_up[n]), 0.0).astype(BF16) for n in range(blocks)]
        updates = [nn(k_up[n].T, v_ref[span(n), lanes]) for n in range(blocks - 1)]
        state = jnp.zeros((DH, DH), F32)
        lows = []
        for n in range(blocks):
            lows.append((mid_scale[n : n + 1] * state).astype(BF16))
            low_ref[head, n] = lows[n]
            if n < blocks - 1:
                state = end_scale[n : n + 1] * state + rest_scale[n : n + 1] * updates[n]
        for n in range(blocks):
            total = nn(
                jnp.concatenate([weights[n], q_up[n]], axis=1),
                jnp.concatenate([v_ref[span(n), lanes], lows[n]], axis=0),
            )
            local_ref[span(n), lanes] = total.astype(BF16)

    if loads:
        for g, copy in enumerate(copies):
            copy.wait()
            if g * GROUP < count:

                @pl.loop(0, GROUP)
                def _(at):
                    one(first_head + g * GROUP + at)
    else:

        @pl.loop(0, count)
        def _(at):
            one(first_head + at)

        go_copy.wait()


def attend_first(after, keys, values, cum, before, queries):
    rows, width = keys.shape
    heads, blocks = width // DH, rows // SPAN
    like = jax.ShapeDtypeStruct((rows, width), BF16)
    return pl.pallas_call(
        functools.partial(attend_body, 0, heads // 2, True),
        in_specs=[ANY, VMEM, VMEM, VMEM, VMEM, HBM],
        out_specs=[VMEM] * 4,
        out_shape=[
            like,
            jax.ShapeDtypeStruct((heads, blocks, DH, DH), BF16),
            jax.ShapeDtypeStruct((heads, DH, rows), BF16),
            like,
        ],
        scratch_shapes=[pltpu.SemaphoreType.DMA((heads // GROUP,))],
        compiler_params=params(8),
        cost_estimate=cost(5 * rows * width * DH, 6 * rows * width),
        name="attend_first",
    )(after, keys, values, cum, before, queries)


def attend_second(after, keys, values, cum, before, queries, grad_out, local, lows, turned):
    rows, width = keys.shape
    heads = width // DH
    return pl.pallas_call(
        functools.partial(attend_body, heads // 2, heads // 2, False),
        in_specs=[ANY, VMEM, VMEM, VMEM, VMEM, VMEM, HBM, VMEM, VMEM, VMEM],
        out_specs=[VMEM] * 4,
        out_shape=[jax.ShapeDtypeStruct(a.shape, a.dtype) for a in (local, lows, turned, grad_out)],
        input_output_aliases={7: 0, 8: 1, 9: 2},
        scratch_shapes=[pltpu.SemaphoreType.DMA],
        compiler_params=params(8),
        cost_estimate=cost(5 * rows * width * DH, 6 * rows * width),
        name="attend_second",
    )(after, keys, values, cum, before, queries, grad_out, local, lows, turned)


def enter_body(core_ref, q_ref, local_ref, go_ref, gain_ref, keep_ref, taken_ref, cum_ref, before_ref,
               attn_ref, low_ref, stats_ref, square_ref, inner_ref):
    rows, width = q_ref.shape
    heads, blocks = width // DH, rows // SPAN
    half = heads // 2
    core = core_ref[0]
    square_ref[...] = jnp.zeros_like(square_ref)
    inner_ref[...] = jnp.zeros_like(inner_ref)

    @pl.loop(0, heads // GROUP)
    def _(g):
        first = lax.rem(core * half + g * GROUP, heads)
        lows, scales, gains = [], [], []
        for at in range(GROUP):
            low = piece_state(keep_ref, taken_ref, g * GROUP + at, half).astype(BF16)
            low_ref[first + at] = low
            lows.append(low)
            scales.append(jnp.exp(head_rows(cum_ref, first + at) + head_rows(before_ref, first + at)).T)
            gains.append(gain_ref[:, head_lanes(first + at)])
        for n in range(blocks):
            square = jnp.zeros((SPAN, DH), F32)
            inner = jnp.zeros((SPAN, DH), F32)
            for at in range(GROUP):
                lanes = head_lanes(first + at)
                carried = nn(q_ref[span(n), lanes], lows[at]) * scales[at][:, n : n + 1]
                attn = (local_ref[span(n), lanes].astype(F32) + carried).astype(BF16)
                attn_ref[span(n), lanes] = attn
                attn = attn.astype(F32)
                square += attn * attn
                inner += go_ref[span(n), lanes].astype(F32) * gains[at] * attn
            square_ref[span(n), :] += square
            inner_ref[span(n), :] += inner

    ones = jnp.ones((8, DH), F32)
    stats_ref[0:1, :] = dot(ones, square_ref[...], (1, 1), EXACT)[0:1]
    stats_ref[1:2, :] = dot(ones, inner_ref[...], (1, 1), EXACT)[0:1]


def attend_entering(core, queries, local, grad_out, gain, keep, taken, cum, before):
    rows, width = queries.shape
    heads = width // DH
    return pl.pallas_call(
        enter_body,
        in_specs=[SMEM] + [VMEM] * 8,
        out_specs=[VMEM] * 3,
        out_shape=[
            jax.ShapeDtypeStruct((rows, width), BF16),
            jax.ShapeDtypeStruct((heads, DH, DH), BF16),
            jax.ShapeDtypeStruct((2, rows), F32),
        ],
        scratch_shapes=[pltpu.VMEM((rows, DH), F32), pltpu.VMEM((rows, DH), F32)],
        compiler_params=params(8),
        cost_estimate=cost(2 * rows * width * DH, 8 * rows * width),
        name="attend_entering",
    )(core, queries, local, grad_out, gain, keep, taken, cum, before)


def columns(row, ref, blocks):
    for n in range(blocks):
        ref[span(n), :] = jnp.broadcast_to(row[:, span(n)], (SPAN, SPAN)).T


def inverse_row(stats_ref):
    return lax.rsqrt(stats_ref[0:1, :] / (HEAD_TOTAL * DH) + 1e-06)


def norm_body(core_ref, turned_ref, attn_ref, go_ref, gain_ref, stats_ref, total_ref, ga_ref, send_ref, own_ref, inverse_ref,
              factor_ref):
    rows, width = attn_ref.shape
    heads, blocks = width // DH, rows // SPAN
    half = heads // 2
    core = core_ref[0]
    inverse = inverse_row(stats_ref)
    columns(inverse, inverse_ref, blocks)
    columns(inverse * inverse * inverse * (stats_ref[1:2, :] / (HEAD_TOTAL * DH)), factor_ref, blocks)

    for out, offset in ((send_ref, 0), (own_ref, half)):

        @pl.loop(0, half // 2)
        def _(g):
            for at in range(2):
                place = 2 * g + at
                head = lax.rem((1 - core) * half + offset + place, heads)
                lanes = head_lanes(head)
                gain = gain_ref[:, lanes]
                gain_sum = jnp.zeros((8, DH), F32)
                grads = []
                for n in range(blocks):
                    attn = attn_ref[span(n), lanes].astype(F32)
                    scaled = go_ref[span(n), lanes].astype(F32) * inverse_ref[span(n), :]
                    gain_sum += jnp.sum((scaled * attn).reshape(SPAN // 8, 8, DH), axis=0)
                    grad = (scaled * gain - attn * factor_ref[span(n), :]).astype(BF16)
                    ga_ref[span(n), lanes] = grad
                    grads.append(grad)
                state = nn(turned_ref[head], jnp.concatenate(grads, axis=0))
                extra = extra_rows(jnp.exp(head_rows(total_ref, head)), jnp.sum(gain_sum, axis=0, keepdims=True))
                piece_store(out, place, state, extra)


def norm_backward(core, turned, attn, grad_out, gain, stats, total):
    rows, width = attn.shape
    heads = width // DH
    pieces = jax.ShapeDtypeStruct((heads, PIECE, DH), F32)
    return pl.pallas_call(
        norm_body,
        in_specs=[SMEM] + [VMEM] * 6,
        out_specs=[VMEM] * 3,
        out_shape=[jax.ShapeDtypeStruct((rows, width), BF16), pieces, pieces],
        scratch_shapes=[pltpu.VMEM((rows, DH), F32), pltpu.VMEM((rows, DH), F32)],
        compiler_params=params(8),
        cost_estimate=cost(2 * rows * width * DH, 8 * rows * width),
        name="norm_backward",
    )(core, turned, attn, grad_out, gain, stats, total)


def grads_body(first_head, count, chained, *refs):
    _, q_ref, k_ref, v_ref, ga_ref, attn_ref, gain_ref, stats_ref, low_ref, enter_ref, cum_ref, before_ref = refs[:12]
    refs = refs[12 + (4 if chained else 0) :]
    out_hbm, gq_hbm, lk_ref, lv_ref, out_ref, gq_ref, inverse_ref, sems = refs
    blocks = q_ref.shape[0] // SPAN
    mask, turned_mask = masks()
    columns(inverse_row(stats_ref), inverse_ref, blocks)

    def one(head, place):
        lanes, here = head_lanes(head), head_lanes(place)
        cum = head_rows(cum_ref, head)
        end, mid = last_lane(cum), middle_lane(cum)
        query_col = jnp.exp(cum - mid).T
        key_col = jnp.exp(mid - cum).T
        mid_scale, end_scale, rest_scale = jnp.exp(mid), jnp.exp(end), jnp.exp(end - mid)
        enter_scale = jnp.exp(mid + head_rows(before_ref, head))
        entering = enter_ref[head].astype(F32)
        gain = gain_ref[:, lanes]
        q_up = [(q_ref[span(n), lanes].astype(F32) * query_col[:, n : n + 1]).astype(BF16) for n in range(blocks)]
        updates = [nn(q_up[n].T, ga_ref[span(n), lanes]) for n in range(blocks)]
        back = jnp.zeros((DH, DH), F32)
        lows = [None] * blocks
        for n in reversed(range(blocks)):
            lows[n] = (rest_scale[n : n + 1] * back).astype(BF16)
            if n > 0:
                back = end_scale[n : n + 1] * back + mid_scale[n : n + 1] * updates[n]
        for n in range(blocks):
            k, v, ga = k_ref[span(n), lanes], v_ref[span(n), lanes], ga_ref[span(n), lanes]
            k_up = (k.astype(F32) * key_col[:, n : n + 1]).astype(BF16)
            out_ref[span(n), here] = (attn_ref[span(n), lanes].astype(F32) * inverse_ref[span(n), :] * gain).astype(BF16)
            scores = jnp.where(mask, nt(ga, v), 0.0).astype(BF16)
            turned_scores = jnp.where(turned_mask, nt(v, ga), 0.0).astype(BF16)
            turned_weights = jnp.where(turned_mask, nt(k_up, q_up[n]), 0.0).astype(BF16)
            state = (low_ref[head, n].astype(F32) + enter_scale[n : n + 1] * entering).astype(BF16)
            grad_q = (nn(scores, k_up) + nt(ga, state)) * query_col[:, n : n + 1]
            gq_ref[span(n), here] = grad_q.astype(BF16)
            grad_k = (nn(turned_scores, q_up[n]) + nt(v, lows[n])) * key_col[:, n : n + 1]
            lk_ref[span(n), lanes] = grad_k.astype(BF16)
            grad_v = nn(
                jnp.concatenate([turned_weights, k_up], axis=1), jnp.concatenate([ga, lows[n]], axis=0)
            )
            lv_ref[span(n), lanes] = grad_v.astype(BF16)

    copies = []
    for g in range(count // GROUP):

        @pl.loop(0, GROUP)
        def _(at):
            one(first_head + g * GROUP + at, g * GROUP + at)

        here = slice(g * GROUP * DH, (g + 1) * GROUP * DH)
        there = slice((first_head + g * GROUP) * DH, (first_head + (g + 1) * GROUP) * DH)
        for which, (source, target) in enumerate(((out_ref, out_hbm), (gq_ref, gq_hbm))):
            copies.append(pltpu.make_async_copy(source.at[:, here], target.at[:, there], sems.at[which, g]))
            copies[-1].start()
    for copy in copies:
        copy.wait()


def grads_local(after, first_head, count, inputs, chained):
    rows, width = inputs[0].shape
    like = jax.ShapeDtypeStruct((rows, width), BF16)
    kinds = [HBM, HBM, VMEM, VMEM]
    return pl.pallas_call(
        functools.partial(grads_body, first_head, count, bool(chained)),
        in_specs=[ANY] + [VMEM] * 11 + (kinds if chained else []),
        out_specs=kinds,
        out_shape=[like] * 4,
        input_output_aliases={12 + i: i for i in range(4)} if chained else {},
        scratch_shapes=[
            pltpu.VMEM((rows, count * DH), BF16),
            pltpu.VMEM((rows, count * DH), BF16),
            pltpu.VMEM((rows, DH), F32),
            pltpu.SemaphoreType.DMA((2, count // GROUP)),
        ],
        compiler_params=params(12),
        cost_estimate=cost(11 * rows * width * DH, 12 * rows * width),
        name="grads_second" if chained else "grads_first",
    )(after, *inputs, *chained)


def leave_body(core_ref, k_ref, v_ref, lk_ref, lv_ref, keep_ref, taken_ref, cum_ref, before_ref, total_ref,
               gk_hbm, gv_hbm, gg_ref, gk_ref, gv_ref, sems):
    rows, width = k_ref.shape
    heads, blocks = width // DH, rows // SPAN
    half = heads // 2
    core = core_ref[0]
    copies = []
    for g in range(heads // GROUP):
        first = lax.rem(core * half + g * GROUP, heads)

        @pl.loop(0, GROUP)
        def _(at):
            head = first + at
            lanes = head_lanes(head)
            low = piece_state(keep_ref, taken_ref, g * GROUP + at, half).astype(BF16)
            place = 2 * ((g * GROUP) % half + at)
            gg_ref[:, lanes] = (keep_ref if g * GROUP < half else taken_ref)[place, HALF + 1 : HALF + 2, :]
            scale = jnp.exp(head_rows(total_ref, head) - head_rows(before_ref, head) - head_rows(cum_ref, head)).T
            for n in range(blocks):
                factor = scale[:, n : n + 1]
                grad_k = lk_ref[span(n), lanes].astype(F32) + factor * nt(v_ref[span(n), lanes], low)
                grad_v = lv_ref[span(n), lanes].astype(F32) + factor * nn(k_ref[span(n), lanes], low)
                gk_ref[span(n), lanes] = grad_k.astype(BF16)
                gv_ref[span(n), lanes] = grad_v.astype(BF16)

        lanes = head_lanes(first, GROUP)
        for which, (source, target) in enumerate(((gk_ref, gk_hbm), (gv_ref, gv_hbm))):
            copies.append(pltpu.make_async_copy(source.at[:, lanes], target.at[:, lanes], sems.at[which, g]))
            copies[-1].start()
    for copy in copies:
        copy.wait()


def grads_leaving(core, keys, values, local_k, local_v, keep, taken, cum, before, total):
    rows, width = keys.shape
    like = jax.ShapeDtypeStruct((rows, width), BF16)
    return pl.pallas_call(
        leave_body,
        in_specs=[SMEM] + [VMEM] * 9,
        out_specs=[HBM, HBM, VMEM],
        out_shape=[like, like, jax.ShapeDtypeStruct((1, width), F32)],
        scratch_shapes=[
            pltpu.VMEM((rows, width), BF16),
            pltpu.VMEM((rows, width), BF16),
            pltpu.SemaphoreType.DMA((2, width // DH // GROUP)),
        ],
        compiler_params=params(12),
        cost_estimate=cost(4 * rows * width * DH, 12 * rows * width),
        name="grads_leaving",
    )(core, keys, values, local_k, local_v, keep, taken, cum, before, total)


def per_device(queries, keys, values, log_decay, gain, grad_out):
    core = lax.rem(lax.axis_index("seq"), 2)
    core_arg = core.astype(jnp.int32).reshape(1)
    gain_row = gain.reshape(1, -1)
    heads = log_decay.shape[0]
    send, own, cum, before, total, keys, values = local_state(core_arg, log_decay, keys, values)

    def attend_out(after):
        return attend_first(after, keys, values, cum, before, queries)

    def attend_back(after, done):
        local, lows, turned, held = done
        return (*attend_second(after, keys, values, cum, before, held, grad_out, local, lows, turned), held)

    keep, taken, (local, lows, turned, grad_out, queries) = scan_over_seq(
        send, own, core, False, attend_out, attend_back
    )
    attn, entering, stats = attend_entering(
        core_arg, queries, local, grad_out, gain_row, keep, taken, cum, before
    )
    stats = lax.psum(stats, "head")
    grad_attn, send, own = norm_backward(core_arg, turned, attn, grad_out, gain_row, stats, total)
    inputs = (queries, keys, values, grad_attn, attn, gain_row, stats, lows, entering, cum, before)

    def grads_out(after):
        return grads_local(after, 0, heads // 2, inputs, ())

    def grads_back(after, done):
        return grads_local(after, heads // 2, heads // 2, inputs, done)

    keep, taken, (output, grad_q, local_k, local_v) = scan_over_seq(send, own, core, True, grads_out, grads_back)
    grad_k, grad_v, grad_gain = grads_leaving(
        core_arg, keys, values, local_k, local_v, keep, taken, cum, before, total
    )
    return output, grad_q, grad_k, grad_v, grad_gain.reshape(-1)


def solution(mesh):
    tokens, heads = P("seq", "head"), P("head")
    return jax.shard_map(
        per_device,
        mesh=mesh,
        in_specs=(tokens, tokens, tokens, P("head", "seq"), heads, tokens),
        out_specs=(tokens, tokens, tokens, tokens, heads),
        check_vma=False,
    )
```

time: 540 us -> 240 us (0.44); the launches traced: 530 us -> 237 us
  blocking collectives: 227 us -> 8.79 us
  other arithmetic: 120 us -> 9.43 us
  Pallas kernels: 0 us -> 73.7 us
  matrix products: 64.1 us -> 0 us
  starting transfers between devices: 0.08 us -> 32.8 us
  local copies, waits for them, and re-layouts: 64.4 us -> 86.9 us
  waiting for transfers between devices: 39.1 us -> 24.4 us
  between operations: 15.3 us -> 1.09 us
    psum x3 -> x1, blocking collectives: 162 us -> 8.79 us  [per_device(): stats = lax.psum(stats, 'head')]
    add x33 -> x2, other arithmetic: 89.6 us -> 4.37 us  [scan_over_seq(): jnp.where(row <= HALF, far[:, HALF:HALF + 1], 1.0) * near]
    pallas_call x0 -> x10, Pallas kernels: none -> 73.7 us  [the longest x2 32.2 us: grads_local(): pl.pallas_call(functools.partial(grads_body, first_head, count, bool(chai...]
    unnamed x1 -> x0, blocking collectives: 65.9 us -> none
    dot_general x12 -> x0, matrix products: 64.1 us -> none  [the longest x1 8.31 us: per_device(): jnp.einsum('njhd,nhde->njhe', key_decayed, state_grad, preferred_element_...]
    unnamed x63 -> x112, local copies, waits for them, and re-layouts: 35 us -> 85.2 us
    all_gather x2 -> x0, waiting for transfers between devices: 39.1 us -> none  [entering_2(): gathered = jax.tree.map(lambda a: lax.all_gather(a, axis), part)]
    all_to_all x0 -> x4, starting transfers between devices: none -> 25.2 us  [the longest x2 13.1 us: scan_over_seq(): entering = lax.all_to_all(scanned, 'seq', 0, 0, axis_index_groups=chips)]
  transfers between devices with their start and end apart: 2 -> 8, of which waited for: 2 -> 4; matrix products, arithmetic and copies ran while one was open for 11% -> 1% of each run, Pallas kernels for 0% -> 20%
where the time goes in v1:
time: 240 us; the launch traced here: 237 us
  local copies, waits for them, and re-layouts  86.9 us (36%)
  Pallas kernels  73.7 us (31%)
  starting transfers between devices  32.8 us (14%)
  waiting for transfers between devices  24.4 us (10%)
  other arithmetic  9.43 us (4%)
  blocking collectives  8.79 us (4%)
    unnamed x112, local copies, waits for them, and re-layouts  85.2 us
    pallas_call x2, Pallas kernels, grads_local(): pl.pallas_call(functools.partial(grads_body, first_head, count, bool(chai...  32.2 us
    all_to_all x2, waiting for transfers between devices, scan_over_seq(): entering = lax.all_to_all(scanned, 'seq', 0, 0, axis_index_groups=chips)  20.4 us
    all_to_all x2, starting transfers between devices, scan_over_seq(): entering = lax.all_to_all(scanned, 'seq', 0, 0, axis_index_groups=chips)  13.1 us
    all_to_all x2, starting transfers between devices, scan_over_seq(): shared = lax.all_to_all(both, 'seq', 0, 0, axis_index_groups=chips)  12.2 us
    psum x1, blocking collectives, per_device(): stats = lax.psum(stats, 'head')  8.79 us
    pallas_call x1, Pallas kernels, grads_leaving(): pl.pallas_call(leave_body, in_specs=[SMEM] + [VMEM] * 9, out_specs=[HBM,...  8.41 us
    pallas_call x1, Pallas kernels, attend_first(): pl.pallas_call(functools.partial(attend_body, 0, heads // 2, True), in_sp...  8.04 us
  transfers between devices with their start and end apart: 8, of which 4 were waited for; matrix products, arithmetic and copies ran while one was open for 1% of the time, Pallas kernels for 20%

profile of v1, /device:TPU:1, one launch (start us, length us, event | category | flops | bytes accessed | tf_op | source)
XLA Modules:
  0.0 237.2 jit_solution(1803328330627695975)
XLA Ops:
  0.6 1.9 copy-done.46
  2.5 1.9 copy-done.47
  5.2 5.3 %local_state.1 = (f32[16,72,128]{2,1,0:T(8,128)}, f32[16,72,128]{2,1,0:T(8,128)S(1)}, f32[128,128]{1,0:T(8,128)S(1)}, f32[128,128]{1,0:T(8,128)S(1)}, f32[128,12...) custom-call(s32[1]{0:T(128)} %bitcast.core_ref, f32[16,768]{1,0:T(8,128)S(1)} %copy-done.55, ...), custom_call_target="tpu_custom_call" | custom-call | flops 402653184 | bytes 6291456 | tf_op jit(solution)/shard_map/local_state/pallas_call | solution.py:148
  14.4 2.0 collective-permute-done
  17.6 2.2 select_add_fusion.1
  19.7 7.7 %all-to-all-start = ((f32[16,72,128]{2,1,0:T(8,128)}), f32[16,72,128]{2,1,0:T(8,128)}, u32[]{:S(2)}, u32[]{:S(2)}) async-start(f32[16,72,128]{2,1,0:T(8,128)} %get-tuple-element.71.refs_0_), calls=%async_computation | async-start | bytes 1179648 | tf_op jit(solution)/shard_map/all_to_all | solution.py:196
  30.4 1.9 copy-done.45
  32.3 8.0 %attend_first.1 = (bf16[768,2048]{1,0:T(8,128)(2,1)S(1)}, bf16[16,6,128,128]{3,2,1,0:T(8,128)(2,1)S(1)}, bf16[16,128,768]{2,1,0:T(8,128)(2,1)S(1)}, bf16[768,2048]{1,0:T(8,128)(2,1)S(1)}) custom-call(f32[16,72,128]{2,1,0:T(8,128)S(1)} %copy-done.42, bf16[768,2048]{1,0:T(8,128)(2,1)S(1)} %get-tuple-element.39.refs_1_.refs_2_.k_ref, ...), custom_call_target="tpu_custom_call" | custom-call | flops 1006632960 | bytes 9437184 | tf_op jit(solution)/shard_map/attend_first/pallas_call | solution.py:274
  47.0 1.9 copy-done.7
  50.8 6.7 %all-to-all-start.1 = ((f32[16,72,128]{2,1,0:T(8,128)}), f32[16,72,128]{2,1,0:T(8,128)}, u32[]{:S(2)}, u32[]{:S(2)}) async-start(f32[16,72,128]{2,1,0:T(8,128)} %copy-done.39), calls=%async_computation.1 | async-start | bytes 1179648 | tf_op jit(solution)/shard_map/all_to_all | solution.py:199
  58.4 10.2 %all-to-all-done.1 = f32[16,72,128]{2,1,0:T(8,128)} async-done(((f32[16,72,128]{2,1,0:T(8,128)}), f32[16,72,128]{2,1,0:T(8,128)}, u32[]{:S(2)}, u32[]{:S(2)}) %all-to-all-start.1) | async-done | bytes 589856 | tf_op jit(solution)/shard_map/all_to_all | solution.py:199
  69.9 2.2 collective-permute-start.1
  72.2 1.9 copy-done.2
  74.1 1.9 copy-done.8
  76.0 1.9 copy-done.20
  77.8 1.9 copy-done.32
  79.7 1.9 copy-done.36
  82.7 1.9 copy-done.48
  84.6 7.5 %attend_second.1 = (bf16[768,2048]{1,0:T(8,128)(2,1)S(1)}, bf16[16,6,128,128]{3,2,1,0:T(8,128)(2,1)S(1)}, bf16[16,128,768]{2,1,0:T(8,128)(2,1)S(1)}, bf16[768,2048]{1,0:T(8,128)(2,1)S(1)}) custom-call(f32[16,72,128]{2,1,0:T(8,128)S(1)} %copy-done.40, ...), custom_call_target="tpu_custom_call", output_to_operand_aliasing={{0}: (7, {}), {1}: (8, {}), {2}: (9, {})} | custom-call | flops 1006632960 | bytes 9437184 | tf_op jit(solution)/shard_map/attend_second/pallas_call | solution.py:294
  97.1 3.0 %copy-done.34 = bf16[768,2048]{1,0:T(8,128)(2,1)S(1)} copy-done((bf16[768,2048]{1,0:T(8,128)(2,1)S(1)}, bf16[768,2048]{1,0:T(8,128)(2,1)}, u32[]{:S(2)}) %copy-start.34) | copy-done | bytes 3145752
  100.1 4.9 %attend_entering.1 = (bf16[768,2048]{1,0:T(8,128)(2,1)S(1)}, bf16[16,128,128]{2,1,0:T(8,128)(2,1)S(1)}, f32[2,768]{1,0:T(2,128)S(1)}) custom-call(s32[1]{0:T(128)} %bitcast.core_ref, bf16[768,2048]{1,0:T(8,128)(2,1)S(1)} %copy-done.9, bf16[768,2048]{1,0:T(8,128)(2,1)S(1)} %copy-done.34, bf16[768,2048]{1,0:T(8,128)(2,1)S(1)} %get-tuple-element.49.go_ref, ...), custom_call_target="tpu_custom_call" | custom-call | flops 402653184 | bytes 12582912 | tf_op jit(solution)/shard_map/attend_entering/pallas_call | solution.py:348
  107.5 8.8 %psum.7.stats_ref.refs_7_ = f32[2,768]{1,0:T(2,128)S(1)} all-reduce(f32[2,768]{1,0:T(2,128)S(1)} %get-tuple-element.51), channel_id=1, replica_groups=mesh['seq'=32,'head'=4] {'head'}, use_global_device_ids=true, to_apply=%region_0.1 | all-reduce | flops 1536 | bytes 12288 | tf_op jit(solution)/shard_map/psum | solution.py:575
  116.3 1.9 copy-done.16
  118.2 1.9 copy-done.30
  120.1 1.9 copy-done.38
  122.0 5.1 %norm_backward.1 = (bf16[768,2048]{1,0:T(8,128)(2,1)S(1)}, f32[16,72,128]{2,1,0:T(8,128)}, f32[16,72,128]{2,1,0:T(8,128)S(1)}) custom-call(s32[1]{0:T(128)} %bitcast.core_ref, bf16[16,128,768]{2,1,0:T(8,128)(2,1)S(1)} %copy-done.38, bf16[768,2048]{1,0:T(8,128)(2,1)S(1)} %copy-done.16, bf16[768,2048]{1,0:T(8,128)(2,1)S(1)} %copy-done.30, ...), custom_call_target="tpu_custom_call" | custom-call | flops 402653184 | bytes 12582912 | tf_op jit(solution)/shard_map/norm_backward/pallas_call | solution.py:410
  129.6 2.0 collective-permute-start.2
  131.7 2.0 collective-permute-done.2
  134.8 2.2 select_add_fusion
  137.0 4.4 %all-to-all-start.2 = ((f32[16,72,128]{2,1,0:T(8,128)}), f32[16,72,128]{2,1,0:T(8,128)}, u32[]{:S(2)}, u32[]{:S(2)}) async-start(f32[16,72,128]{2,1,0:T(8,128)} %get-tuple-element.69.refs_0_), calls=%async_computation.2 | async-start | bytes 1179648 | tf_op jit(solution)/shard_map/all_to_all | solution.py:196
  143.3 1.9 copy-done.10
  145.2 1.9 copy-done.17
  147.1 1.9 copy-done.22
  149.0 1.9 copy-done.27
  153.0 16.1 %grads_first.1 = (bf16[768,2048]{1,0:T(8,128)(2,1)}, bf16[768,2048]{1,0:T(8,128)(2,1)}, bf16[768,2048]{1,0:T(8,128)(2,1)S(1)}, bf16[768,2048]{1,0:T(8,128)(2,1)S(1)}) custom-call(f32[16,72,128]{2,1,0:T(8,128)S(1)} %copy-done.41, bf16[768,2048]{1,0:T(8,128)(2,1)S(1)} %copy-done.10, bf16[768,2048]{1,0:T(8,128)(2,1)S(1)} %get-tuple-element.39.refs_1_.refs_2_.k_ref, ...), custom_call_target="tpu_custom_call" | custom-call | flops 2214592512 | bytes 18874368 | tf_op jit(solution)/shard_map/grads_first/pallas_call | solution.py:485
  172.5 1.9 copy-done.13
  176.3 6.4 %all-to-all-start.3 = ((f32[16,72,128]{2,1,0:T(8,128)}), f32[16,72,128]{2,1,0:T(8,128)}, u32[]{:S(2)}, u32[]{:S(2)}) async-start(f32[16,72,128]{2,1,0:T(8,128)} %copy-done.43), calls=%async_computation.3 | async-start | bytes 1179648 | tf_op jit(solution)/shard_map/all_to_all | solution.py:199
  183.6 10.2 %all-to-all-done.3 = f32[16,72,128]{2,1,0:T(8,128)} async-done(((f32[16,72,128]{2,1,0:T(8,128)}), f32[16,72,128]{2,1,0:T(8,128)}, u32[]{:S(2)}, u32[]{:S(2)}) %all-to-all-start.3) | async-done | bytes 589856 | tf_op jit(solution)/shard_map/all_to_all | solution.py:199
  195.2 1.9 collective-permute-start.3
  197.1 1.9 copy-done.4
  199.0 1.9 copy-done.11
  200.9 1.9 copy-done.14
  202.8 1.9 copy-done.18
  204.7 1.9 copy-done.23
  206.6 1.9 copy-done.25
  208.5 1.9 copy-done.28
  212.5 16.1 %grads_second.1 = (bf16[768,2048]{1,0:T(8,128)(2,1)}, bf16[768,2048]{1,0:T(8,128)(2,1)}, bf16[768,2048]{1,0:T(8,128)(2,1)S(1)}, bf16[768,2048]{1,0:T(8,128)(2,1)S(1)}) custom-call(f32[16,72,128]{2,1,0:T(8,128)S(1)} %copy-done.44, bf16[768,2048]{1,0:T(8,128)(2,1)S(1)} %copy-done.11, ...), custom_call_target="tpu_custom_call", output_to_operand_aliasing={{0}: (12, {}), {1}: (13, {}), {2}: (14, {}), {3}: (15, {})} | custom-call | flops 2214592512 | bytes 18874368 | tf_op jit(solution)/shard_map/grads_second/pallas_call | solution.py:485
  228.6 8.4 %grads_leaving.1 = (bf16[768,2048]{1,0:T(8,128)(2,1)}, bf16[768,2048]{1,0:T(8,128)(2,1)}, f32[1,2048]{1,0:T(1,128)}) custom-call(s32[1]{0:T(128)} %bitcast.core_ref, bf16[768,2048]{1,0:T(8,128)(2,1)S(1)} %get-tuple-element.39.refs_1_.refs_2_.k_ref, bf16[768,2048]{1,0:T(8,128)(2,1)S(1)} %copy-done.5, bf16[768,2048]{1,0:T(8,128)(2,1)S(1)} %get-tuple-element.64.lk_ref, ...), custom_call_target="tpu_custom_call" | custom-call | flops 805306368 | bytes 18874368 | tf_op jit(solution)/shard_map/grads_leaving/pallas_call | solution.py:539
  (103 shorter events, 45.5 us)
Async XLA Ops:
  0.6 1.9 copy-start.46
  2.5 1.9 copy-start.47
  10.5 1.7 copy-start
  13.0 3.4 %collective-permute-start = (f32[16,72,128]{2,1,0:T(8,128)}, f32[16,72,128]{2,1,0:T(8,128)}, u32[]{:S(2)}, u32[]{:S(2)}) collective-permute-start(f32[16,72,128]{2,1,0:T(8,128)} %get-tuple-element.37), channel_id=1, source_target_pairs={{0,4},{4,0},{8,12},{12,8},{16,20},{20,16},{24,28},{28,24},{32,36},... | collective-permute-start | bytes 1769480 | tf_op jit(solution)/shard_map/ppermute | solution.py:190
  19.7 27.3 %all-to-all-start = ((f32[16,72,128]{2,1,0:T(8,128)}), f32[16,72,128]{2,1,0:T(8,128)}, u32[]{:S(2)}, u32[]{:S(2)}) async-start(f32[16,72,128]{2,1,0:T(8,128)} %get-tuple-element.71.refs_0_), calls=%async_computation | async-start | bytes 1179648 | tf_op jit(solution)/shard_map/all_to_all | solution.py:196
  27.5 1.9 copy-start.1
  30.4 1.9 copy-start.45
  40.4 1.7 copy-start.6
  42.0 1.7 copy-start.19
  43.7 1.7 copy-start.31
  47.0 1.9 copy-start.7
  50.8 17.7 %all-to-all-start.1 = ((f32[16,72,128]{2,1,0:T(8,128)}), f32[16,72,128]{2,1,0:T(8,128)}, u32[]{:S(2)}, u32[]{:S(2)}) async-start(f32[16,72,128]{2,1,0:T(8,128)} %copy-done.39), calls=%async_computation.1 | async-start | bytes 1179648 | tf_op jit(solution)/shard_map/all_to_all | solution.py:199
  69.9 27.1 %collective-permute-start.1 = (f32[16,72,128]{2,1,0:T(8,128)S(1)}, f32[16,72,128]{2,1,0:T(8,128)S(1)}, u32[]{:S(2)}, u32[]{:S(2)}) collective-permute-start(f32[16,72,128]{2,1,0:T(8,128)S(1)} %get-tuple-element.75), channel_id=1, source_target_pairs={{0,4},{4,0},{8,12},{12,8},{16,20},{20,16},{24,28},{28,24},{32,36},... | collective-permute-start | bytes 1769480 | tf_op jit(solution)/shard_map/ppermute | solution.py:204
  72.2 1.9 copy-start.2
  74.1 1.9 copy-start.8
  76.0 1.9 copy-start.20
  77.8 1.9 copy-start.32
  79.7 1.9 copy-start.36
  82.7 1.9 copy-start.48
  84.6 12.5 %copy-start.9 = (bf16[768,2048]{1,0:T(8,128)(2,1)S(1)}, bf16[768,2048]{1,0:T(8,128)(2,1)}, u32[]{:S(2)}) copy-start(bf16[768,2048]{1,0:T(8,128)(2,1)} %copy-done.6) | copy-start | bytes 9437188
  84.6 12.5 %copy-start.54 = (f32[2048]{0:T(1024)S(1)}, f32[2048]{0:T(1024)}, u32[]{:S(2)}) copy-start(f32[2048]{0:T(1024)} %param.10) | copy-start | bytes 24580
  93.7 1.7 copy-start.33
  97.0 8.0 %copy-start.29 = (bf16[768,2048]{1,0:T(8,128)(2,1)}, bf16[768,2048]{1,0:T(8,128)(2,1)S(1)}, u32[]{:S(2)}) copy-start(bf16[768,2048]{1,0:T(8,128)(2,1)S(1)} %get-tuple-element.49.go_ref) | copy-start | bytes 9437188
  97.0 3.0 %copy-start.34 = (bf16[768,2048]{1,0:T(8,128)(2,1)S(1)}, bf16[768,2048]{1,0:T(8,128)(2,1)}, u32[]{:S(2)}) copy-start(bf16[768,2048]{1,0:T(8,128)(2,1)} %copy-done.33) | copy-start | bytes 9437188
  105.0 1.7 copy-start.15
  116.3 1.9 copy-start.16
  118.2 1.9 copy-start.30
  120.1 1.9 copy-start.38
  127.1 1.7 copy-start.26
  129.6 4.0 %collective-permute-start.2 = (f32[16,72,128]{2,1,0:T(8,128)}, f32[16,72,128]{2,1,0:T(8,128)}, u32[]{:S(2)}, u32[]{:S(2)}) collective-permute-start(f32[16,72,128]{2,1,0:T(8,128)} %get-tuple-element.53), channel_id=1, source_target_pairs={{0,4},{4,0},{8,12},{12,8},{16,20},{20,16},{24,28},{28,24},{32,36},... | collective-permute-start | bytes 1769480 | tf_op jit(solution)/shard_map/ppermute | solution.py:190
  137.0 35.5 %all-to-all-start.2 = ((f32[16,72,128]{2,1,0:T(8,128)}), f32[16,72,128]{2,1,0:T(8,128)}, u32[]{:S(2)}, u32[]{:S(2)}) async-start(f32[16,72,128]{2,1,0:T(8,128)} %get-tuple-element.69.refs_0_), calls=%async_computation.2 | async-start | bytes 1179648 | tf_op jit(solution)/shard_map/all_to_all | solution.py:196
  141.4 1.9 copy-start.3
  143.3 1.9 copy-start.10
  145.2 1.9 copy-start.17
  147.1 1.9 copy-start.22
  149.0 1.9 copy-start.27
  170.7 1.8 copy-start.24
  172.5 1.9 copy-start.13
  176.3 17.5 %all-to-all-start.3 = ((f32[16,72,128]{2,1,0:T(8,128)}), f32[16,72,128]{2,1,0:T(8,128)}, u32[]{:S(2)}, u32[]{:S(2)}) async-start(f32[16,72,128]{2,1,0:T(8,128)} %copy-done.43), calls=%async_computation.3 | async-start | bytes 1179648 | tf_op jit(solution)/shard_map/all_to_all | solution.py:199
  195.2 33.4 %collective-permute-start.3 = (f32[16,72,128]{2,1,0:T(8,128)S(1)}, f32[16,72,128]{2,1,0:T(8,128)S(1)}, u32[]{:S(2)}, u32[]{:S(2)}) collective-permute-start(f32[16,72,128]{2,1,0:T(8,128)S(1)} %get-tuple-element.73), channel_id=1, source_target_pairs={{0,4},{4,0},{8,12},{12,8},{16,20},{20,16},{24,28},{28,24},{32,36},... | collective-permute-start | bytes 1769480 | tf_op jit(solution)/shard_map/ppermute | solution.py:204
  197.1 1.9 copy-start.4
  199.0 1.9 copy-start.11
  200.9 1.9 copy-start.14
  202.8 1.9 copy-start.18
  204.7 1.9 copy-start.23
  206.6 1.9 copy-start.25
  208.5 1.9 copy-start.28
  212.5 16.1 %copy-start.5 = (bf16[768,2048]{1,0:T(8,128)(2,1)S(1)}, bf16[768,2048]{1,0:T(8,128)(2,1)}, u32[]{:S(2)}) copy-start(bf16[768,2048]{1,0:T(8,128)(2,1)} %copy-done) | copy-start | bytes 9437188
  (16 other events, 17.7 us)

commit v2 on v1

v2 whole, which is shorter than its diff:
```python
import functools

import jax
import jax.numpy as jnp
from jax import lax
from jax.experimental import pallas as pl
from jax.experimental.pallas import tpu as pltpu
from jax.sharding import PartitionSpec as P

HEAD_TOTAL = 64
DH = 128
SPAN = 128
ROWS = 8
PIECE = DH + ROWS
GROUP = 4
PAIR = 2
ALONG_X, ALONG_Z = 4, 4
F32 = jnp.float32
BF16 = jnp.bfloat16
EXACT = lax.Precision.HIGHEST
VMEM = pl.BlockSpec(memory_space=pltpu.VMEM)
SMEM = pl.BlockSpec(memory_space=pltpu.SMEM)
HBM = pl.BlockSpec(memory_space=pltpu.HBM)
ANY = pl.BlockSpec(memory_space=pl.ANY)


def dot(a, b, contract, precision=None):
    return lax.dot_general(
        a, b, ((contract[:1], contract[1:]), ((), ())), precision=precision, preferred_element_type=F32
    )


def nn(a, b):
    return dot(a, b, (1, 0))


def nt(a, b):
    return dot(a, b, (1, 1))


def params(mib):
    return pltpu.CompilerParams(vmem_limit_bytes=mib * 1024 * 1024)


def cost(flops, nbytes):
    return pl.CostEstimate(flops=int(flops), bytes_accessed=int(nbytes), transcendentals=0)


def head_rows(ref, head):
    return ref[pl.ds(pl.multiple_of(head * ROWS, ROWS), ROWS), :]


def head_lanes(head, count=1):
    return pl.ds(pl.multiple_of(head * DH, DH), count * DH)


def span(n):
    return slice(n * SPAN, (n + 1) * SPAN)


def last_lane(rows):
    return jnp.broadcast_to(rows[:, SPAN - 1 :], rows.shape)


def middle_lane(rows):
    return jnp.broadcast_to(rows[:, SPAN // 2 - 1 : SPAN // 2], rows.shape)


def masks():
    i = lax.broadcasted_iota(jnp.int32, (SPAN, SPAN), 0)
    j = lax.broadcasted_iota(jnp.int32, (SPAN, SPAN), 1)
    return i >= j, i <= j


def join_rows(rows, blocks):
    return jnp.concatenate([rows[n : n + 1] for n in range(blocks)], axis=1)


def piece_store(ref, at, state, extra):
    ref[at, :DH, :] = state
    ref[at, DH:, :] = extra


def piece_state(keep_ref, taken_ref, at, half):
    kept = at < half
    place = jnp.where(kept, at, at - half)
    return jnp.where(kept, keep_ref[place, :DH, :], taken_ref[place, :DH, :])


def extra_rows(decay, gain_row=None):
    place = lax.broadcasted_iota(jnp.int32, (ROWS, DH), 0)
    rest = 0.0 if gain_row is None else jnp.where(place == 1, gain_row, 0.0)
    return jnp.where(place == 0, decay, rest)


def state_body(core_ref, log_ref, k_hbm, v_hbm, send_ref, own_ref, cum_ref, before_ref, total_ref, k_ref, v_ref, sems):
    heads, rows = log_ref.shape
    blocks, half = rows // SPAN, heads // 2
    core = core_ref[0]
    copies = []
    for g in range(heads // GROUP):
        first = lax.rem((1 - core) * half + g * GROUP, heads)
        lanes = head_lanes(first, GROUP)
        pair = [
            pltpu.make_async_copy(k_hbm.at[:, lanes], k_ref.at[:, lanes], sems.at[0, g]),
            pltpu.make_async_copy(v_hbm.at[:, lanes], v_ref.at[:, lanes], sems.at[1, g]),
        ]
        for copy in pair:
            copy.start()
        copies.append((first, pair))

    _, triangle = masks()
    triangle = triangle.astype(F32)
    cum_ref[...] = jnp.zeros_like(cum_ref)
    before_ref[...] = jnp.zeros_like(before_ref)
    before = jnp.zeros((heads, SPAN), F32)
    for n in range(blocks):
        cum = dot(log_ref[:, span(n)], triangle, (1, 0), EXACT)
        for h in range(heads):
            cum_ref[h * ROWS + n : h * ROWS + n + 1, :] = cum[h : h + 1]
            before_ref[h * ROWS + n : h * ROWS + n + 1, :] = before[h : h + 1]
        before = before + last_lane(cum)
    for h in range(heads):
        total_ref[h * ROWS : (h + 1) * ROWS, :] = jnp.broadcast_to(before[h : h + 1], (ROWS, SPAN))

    for g, (first, pair) in enumerate(copies):
        for copy in pair:
            copy.wait()
        totals = [head_rows(total_ref, first + at) for at in range(GROUP)]
        scales = [
            jnp.exp(totals[at] - head_rows(before_ref, first + at) - head_rows(cum_ref, first + at)) for at in range(GROUP)
        ]
        decayed = [
            (k_ref[:, head_lanes(first + at)].T.astype(F32) * join_rows(scales[at], blocks)).astype(BF16)
            for at in range(GROUP)
        ]
        states = [nn(decayed[at], v_ref[:, head_lanes(first + at)]) for at in range(GROUP)]
        for at in range(GROUP):
            place = (g * GROUP + at) % half
            out = send_ref if g * GROUP < half else own_ref
            piece_store(out, place, states[at], extra_rows(jnp.exp(totals[at])))


def local_state(position, log_decay, keys, values):
    heads, rows = log_decay.shape
    pieces = jax.ShapeDtypeStruct((heads // 2, PIECE, DH), F32)
    table = jax.ShapeDtypeStruct((heads * ROWS, SPAN), F32)
    like = jax.ShapeDtypeStruct(keys.shape, BF16)
    return pl.pallas_call(
        state_body,
        in_specs=[SMEM, VMEM, HBM, HBM],
        out_specs=[VMEM] * 7,
        out_shape=[pieces, pieces, table, table, table, like, like],
        scratch_shapes=[pltpu.SemaphoreType.DMA((2, heads // GROUP))],
        compiler_params=params(16),
        cost_estimate=cost(2 * heads * rows * DH * DH, 4 * rows * heads * DH),
        name="local_state",
    )(position, log_decay, keys, values)


def first_row():
    return lax.broadcasted_iota(jnp.int32, (ROWS, DH), 0) == 0


def join_extra(a, b):
    return jnp.where(first_row(), a * b, a + b)


def cores_body(reverse, position_ref, own_ref, got_ref, *out_refs):
    z = position_ref[1]
    near_here = (position_ref[0] == 0) != reverse
    each = own_ref.shape[0] // ALONG_Z
    for shift, out_ref in enumerate(out_refs):
        for j in range(each):
            head = lax.rem(z + shift, ALONG_Z) * each + j
            own, got = own_ref[head], got_ref[head]
            near, far = jnp.where(near_here, own, got), jnp.where(near_here, got, own)
            piece_store(out_ref, j, far[DH : DH + 1] * near[:DH] + far[:DH], join_extra(near[DH:], far[DH:]))


def along_z_body(reverse, position_ref, *refs):
    in_refs, (_, total_ref, prefix_ref, slots) = refs[:ALONG_Z], refs[ALONG_Z:]
    z = position_ref[1]
    for shift, ref in enumerate(in_refs):
        slots[lax.rem(z - shift + ALONG_Z, ALONG_Z)] = ref[...]
    for j in range(total_ref.shape[0]):
        state = jnp.zeros((DH, DH), F32)
        extra = jnp.where(first_row(), 1.0, 0.0)
        for lap in range(ALONG_Z):
            at = ALONG_Z - 1 - lap if reverse else lap
            prefix_ref[at, j, :DH, :] = state
            prefix_ref[at, j, DH:, :] = extra
            state = slots[at, j, DH : DH + 1, :] * state + slots[at, j, :DH, :]
            extra = join_extra(extra, slots[at, j, DH:, :])
        piece_store(total_ref, j, state, extra)


def along_x_body(reverse, position_ref, *refs):
    in_refs, prefix_ref, out_refs, slots = refs[:ALONG_X], refs[ALONG_X], refs[ALONG_X + 2 : -1], refs[-1]
    z, x = position_ref[1], position_ref[2]
    for shift, ref in enumerate(in_refs):
        slots[lax.rem(x - shift + ALONG_X, ALONG_X)] = ref[...]
    for j in range(prefix_ref.shape[1]):
        state = jnp.zeros((DH, DH), F32)
        extra = jnp.zeros((ROWS, DH), F32)
        for lap in range(ALONG_X):
            at = ALONG_X - 1 - lap if reverse else lap
            taken = (at > x) if reverse else (at < x)
            state = jnp.where(taken, slots[at, j, DH : DH + 1, :] * state + slots[at, j, :DH, :], state)
            extra = extra + slots[at, j, DH:, :]
        for shift, out_ref in enumerate(out_refs):
            at = lax.rem(z + shift, ALONG_Z)
            piece_store(out_ref, j, prefix_ref[at, j, :DH, :] + prefix_ref[at, j, DH : DH + 1, :] * state, extra)


def entering_body(reverse, position_ref, *refs):
    in_refs, (own_ref, got_ref, _, keep_ref, give_ref) = refs[:ALONG_Z], refs[ALONG_Z:]
    z = position_ref[1]
    near_here = (position_ref[0] == 0) != reverse
    each = own_ref.shape[0] // ALONG_Z
    for shift, ref in enumerate(in_refs):
        for j in range(each):
            head = lax.rem(z - shift + ALONG_Z, ALONG_Z) * each + j
            near = jnp.where(near_here, own_ref[head], got_ref[head])
            entering, extra = ref[j, :DH, :], ref[j, DH:, :]
            passed = near[DH : DH + 1] * entering + near[:DH]
            piece_store(keep_ref, head, jnp.where(near_here, entering, passed), extra)
            piece_store(give_ref, head, jnp.where(near_here, passed, entering), extra)


def scan_step(body, name, reverse, position, arrays, after, out_counts, scratch):
    shapes = [jax.ShapeDtypeStruct(shape, F32) for shape in out_counts]
    afters = [] if after is None else [after]
    return pl.pallas_call(
        functools.partial(body, reverse),
        in_specs=[SMEM] + [VMEM] * len(arrays) + [ANY] * len(afters),
        out_specs=[VMEM] * len(shapes),
        out_shape=shapes,
        scratch_shapes=scratch,
        compiler_params=params(4),
        cost_estimate=cost(10**6, 10**6),
        name=name,
    )(position, *arrays, *afters)


def scan_over_seq(send, own, position, reverse, works):
    count = lax.axis_size("seq")
    heads = own.shape[0]
    each = heads // ALONG_Z

    def index(x, z, c):
        return (x % ALONG_X * ALONG_Z + z % ALONG_Z) * 2 + c

    every = [(x, z, c) for x in range(ALONG_X) for z in range(ALONG_Z) for c in range(2)]
    across = [(i, i ^ 1) for i in range(count)]
    by_z = [[(index(x, z, c), index(x, z + s, c)) for x, z, c in every] for s in range(ALONG_Z)]
    by_x = [[(index(x, z, c), index(x + s, z, c)) for x, z, c in every] for s in range(ALONG_X)]
    piece = (each, PIECE, DH)

    got = lax.ppermute(send, "seq", across)
    parts = scan_step(cores_body, "join_cores", reverse, position, [own, got], None, [piece] * ALONG_Z, [])
    arrived = [parts[0]] + [lax.ppermute(parts[s], "seq", by_z[s]) for s in range(1, ALONG_Z)]
    done = works[0](parts[0], ())
    total, prefix = scan_step(
        along_z_body, "join_z", reverse, position, arrived, done[-1],
        [piece, (ALONG_Z,) + piece], [pltpu.VMEM((ALONG_Z,) + piece, F32)],
    )
    totals = [total] + [lax.ppermute(total, "seq", by_x[s]) for s in range(1, ALONG_X)]
    done = works[1](total, done)
    parts = scan_step(
        along_x_body, "join_x", reverse, position, totals + [prefix], done[-1],
        [piece] * ALONG_Z, [pltpu.VMEM((ALONG_X,) + piece, F32)],
    )
    arrived = [parts[0]] + [lax.ppermute(parts[s], "seq", by_z[s]) for s in range(1, ALONG_Z)]
    done = works[2](parts[0], done)
    keep, give = scan_step(
        entering_body, "entering", reverse, position, arrived + [own, got], done[-1], [own.shape] * 2, []
    )
    return keep, lax.ppermute(give, "seq", across), done


def attend_pair(heads, q_ref, k_ref, v_ref, cum_ref, before_ref, local_ref, low_ref, turned_ref, mask):
    blocks = k_ref.shape[0] // SPAN
    each = range(len(heads))
    steps = [(a, n) for n in range(blocks) for a in each]
    lanes = [head_lanes(h) for h in heads]
    cums = [head_rows(cum_ref, h) for h in heads]
    mids = [middle_lane(c) for c in cums]
    ends = [last_lane(c) for c in cums]
    query_col = [jnp.exp(c - m).T for c, m in zip(cums, mids)]
    key_col = [jnp.exp(m - c).T for c, m in zip(cums, mids)]
    query_row = [jnp.exp(c + head_rows(before_ref, h)) for c, h in zip(cums, heads)]
    mid_scale, end_scale = [jnp.exp(m) for m in mids], [jnp.exp(e) for e in ends]
    rest_scale = [jnp.exp(e - m) for e, m in zip(ends, mids)]
    q_up = {(a, n): (q_ref[span(n), lanes[a]].astype(F32) * query_col[a][:, n : n + 1]).astype(BF16) for a, n in steps}
    k_up = {(a, n): (k_ref[span(n), lanes[a]].astype(F32) * key_col[a][:, n : n + 1]).astype(BF16) for a, n in steps}
    scores = {s: nt(q_up[s], k_up[s]) for s in steps}
    updates = {(a, n): nn(k_up[a, n].T, v_ref[span(n), lanes[a]]) for a, n in steps if n < blocks - 1}
    weights = {s: jnp.where(mask, scores[s], 0.0).astype(BF16) for s in steps}
    lows = {}
    for a in each:
        state = jnp.zeros((DH, DH), F32)
        for n in range(blocks):
            lows[a, n] = (mid_scale[a][n : n + 1] * state).astype(BF16)
            low_ref[heads[a], n] = lows[a, n]
            if n < blocks - 1:
                state = end_scale[a][n : n + 1] * state + rest_scale[a][n : n + 1] * updates[a, n]
    totals = {
        (a, n): nn(
            jnp.concatenate([weights[a, n], q_up[a, n]], axis=1),
            jnp.concatenate([v_ref[span(n), lanes[a]], lows[a, n]], axis=0),
        )
        for a, n in steps
    }
    for a, n in steps:
        local_ref[span(n), lanes[a]] = totals[a, n].astype(BF16)
    for a in each:
        turned_ref[heads[a]] = (q_ref[:, lanes[a]].T.astype(F32) * join_rows(query_row[a], blocks)).astype(BF16)


def attend_body(first, count, load, *refs):
    k_ref, v_ref, cum_ref, before_ref = refs[1:5]
    refs = refs[5:]
    copies = []
    if load == "queries":
        q_hbm, local_ref, low_ref, turned_ref, q_ref, sems = refs
        for g in range(q_hbm.shape[1] // (GROUP * DH)):
            lanes = slice(g * GROUP * DH, (g + 1) * GROUP * DH)
            copies.append(pltpu.make_async_copy(q_hbm.at[:, lanes], q_ref.at[:, lanes], sems.at[g]))
    elif load == "grad_out":
        q_ref, go_hbm, _, _, _, local_ref, low_ref, turned_ref, go_ref, sems = refs
        copies.append(pltpu.make_async_copy(go_hbm, go_ref, sems.at[0]))
    else:
        q_ref, _, _, _, local_ref, low_ref, turned_ref = refs
    for copy in copies:
        copy.start()
    mask, _ = masks()

    def pairs(start, stop):
        @pl.loop(start // PAIR, stop // PAIR)
        def _(at):
            heads = [at * PAIR + a for a in range(PAIR)]
            attend_pair(heads, q_ref, k_ref, v_ref, cum_ref, before_ref, local_ref, low_ref, turned_ref, mask)

    if load == "queries":
        for g, copy in enumerate(copies):
            copy.wait()
            if g * GROUP < count:
                pairs(g * GROUP, min((g + 1) * GROUP, count))
    else:
        pairs(first, first + count)
        for copy in copies:
            copy.wait()


def attend(after, first, count, load, keys, values, cum, before, queries, grad_out, done):
    rows, width = keys.shape
    heads, blocks = width // DH, rows // SPAN
    like = jax.ShapeDtypeStruct((rows, width), BF16)
    outs = [
        like,
        jax.ShapeDtypeStruct((heads, blocks, DH, DH), BF16),
        jax.ShapeDtypeStruct((heads, DH, rows), BF16),
    ]
    arrays, specs = [after, keys, values, cum, before, queries], [ANY, VMEM, VMEM, VMEM, VMEM]
    specs.append(HBM if load == "queries" else VMEM)
    if load == "grad_out":
        arrays.append(grad_out)
        specs.append(HBM)
    aliases = {len(arrays) + i: i for i in range(len(done))}
    if load is not None:
        outs.append(like)
    return pl.pallas_call(
        functools.partial(attend_body, first, count, load),
        in_specs=specs + [VMEM] * len(done),
        out_specs=[VMEM] * len(outs),
        out_shape=outs,
        input_output_aliases=aliases,
        scratch_shapes=[] if load is None else [pltpu.SemaphoreType.DMA((heads // GROUP,))],
        compiler_params=params(12),
        cost_estimate=cost(10 * rows * count * DH * DH, 12 * rows * count * DH),
        name=f"attend_{first}",
    )(*arrays, *done)


def enter_body(position_ref, q_ref, local_ref, go_ref, gain_ref, keep_ref, taken_ref, cum_ref, before_ref,
               attn_ref, low_ref, stats_ref, square_ref, inner_ref):
    rows, width = q_ref.shape
    heads, blocks = width // DH, rows // SPAN
    half = heads // 2
    core = position_ref[0]
    square_ref[...] = jnp.zeros_like(square_ref)
    inner_ref[...] = jnp.zeros_like(inner_ref)

    @pl.loop(0, heads // GROUP)
    def _(g):
        first = lax.rem(core * half + g * GROUP, heads)
        lanes = [head_lanes(first + at) for at in range(GROUP)]
        carried, scales, gains = [], [], []
        for at in range(GROUP):
            low = piece_state(keep_ref, taken_ref, g * GROUP + at, half).astype(BF16)
            low_ref[first + at] = low
            carried.append(nn(q_ref[:, lanes[at]], low))
            scales.append(jnp.exp(head_rows(cum_ref, first + at) + head_rows(before_ref, first + at)).T)
            gains.append(gain_ref[:, lanes[at]])
        for n in range(blocks):
            square = jnp.zeros((SPAN, DH), F32)
            inner = jnp.zeros((SPAN, DH), F32)
            for at in range(GROUP):
                entered = carried[at][span(n)] * scales[at][:, n : n + 1]
                attn = (local_ref[span(n), lanes[at]].astype(F32) + entered).astype(BF16)
                attn_ref[span(n), lanes[at]] = attn
                attn = attn.astype(F32)
                square += attn * attn
                inner += go_ref[span(n), lanes[at]].astype(F32) * gains[at] * attn
            square_ref[span(n), :] += square
            inner_ref[span(n), :] += inner

    ones = jnp.ones((8, DH), F32)
    stats_ref[0:1, :] = dot(ones, square_ref[...], (1, 1), EXACT)[0:1]
    stats_ref[1:2, :] = dot(ones, inner_ref[...], (1, 1), EXACT)[0:1]


def attend_entering(position, queries, local, grad_out, gain, keep, taken, cum, before):
    rows, width = queries.shape
    heads = width // DH
    return pl.pallas_call(
        enter_body,
        in_specs=[SMEM] + [VMEM] * 8,
        out_specs=[VMEM] * 3,
        out_shape=[
            jax.ShapeDtypeStruct((rows, width), BF16),
            jax.ShapeDtypeStruct((heads, DH, DH), BF16),
            jax.ShapeDtypeStruct((2, rows), F32),
        ],
        scratch_shapes=[pltpu.VMEM((rows, DH), F32), pltpu.VMEM((rows, DH), F32)],
        compiler_params=params(12),
        cost_estimate=cost(2 * rows * width * DH, 8 * rows * width),
        name="attend_entering",
    )(position, queries, local, grad_out, gain, keep, taken, cum, before)


def columns(row, ref, blocks):
    for n in range(blocks):
        ref[span(n), :] = jnp.broadcast_to(row[:, span(n)], (SPAN, SPAN)).T


def norm_body(position_ref, turned_ref, attn_ref, go_ref, gain_ref, total_ref, *refs):
    stats_refs, (ga_ref, send_ref, own_ref, row_ref, inverse_ref, factor_ref) = refs[:-6], refs[-6:]
    rows, width = attn_ref.shape
    heads, blocks = width // DH, rows // SPAN
    half = heads // 2
    core = position_ref[0]
    stats = functools.reduce(jnp.add, [ref[...] for ref in stats_refs]) / (HEAD_TOTAL * DH)
    inverse = lax.rsqrt(stats[0:1] + 1e-06)
    row_ref[...] = inverse
    columns(inverse, inverse_ref, blocks)
    columns(inverse * inverse * inverse * stats[1:2], factor_ref, blocks)

    for out, offset in ((send_ref, 0), (own_ref, half)):

        @pl.loop(0, half // GROUP)
        def _(g):
            places = [g * GROUP + at for at in range(GROUP)]
            heads_now = [lax.rem((1 - core) * half + offset + place, heads) for place in places]
            lanes = [head_lanes(head) for head in heads_now]
            gains = [gain_ref[:, lane] for lane in lanes]
            gain_sums = [jnp.zeros((8, DH), F32) for _ in places]
            grads = [[] for _ in places]
            for n in range(blocks):
                for at in range(GROUP):
                    attn = attn_ref[span(n), lanes[at]].astype(F32)
                    scaled = go_ref[span(n), lanes[at]].astype(F32) * inverse_ref[span(n), :]
                    gain_sums[at] += jnp.sum((scaled * attn).reshape(SPAN // 8, 8, DH), axis=0)
                    grad = (scaled * gains[at] - attn * factor_ref[span(n), :]).astype(BF16)
                    ga_ref[span(n), lanes[at]] = grad
                    grads[at].append(grad)
            states = [nn(turned_ref[heads_now[at]], jnp.concatenate(grads[at], axis=0)) for at in range(GROUP)]
            for at in range(GROUP):
                decay = jnp.exp(head_rows(total_ref, heads_now[at]))
                piece_store(out, places[at], states[at], extra_rows(decay, jnp.sum(gain_sums[at], axis=0, keepdims=True)))


def norm_backward(position, turned, attn, grad_out, gain, total, stats):
    rows, width = attn.shape
    heads = width // DH
    pieces = jax.ShapeDtypeStruct((heads // 2, PIECE, DH), F32)
    return pl.pallas_call(
        norm_body,
        in_specs=[SMEM] + [VMEM] * (5 + len(stats)),
        out_specs=[VMEM] * 4,
        out_shape=[jax.ShapeDtypeStruct((rows, width), BF16), pieces, pieces, jax.ShapeDtypeStruct((1, rows), F32)],
        scratch_shapes=[pltpu.VMEM((rows, DH), F32), pltpu.VMEM((rows, DH), F32)],
        compiler_params=params(12),
        cost_estimate=cost(2 * rows * width * DH, 8 * rows * width),
        name="norm_backward",
    )(position, turned, attn, grad_out, gain, total, *stats)


def grads_pair(heads, places, refs, out_ref, gq_ref, lk_ref, lv_ref, inverse_ref, both_masks):
    q_ref, k_ref, v_ref, ga_ref, attn_ref, gain_ref, _, low_ref, enter_ref, cum_ref, before_ref = refs
    mask, turned_mask = both_masks
    blocks = k_ref.shape[0] // SPAN
    each = range(len(heads))
    steps = [(a, n) for n in range(blocks) for a in each]
    lanes = [head_lanes(h) for h in heads]
    here = [head_lanes(p) for p in places]
    cums = [head_rows(cum_ref, h) for h in heads]
    mids = [middle_lane(c) for c in cums]
    ends = [last_lane(c) for c in cums]
    query_col = [jnp.exp(c - m).T for c, m in zip(cums, mids)]
    key_col = [jnp.exp(m - c).T for c, m in zip(cums, mids)]
    mid_scale, end_scale = [jnp.exp(m) for m in mids], [jnp.exp(e) for e in ends]
    rest_scale = [jnp.exp(e - m) for e, m in zip(ends, mids)]
    enter_scale = [jnp.exp(m + head_rows(before_ref, h)) for m, h in zip(mids, heads)]
    entering = [enter_ref[h].astype(F32) for h in heads]

    def at(ref, a, n):
        return ref[span(n), lanes[a]]

    q_up = {(a, n): (at(q_ref, a, n).astype(F32) * query_col[a][:, n : n + 1]).astype(BF16) for a, n in steps}
    updates = {(a, n): nn(q_up[a, n].T, at(ga_ref, a, n)) for a, n in steps if n > 0}
    k_up = {(a, n): (at(k_ref, a, n).astype(F32) * key_col[a][:, n : n + 1]).astype(BF16) for a, n in steps}
    states = {
        (a, n): (low_ref[heads[a], n].astype(F32) + enter_scale[a][n : n + 1] * entering[a]).astype(BF16)
        for a, n in steps
    }
    from_query = {
        (a, n): nt(at(ga_ref, a, n), jnp.concatenate([at(v_ref, a, n), states[a, n]], axis=0)) for a, n in steps
    }
    lows = {}
    for a in each:
        back = jnp.zeros((DH, DH), F32)
        for n in reversed(range(blocks)):
            lows[a, n] = (rest_scale[a][n : n + 1] * back).astype(BF16)
            if n > 0:
                back = end_scale[a][n : n + 1] * back + mid_scale[a][n : n + 1] * updates[a, n]
    turned_weights = {s: nt(k_up[s], q_up[s]) for s in steps}
    from_key = {
        (a, n): nt(at(v_ref, a, n), jnp.concatenate([at(ga_ref, a, n), lows[a, n]], axis=0)) for a, n in steps
    }
    scores = {s: jnp.where(mask, from_query[s][:, :SPAN], 0.0).astype(BF16) for s in steps}
    grad_q = {s: nn(scores[s], k_up[s]) + from_query[s][:, SPAN:] for s in steps}
    turned_weights = {s: jnp.where(turned_mask, turned_weights[s], 0.0).astype(BF16) for s in steps}
    grad_v = {
        (a, n): nn(
            jnp.concatenate([turned_weights[a, n], k_up[a, n]], axis=1),
            jnp.concatenate([at(ga_ref, a, n), lows[a, n]], axis=0),
        )
        for a, n in steps
    }
    turned_scores = {s: jnp.where(turned_mask, from_key[s][:, :SPAN], 0.0).astype(BF16) for s in steps}
    grad_k = {s: nn(turned_scores[s], q_up[s]) + from_key[s][:, SPAN:] for s in steps}
    for a, n in steps:
        gq_ref[span(n), here[a]] = (grad_q[a, n] * query_col[a][:, n : n + 1]).astype(BF16)
        lv_ref[span(n), lanes[a]] = grad_v[a, n].astype(BF16)
        lk_ref[span(n), lanes[a]] = (grad_k[a, n] * key_col[a][:, n : n + 1]).astype(BF16)
        normed = at(attn_ref, a, n).astype(F32) * inverse_ref[span(n), :]
        out_ref[span(n), here[a]] = (normed * gain_ref[:, lanes[a]]).astype(BF16)


def grads_body(first, count, chained, *refs):
    inputs = refs[1:12]
    refs = refs[12 + (4 if chained else 0) :]
    out_hbm, gq_hbm, lk_ref, lv_ref, out_ref, gq_ref, inverse_ref, sems = refs
    blocks = inputs[0].shape[0] // SPAN
    both_masks = masks()
    columns(inputs[6][...], inverse_ref, blocks)

    def copies(at):
        here, there = head_lanes(at * PAIR, PAIR), head_lanes(first + at * PAIR, PAIR)
        return [
            pltpu.make_async_copy(out_ref.at[:, here], out_hbm.at[:, there], sems.at[0, at]),
            pltpu.make_async_copy(gq_ref.at[:, here], gq_hbm.at[:, there], sems.at[1, at]),
        ]

    @pl.loop(0, count // PAIR)
    def _(at):
        places = [at * PAIR + a for a in range(PAIR)]
        heads = [first + p for p in places]
        grads_pair(heads, places, inputs, out_ref, gq_ref, lk_ref, lv_ref, inverse_ref, both_masks)
        for copy in copies(at):
            copy.start()

    @pl.loop(0, count // PAIR)
    def _(at):
        for copy in copies(at):
            copy.wait()


def grads_local(after, first, count, inputs, done):
    rows, width = inputs[0].shape
    like = jax.ShapeDtypeStruct((rows, width), BF16)
    kinds = [HBM, HBM, VMEM, VMEM]
    return pl.pallas_call(
        functools.partial(grads_body, first, count, bool(done)),
        in_specs=[ANY] + [VMEM] * 11 + (kinds if done else []),
        out_specs=kinds,
        out_shape=[like] * 4,
        input_output_aliases={12 + i: i for i in range(4)} if done else {},
        scratch_shapes=[
            pltpu.VMEM((rows, count * DH), BF16),
            pltpu.VMEM((rows, count * DH), BF16),
            pltpu.VMEM((rows, DH), F32),
            pltpu.SemaphoreType.DMA((2, count // PAIR)),
        ],
        compiler_params=params(16),
        cost_estimate=cost(22 * rows * count * DH * DH, 24 * rows * count * DH),
        name=f"grads_{first}",
    )(after, *inputs, *done)


def leave_body(position_ref, k_ref, v_ref, lk_ref, lv_ref, keep_ref, taken_ref, cum_ref, before_ref, total_ref,
               gk_hbm, gv_hbm, gg_ref, gk_ref, gv_ref, sems):
    rows, width = k_ref.shape
    heads, blocks = width // DH, rows // SPAN
    half = heads // 2
    core = position_ref[0]

    def copies(at):
        lanes = head_lanes(lax.rem(core * half + at * PAIR, heads), PAIR)
        return [
            pltpu.make_async_copy(gk_ref.at[:, lanes], gk_hbm.at[:, lanes], sems.at[0, at]),
            pltpu.make_async_copy(gv_ref.at[:, lanes], gv_hbm.at[:, lanes], sems.at[1, at]),
        ]

    @pl.loop(0, heads // PAIR)
    def _(at):
        first = lax.rem(core * half + at * PAIR, heads)
        lanes = [head_lanes(first + a) for a in range(PAIR)]
        lows = [piece_state(keep_ref, taken_ref, at * PAIR + a, half).astype(BF16) for a in range(PAIR)]
        from_v = [nt(v_ref[:, lanes[a]], lows[a]) for a in range(PAIR)]
        from_k = [nn(k_ref[:, lanes[a]], lows[a]) for a in range(PAIR)]
        scales = [
            jnp.exp(
                head_rows(total_ref, first + a) - head_rows(before_ref, first + a) - head_rows(cum_ref, first + a)
            ).T
            for a in range(PAIR)
        ]
        for n in range(blocks):
            for a in range(PAIR):
                factor = scales[a][:, n : n + 1]
                grad_k = lk_ref[span(n), lanes[a]].astype(F32) + factor * from_v[a][span(n)]
                grad_v = lv_ref[span(n), lanes[a]].astype(F32) + factor * from_k[a][span(n)]
                gk_ref[span(n), lanes[a]] = grad_k.astype(BF16)
                gv_ref[span(n), lanes[a]] = grad_v.astype(BF16)
        for copy in copies(at):
            copy.start()
        kept = at * PAIR < half
        for a in range(PAIR):
            place = jnp.where(kept, at * PAIR + a, at * PAIR + a - half)
            row = slice(DH + 1, DH + 2)
            gg_ref[:, lanes[a]] = jnp.where(kept, keep_ref[place, row, :], taken_ref[place, row, :])

    @pl.loop(0, heads // PAIR)
    def _(at):
        for copy in copies(at):
            copy.wait()


def grads_leaving(position, keys, values, local_k, local_v, keep, taken, cum, before, total):
    rows, width = keys.shape
    like = jax.ShapeDtypeStruct((rows, width), BF16)
    return pl.pallas_call(
        leave_body,
        in_specs=[SMEM] + [VMEM] * 9,
        out_specs=[HBM, HBM, VMEM],
        out_shape=[like, like, jax.ShapeDtypeStruct((1, width), F32)],
        scratch_shapes=[
            pltpu.VMEM((rows, width), BF16),
            pltpu.VMEM((rows, width), BF16),
            pltpu.SemaphoreType.DMA((2, width // DH // PAIR)),
        ],
        compiler_params=params(16),
        cost_estimate=cost(4 * rows * width * DH, 12 * rows * width),
        name="grads_leaving",
    )(position, keys, values, local_k, local_v, keep, taken, cum, before, total)


def per_device(queries, keys, values, log_decay, gain, grad_out):
    place = lax.axis_index("seq")
    position = jnp.stack([place % 2, place // 2 % ALONG_Z, place // (2 * ALONG_Z)]).astype(jnp.int32)
    gain_row = gain.reshape(1, -1)
    keys, values, queries, grad_out = (
        pltpu.with_memory_space_constraint(a, pltpu.HBM) for a in (keys, values, queries, grad_out)
    )
    send, own, cum, before, total, keys, values = local_state(position, log_decay, keys, values)

    def attend_part(first, count, load):
        def run(after, done):
            held = done[3] if done else queries
            more = done[4:] if done else ()
            outs = attend(after, first, count, load, keys, values, cum, before, held, grad_out, done[:3])
            if load == "queries":
                return (*outs[:3], outs[3], outs[0])
            if load == "grad_out":
                return (*outs[:3], held, outs[3])
            return (*outs[:3], held, more[0])

        return run

    keep, taken, (local, lows, turned, queries, grad_out) = scan_over_seq(
        send, own, position, False, [attend_part(0, 6, "queries"), attend_part(6, 6, "grad_out"), attend_part(12, 4, None)]
    )
    attn, entering, stats = attend_entering(
        position, queries, local, grad_out, gain_row, keep, taken, cum, before
    )
    count = lax.axis_size("head")
    stats = [stats] + [
        lax.ppermute(stats, "head", [(i, (i + s) % count) for i in range(count)]) for s in range(1, count)
    ]
    grad_attn, send, own, inverse = norm_backward(position, turned, attn, grad_out, gain_row, total, stats)
    inputs = (queries, keys, values, grad_attn, attn, gain_row, inverse, lows, entering, cum, before)

    def grads_part(first, count):
        return lambda after, done: grads_local(after, first, count, inputs, done)

    keep, taken, (output, grad_q, local_k, local_v) = scan_over_seq(
        send, own, position, True, [grads_part(0, 6), grads_part(6, 6), grads_part(12, 4)]
    )
    grad_k, grad_v, grad_gain = grads_leaving(
        position, keys, values, local_k, local_v, keep, taken, cum, before, total
    )
    return output, grad_q, grad_k, grad_v, grad_gain.reshape(-1)


def solution(mesh):
    tokens, heads = P("seq", "head"), P("head")
    return jax.shard_map(
        per_device,
        mesh=mesh,
        in_specs=(tokens, tokens, tokens, P("head", "seq"), heads, tokens),
        out_specs=(tokens, tokens, tokens, tokens, heads),
        check_vma=False,
    )
```

time: 240 us -> 114 us (0.47); the launches traced: 237 us -> 114 us
  local copies, waits for them, and re-layouts: 86.9 us -> 0.8 us
  Pallas kernels: 73.7 us -> 59.2 us
  other arithmetic: 9.43 us -> 0.08 us
  blocking collectives: 8.79 us -> 0 us
  waiting for transfers between devices: 24.4 us -> 20 us
    unnamed x112 -> x4, local copies, waits for them, and re-layouts: 85.2 us -> 0.8 us
    ppermute x4 -> x25, starting transfers between devices: 7.63 us -> 33 us  [the longest x12 17.4 us: scan_over_seq(): lax.ppermute(parts[s], 'seq', by_z[s])]
    all_to_all x4 -> x0, starting transfers between devices: 25.2 us -> none  [the longest x2 13.1 us: scan_over_seq(): entering = lax.all_to_all(scanned, 'seq', 0, 0, axis_index_groups=chips)]
    all_to_all x4 -> x0, waiting for transfers between devices: 20.4 us -> none  [the longest x2 20.4 us: scan_over_seq(): entering = lax.all_to_all(scanned, 'seq', 0, 0, axis_index_groups=chips)]
    ppermute x4 -> x25, waiting for transfers between devices: 3.94 us -> 20 us  [the longest x12 7.24 us: scan_over_seq(): lax.ppermute(parts[s], 'seq', by_z[s])]
    pallas_call x7 -> x15, Pallas kernels: 55.1 us -> 41.7 us  [the longest x3 19.8 us: grads_local(): pl.pallas_call(functools.partial(grads_body, first, count, bool(done)), i...]
    psum x1 -> x0, blocking collectives: 8.79 us -> none  [per_device(): stats = lax.psum(stats, 'head')]
    select_n x4 -> x0, other arithmetic: 5.04 us -> none  [the longest x2 2.78 us: scan_over_seq(): give = jnp.where(near_here, passed, entering)]
  transfers between devices with their start and end apart: 8 -> 25, of which waited for: 4 -> 12; matrix products, arithmetic and copies ran while one was open for 1% -> 0% of each run, Pallas kernels for 20% -> 28%
where the time goes in v2:
time: 114 us
  Pallas kernels  59.2 us (52%)
  starting transfers between devices  33 us (29%)
  waiting for transfers between devices  20 us (18%)
    pallas_call x3, Pallas kernels, grads_local(): pl.pallas_call(functools.partial(grads_body, first, count, bool(done)), i...  19.8 us
    ppermute x12, starting transfers between devices, scan_over_seq(): lax.ppermute(parts[s], 'seq', by_z[s])  17.4 us
    pallas_call x3, Pallas kernels, attend(): pl.pallas_call(functools.partial(attend_body, first, count, load), in_spe...  11.7 us
    pallas_call x1, Pallas kernels, grads_leaving(): pl.pallas_call(leave_body, in_specs=[SMEM] + [VMEM] * 9, out_specs=[HBM,...  7.44 us
    ppermute x12, waiting for transfers between devices, scan_over_seq(): lax.ppermute(parts[s], 'seq', by_z[s])  7.24 us
    pallas_call x1, Pallas kernels, attend_entering(): pl.pallas_call(enter_body, in_specs=[SMEM] + [VMEM] * 8, out_specs=[VMEM]...  5.3 us
    pallas_call x8, Pallas kernels, scan_step(): pl.pallas_call(functools.partial(body, reverse), in_specs=[SMEM] + [VMEM]...  5.23 us
    ppermute x6, starting transfers between devices, scan_over_seq(): lax.ppermute(total, 'seq', by_x[s])  5.2 us
  transfers between devices with their start and end apart: 25, of which 12 were waited for; matrix products, arithmetic and copies ran while one was open for 0% of the time, Pallas kernels for 28%

profile of v2, /device:TPU:1, one launch (start us, length us, event | category | flops | bytes accessed | tf_op | source)
XLA Modules:
  0.0 114.2 jit_solution(14644629975597155923)
XLA Ops:
  0.7 0.8 copy-done.1
  1.5 4.7 %local_state.1 = (f32[8,136,128]{2,1,0:T(8,128)S(1)}, f32[8,136,128]{2,1,0:T(8,128)S(1)}, f32[128,128]{1,0:T(8,128)S(1)}, f32[128,128]{1,0:T(8,128)S(1)}, f32[12...) custom-call(s32[3]{0:T(128)S(1)} %pad_add_fusion.core_ref.position_ref, ...), custom_call_target="tpu_custom_call" | custom-call | flops 402653184 | bytes 6291456 | tf_op jit(solution)/shard_map/local_state/pallas_call | solution.py:149
  6.3 1.5 %collective-permute-start = (f32[8,136,128]{2,1,0:T(8,128)S(1)}, f32[8,136,128]{2,1,0:T(8,128)S(1)}, u32[]{:S(2)}, u32[]{:S(2)}) collective-permute-start(f32[8,136,128]{2,1,0:T(8,128)S(1)} %get-tuple-element.70), channel_id=1, source_target_pairs={{0,4},{4,0},{8,12},{12,8},{16,20},{20,16},{24,28},{28,24},{32,36},... | collective-permute-start | bytes 1671176 | tf_op jit(solution)/shard_map/ppermute | solution.py:260
  7.8 1.6 %collective-permute-done.got_ref.refs_5_ = f32[8,136,128]{2,1,0:T(8,128)S(1)} collective-permute-done((f32[8,136,128]{2,1,0:T(8,128)S(1)}, f32[8,136,128]{2,1,0:T(8,128)S(1)}, u32[]{:S(2)}, u32[]{:S(2)}) %collective-permute-start) | collective-permute-done | bytes 557088 | tf_op jit(solution)/shard_map/ppermute | solution.py:260
  9.4 0.6 join_cores.2
  10.0 1.8 %collective-permute-start.1 = (f32[2,136,128]{2,1,0:T(8,128)S(1)}, f32[2,136,128]{2,1,0:T(8,128)S(1)}, u32[]{:S(2)}, u32[]{:S(2)}) collective-permute-start(f32[2,136,128]{2,1,0:T(8,128)S(1)} %get-tuple-element.72), channel_id=1, source_target_pairs={{0,8},{4,12},{8,16},{12,20},{16,24},{20,28},{24,0},{28,4},{32,40},... | collective-permute-start | bytes 417800 | tf_op jit(solution)/shard_map/ppermute | solution.py:262
  11.8 3.3 %collective-permute-start.2 = (f32[2,136,128]{2,1,0:T(8,128)S(1)}, f32[2,136,128]{2,1,0:T(8,128)S(1)}, u32[]{:S(2)}, u32[]{:S(2)}) collective-permute-start(f32[2,136,128]{2,1,0:T(8,128)S(1)} %get-tuple-element.73), channel_id=1, source_target_pairs={{0,16},{4,20},{8,24},{12,28},{16,0},{20,4},{24,8},{28,12},{32,48},... | collective-permute-start | bytes 417800 | tf_op jit(solution)/shard_map/ppermute | solution.py:262
  15.1 0.7 collective-permute-start.3
  15.8 5.1 %attend_0.1 = (bf16[768,2048]{1,0:T(8,128)(2,1)S(1)}, bf16[16,6,128,128]{3,2,1,0:T(8,128)(2,1)S(1)}, bf16[16,128,768]{2,1,0:T(8,128)(2,1)S(1)}, bf16[768,2048]{1,0:T(8,128)(2,1)S(1)}) custom-call(f32[2,136,128]{2,1,0:T(8,128)S(1)} %get-tuple-element.71.refs_0_, bf16[768,2048]{1,0:T(8,128)(2,1)S(1)} %get-tuple-element.75.refs_1_.refs_2_.k_ref, ...), custom_call_target="tpu_custom_call" | custom-call | flops 754974720 | bytes 7077888 | tf_op jit(solution)/shard_map/attend_0/pallas_call | solution.py:373
  20.9 0.6 collective-permute-done.2.refs_2_
  21.5 0.6 join_z.2
  22.2 2.6 %collective-permute-start.6 = (f32[2,136,128]{2,1,0:T(8,128)S(1)}, f32[2,136,128]{2,1,0:T(8,128)S(1)}, u32[]{:S(2)}, u32[]{:S(2)}) collective-permute-start(f32[2,136,128]{2,1,0:T(8,128)S(1)} %get-tuple-element.80.refs_0_), channel_id=1, source_target_pairs={{0,96},{4,100},{8,104},{12,108},{16,112},{20,116},{24,120},{28,124... | collective-permute-start | bytes 417800 | tf_op jit(solution)/shard_map/ppermute | solution.py:268
  24.7 0.5 collective-permute-start.5
  25.2 0.6 collective-permute-start.4
  25.8 4.0 %attend_6.1 = (bf16[768,2048]{1,0:T(8,128)(2,1)S(1)}, bf16[16,6,128,128]{3,2,1,0:T(8,128)(2,1)S(1)}, bf16[16,128,768]{2,1,0:T(8,128)(2,1)S(1)}, bf16[768,2048]{1,0:T(8,128)(2,1)S(1)}) custom-call(f32[2,136,128]{2,1,0:T(8,128)S(1)} %get-tuple-element.80.refs_0_, ...), custom_call_target="tpu_custom_call", output_to_operand_aliasing={{0}: (7, {}), {1}: (8, {}), {2}: (9, {})} | custom-call | flops 754974720 | bytes 7077888 | tf_op jit(solution)/shard_map/attend_6/pallas_call | solution.py:373
  30.2 3.9 %collective-permute-done.4.refs_1_ = f32[2,136,128]{2,1,0:T(8,128)S(1)} collective-permute-done((f32[2,136,128]{2,1,0:T(8,128)S(1)}, f32[2,136,128]{2,1,0:T(8,128)S(1)}, u32[]{:S(2)}, u32[]{:S(2)}) %collective-permute-start.4) | collective-permute-done | bytes 139296 | tf_op jit(solution)/shard_map/ppermute | solution.py:268
  34.1 0.7 join_x.2
  34.8 1.7 %collective-permute-start.7 = (f32[2,136,128]{2,1,0:T(8,128)S(1)}, f32[2,136,128]{2,1,0:T(8,128)S(1)}, u32[]{:S(2)}, u32[]{:S(2)}) collective-permute-start(f32[2,136,128]{2,1,0:T(8,128)S(1)} %get-tuple-element.92), channel_id=1, source_target_pairs={{0,8},{4,12},{8,16},{12,20},{16,24},{20,28},{24,0},{28,4},{32,40},... | collective-permute-start | bytes 417800 | tf_op jit(solution)/shard_map/ppermute | solution.py:274
  36.5 2.2 %collective-permute-start.8 = (f32[2,136,128]{2,1,0:T(8,128)S(1)}, f32[2,136,128]{2,1,0:T(8,128)S(1)}, u32[]{:S(2)}, u32[]{:S(2)}) collective-permute-start(f32[2,136,128]{2,1,0:T(8,128)S(1)} %get-tuple-element.93), channel_id=1, source_target_pairs={{0,16},{4,20},{8,24},{12,28},{16,0},{20,4},{24,8},{28,12},{32,48},... | collective-permute-start | bytes 417800 | tf_op jit(solution)/shard_map/ppermute | solution.py:274
  39.0 1.0 collective-permute-done.7.refs_1_
  40.0 4.6 %collective-permute-done.8.refs_2_ = f32[2,136,128]{2,1,0:T(8,128)S(1)} collective-permute-done((f32[2,136,128]{2,1,0:T(8,128)S(1)}, f32[2,136,128]{2,1,0:T(8,128)S(1)}, u32[]{:S(2)}, u32[]{:S(2)}) %collective-permute-start.8) | collective-permute-done | bytes 139296 | tf_op jit(solution)/shard_map/ppermute | solution.py:274
  44.6 0.7 entering.2
  45.2 2.0 %collective-permute-start.10 = (f32[8,136,128]{2,1,0:T(8,128)S(1)}, f32[8,136,128]{2,1,0:T(8,128)S(1)}, u32[]{:S(2)}, u32[]{:S(2)}) collective-permute-start(f32[8,136,128]{2,1,0:T(8,128)S(1)} %get-tuple-element.96), channel_id=1, source_target_pairs={{0,4},{4,0},{8,12},{12,8},{16,20},{20,16},{24,28},{28,24},{32,36},... | collective-permute-start | bytes 1671176 | tf_op jit(solution)/shard_map/ppermute | solution.py:279
  47.2 2.6 %attend_12.1 = (bf16[768,2048]{1,0:T(8,128)(2,1)S(1)}, bf16[16,6,128,128]{3,2,1,0:T(8,128)(2,1)S(1)}, bf16[16,128,768]{2,1,0:T(8,128)(2,1)S(1)}) custom-call(f32[2,136,128]{2,1,0:T(8,128)S(1)} %get-tuple-element.86.refs_0_, bf16[768,2048]{1,0:T(8,128)(2,1)S(1)} %get-tuple-element.75.refs_1_.refs_2_.k_ref, ...), custom_call_target="tpu_custom_call", output_to_operand_aliasing={{0}: (6, {}), {1}: (7, {}), {2}: (8, {})} | custom-call | flops 503316480 | bytes 4718592 | tf_op jit(solution)/shard_map/attend_12/pallas_call | solution.py:373
  49.8 5.3 %attend_entering.1 = (bf16[768,2048]{1,0:T(8,128)(2,1)S(1)}, bf16[16,128,128]{2,1,0:T(8,128)(2,1)S(1)}, f32[2,768]{1,0:T(2,128)S(1)}) custom-call(s32[3]{0:T(128)S(1)} %pad_add_fusion.core_ref.position_ref, bf16[768,2048]{1,0:T(8,128)(2,1)S(1)} %get-tuple-element.82.refs_5_.q_ref.refs_1_, bf16[768,2048]{1,0:T(8,128)(2,1)S(1)} %get-tuple-element.91.local_ref, ...), custom_call_target="tpu_custom_call" | custom-call | flops 402653184 | bytes 12582912 | tf_op jit(solution)/shard_map/attend_entering/pallas_call | solution.py:427
  55.1 2.7 %collective-permute-start.13 = (f32[2,768]{1,0:T(2,128)S(1)}, f32[2,768]{1,0:T(2,128)S(1)}, u32[]{:S(2)}, u32[]{:S(2)}) collective-permute-start(f32[2,768]{1,0:T(2,128)S(1)} %get-tuple-element.99.refs_0_), channel_id=1, source_target_pairs={{0,3},{1,0},{2,1},{3,2},{4,7},{5,4},{6,5},{7,6},{8,11},{9,8},{10,9... | collective-permute-start | bytes 18440 | tf_op jit(solution)/shard_map/ppermute | solution.py:710
  58.2 0.7 collective-permute-start.11
  58.9 2.9 %collective-permute-done.12.refs_2_ = f32[2,768]{1,0:T(2,128)S(1)} collective-permute-done((f32[2,768]{1,0:T(2,128)S(1)}, f32[2,768]{1,0:T(2,128)S(1)}, u32[]{:S(2)}, u32[]{:S(2)}) %collective-permute-start.12) | collective-permute-done | bytes 6176 | tf_op jit(solution)/shard_map/ppermute | solution.py:710
  61.9 5.1 %norm_backward.1 = (bf16[768,2048]{1,0:T(8,128)(2,1)S(1)}, f32[8,136,128]{2,1,0:T(8,128)S(1)}, f32[8,136,128]{2,1,0:T(8,128)S(1)}, f32[1,768]{1,0:T(1,128)S(1)}) custom-call(s32[3]{0:T(128)S(1)} %pad_add_fusion.core_ref.position_ref, bf16[16,128,768]{2,1,0:T(8,128)(2,1)S(1)} %get-tuple-element.90.turned_ref, ...), custom_call_target="tpu_custom_call" | custom-call | flops 402653184 | bytes 12582912 | tf_op jit(solution)/shard_map/norm_backward/pallas_call | solution.py:488
  67.0 1.8 %collective-permute-start.14 = (f32[8,136,128]{2,1,0:T(8,128)S(1)}, f32[8,136,128]{2,1,0:T(8,128)S(1)}, u32[]{:S(2)}, u32[]{:S(2)}) collective-permute-start(f32[8,136,128]{2,1,0:T(8,128)S(1)} %get-tuple-element.101), channel_id=1, source_target_pairs={{0,4},{4,0},{8,12},{12,8},{16,20},{20,16},{24,28},{28,24},{32,36},... | collective-permute-start | bytes 1671176 | tf_op jit(solution)/shard_map/ppermute | solution.py:260
  68.8 1.6 %collective-permute-done.14.got_ref.refs_5_ = f32[8,136,128]{2,1,0:T(8,128)S(1)} collective-permute-done((f32[8,136,128]{2,1,0:T(8,128)S(1)}, f32[8,136,128]{2,1,0:T(8,128)S(1)}, u32[]{:S(2)}, u32[]{:S(2)}) %collective-permute-start.14) | collective-permute-done | bytes 557088 | tf_op jit(solution)/shard_map/ppermute | solution.py:260
  70.4 0.6 join_cores.3
  71.0 0.9 collective-permute-start.15
  71.9 2.2 %collective-permute-start.16 = (f32[2,136,128]{2,1,0:T(8,128)S(1)}, f32[2,136,128]{2,1,0:T(8,128)S(1)}, u32[]{:S(2)}, u32[]{:S(2)}) collective-permute-start(f32[2,136,128]{2,1,0:T(8,128)S(1)} %get-tuple-element.104), channel_id=1, source_target_pairs={{0,16},{4,20},{8,24},{12,28},{16,0},{20,4},{24,8},{28,12},{32,48},... | collective-permute-start | bytes 417800 | tf_op jit(solution)/shard_map/ppermute | solution.py:262
  74.6 7.2 %grads_0.1 = (bf16[768,2048]{1,0:T(8,128)(2,1)}, bf16[768,2048]{1,0:T(8,128)(2,1)}, bf16[768,2048]{1,0:T(8,128)(2,1)S(1)}, bf16[768,2048]{1,0:T(8,128)(2,1)S(1)}) custom-call(f32[2,136,128]{2,1,0:T(8,128)S(1)} %get-tuple-element.102.refs_0_, bf16[768,2048]{1,0:T(8,128)(2,1)S(1)} %get-tuple-element.82.refs_5_.q_ref.refs_1_, ...), custom_call_target="tpu_custom_call" | custom-call | flops 1660944384 | bytes 14155776 | tf_op jit(solution)/shard_map/grads_0/pallas_call | solution.py:595
  81.9 0.6 join_z.3
  82.8 1.2 %collective-permute-start.18 = (f32[2,136,128]{2,1,0:T(8,128)S(1)}, f32[2,136,128]{2,1,0:T(8,128)S(1)}, u32[]{:S(2)}, u32[]{:S(2)}) collective-permute-start(f32[2,136,128]{2,1,0:T(8,128)S(1)} %get-tuple-element.111.refs_0_), channel_id=1, source_target_pairs={{0,32},{4,36},{8,40},{12,44},{16,48},{20,52},{24,56},{28,60},{32,6... | collective-permute-start | bytes 417800 | tf_op jit(solution)/shard_map/ppermute | solution.py:268
  84.0 7.4 %grads_6.1 = (bf16[768,2048]{1,0:T(8,128)(2,1)}, bf16[768,2048]{1,0:T(8,128)(2,1)}, bf16[768,2048]{1,0:T(8,128)(2,1)S(1)}, bf16[768,2048]{1,0:T(8,128)(2,1)S(1)}) custom-call(f32[2,136,128]{2,1,0:T(8,128)S(1)} %get-tuple-element.111.refs_0_, ...), custom_call_target="tpu_custom_call", output_to_operand_aliasing={{0}: (12, {}), {1}: (13, {}), {2}: (14, {}), {3}: (15, {})} | custom-call | flops 1660944384 | bytes 14155776 | tf_op jit(solution)/shard_map/grads_6/pallas_call | solution.py:595
  91.4 0.8 collective-permute-done.18.refs_1_
  92.2 0.7 join_x.3
  92.9 1.0 collective-permute-start.21
  93.9 2.7 %collective-permute-start.22 = (f32[2,136,128]{2,1,0:T(8,128)S(1)}, f32[2,136,128]{2,1,0:T(8,128)S(1)}, u32[]{:S(2)}, u32[]{:S(2)}) collective-permute-start(f32[2,136,128]{2,1,0:T(8,128)S(1)} %get-tuple-element.126), channel_id=1, source_target_pairs={{0,16},{4,20},{8,24},{12,28},{16,0},{20,4},{24,8},{28,12},{32,48},... | collective-permute-start | bytes 417800 | tf_op jit(solution)/shard_map/ppermute | solution.py:274
  96.7 5.2 %grads_12.1 = (bf16[768,2048]{1,0:T(8,128)(2,1)}, bf16[768,2048]{1,0:T(8,128)(2,1)}, bf16[768,2048]{1,0:T(8,128)(2,1)S(1)}, bf16[768,2048]{1,0:T(8,128)(2,1)S(1)}) custom-call(f32[2,136,128]{2,1,0:T(8,128)S(1)} %get-tuple-element.117.refs_0_, ...), custom_call_target="tpu_custom_call", output_to_operand_aliasing={{0}: (12, {}), {1}: (13, {}), {2}: (14, {}), {3}: (15, {})} | custom-call | flops 1107296256 | bytes 9437184 | tf_op jit(solution)/shard_map/grads_12/pallas_call | solution.py:595
  101.9 1.0 collective-permute-done.22.refs_2_
  102.9 0.7 entering.3
  103.6 1.4 %collective-permute-start.24 = (f32[8,136,128]{2,1,0:T(8,128)S(1)}, f32[8,136,128]{2,1,0:T(8,128)S(1)}, u32[]{:S(2)}, u32[]{:S(2)}) collective-permute-start(f32[8,136,128]{2,1,0:T(8,128)S(1)} %get-tuple-element.129), channel_id=1, source_target_pairs={{0,4},{4,0},{8,12},{12,8},{16,20},{20,16},{24,28},{28,24},{32,36},... | collective-permute-start | bytes 1671176 | tf_op jit(solution)/shard_map/ppermute | solution.py:279
  105.0 1.6 %collective-permute-done.24.taken_ref = f32[8,136,128]{2,1,0:T(8,128)S(1)} collective-permute-done((f32[8,136,128]{2,1,0:T(8,128)S(1)}, f32[8,136,128]{2,1,0:T(8,128)S(1)}, u32[]{:S(2)}, u32[]{:S(2)}) %collective-permute-start.24) | collective-permute-done | bytes 557088 | tf_op jit(solution)/shard_map/ppermute | solution.py:279
  106.6 7.4 %grads_leaving.1 = (bf16[768,2048]{1,0:T(8,128)(2,1)}, bf16[768,2048]{1,0:T(8,128)(2,1)}, f32[1,2048]{1,0:T(1,128)}) custom-call(s32[3]{0:T(128)S(1)} %pad_add_fusion.core_ref.position_ref, bf16[768,2048]{1,0:T(8,128)(2,1)S(1)} %get-tuple-element.75.refs_1_.refs_2_.k_ref, bf16[768,2048]{1,0:T(8,128)(2,1)S(1)} %get-tuple-element.76.refs_2_.refs_3_.v_ref, ...), custom_call_target="tpu_custom_call" | custom-call | flops 805306368 | bytes 18874368 | tf_op jit(solution)/shard_map/grads_leaving/pallas_call | solution.py:664
  (25 shorter events, 2.0 us)
Async XLA Ops:
  0.7 0.8 copy-start.1
  6.3 3.1 %collective-permute-start = (f32[8,136,128]{2,1,0:T(8,128)S(1)}, f32[8,136,128]{2,1,0:T(8,128)S(1)}, u32[]{:S(2)}, u32[]{:S(2)}) collective-permute-start(f32[8,136,128]{2,1,0:T(8,128)S(1)} %get-tuple-element.70), channel_id=1, source_target_pairs={{0,4},{4,0},{8,12},{12,8},{16,20},{20,16},{24,28},{28,24},{32,36},... | collective-permute-start | bytes 1671176 | tf_op jit(solution)/shard_map/ppermute | solution.py:260
  10.0 10.9 %collective-permute-start.1 = (f32[2,136,128]{2,1,0:T(8,128)S(1)}, f32[2,136,128]{2,1,0:T(8,128)S(1)}, u32[]{:S(2)}, u32[]{:S(2)}) collective-permute-start(f32[2,136,128]{2,1,0:T(8,128)S(1)} %get-tuple-element.72), channel_id=1, source_target_pairs={{0,8},{4,12},{8,16},{12,20},{16,24},{20,28},{24,0},{28,4},{32,40},... | collective-permute-start | bytes 417800 | tf_op jit(solution)/shard_map/ppermute | solution.py:262
  11.8 9.7 %collective-permute-start.2 = (f32[2,136,128]{2,1,0:T(8,128)S(1)}, f32[2,136,128]{2,1,0:T(8,128)S(1)}, u32[]{:S(2)}, u32[]{:S(2)}) collective-permute-start(f32[2,136,128]{2,1,0:T(8,128)S(1)} %get-tuple-element.73), channel_id=1, source_target_pairs={{0,16},{4,20},{8,24},{12,28},{16,0},{20,4},{24,8},{28,12},{32,48},... | collective-permute-start | bytes 417800 | tf_op jit(solution)/shard_map/ppermute | solution.py:262
  15.1 6.4 %collective-permute-start.3 = (f32[2,136,128]{2,1,0:T(8,128)S(1)}, f32[2,136,128]{2,1,0:T(8,128)S(1)}, u32[]{:S(2)}, u32[]{:S(2)}) collective-permute-start(f32[2,136,128]{2,1,0:T(8,128)S(1)} %get-tuple-element.74), channel_id=1, source_target_pairs={{0,24},{4,28},{8,0},{12,4},{16,8},{20,12},{24,16},{28,20},{32,56},... | collective-permute-start | bytes 417800 | tf_op jit(solution)/shard_map/ppermute | solution.py:262
  22.2 7.7 %collective-permute-start.6 = (f32[2,136,128]{2,1,0:T(8,128)S(1)}, f32[2,136,128]{2,1,0:T(8,128)S(1)}, u32[]{:S(2)}, u32[]{:S(2)}) collective-permute-start(f32[2,136,128]{2,1,0:T(8,128)S(1)} %get-tuple-element.80.refs_0_), channel_id=1, source_target_pairs={{0,96},{4,100},{8,104},{12,108},{16,112},{20,116},{24,120},{28,124... | collective-permute-start | bytes 417800 | tf_op jit(solution)/shard_map/ppermute | solution.py:268
  24.7 5.5 %collective-permute-start.5 = (f32[2,136,128]{2,1,0:T(8,128)S(1)}, f32[2,136,128]{2,1,0:T(8,128)S(1)}, u32[]{:S(2)}, u32[]{:S(2)}) collective-permute-start(f32[2,136,128]{2,1,0:T(8,128)S(1)} %get-tuple-element.80.refs_0_), channel_id=1, source_target_pairs={{0,64},{4,68},{8,72},{12,76},{16,80},{20,84},{24,88},{28,92},{32,9... | collective-permute-start | bytes 417800 | tf_op jit(solution)/shard_map/ppermute | solution.py:268
  25.2 8.9 %collective-permute-start.4 = (f32[2,136,128]{2,1,0:T(8,128)S(1)}, f32[2,136,128]{2,1,0:T(8,128)S(1)}, u32[]{:S(2)}, u32[]{:S(2)}) collective-permute-start(f32[2,136,128]{2,1,0:T(8,128)S(1)} %get-tuple-element.80.refs_0_), channel_id=1, source_target_pairs={{0,32},{4,36},{8,40},{12,44},{16,48},{20,52},{24,56},{28,60},{32,6... | collective-permute-start | bytes 417800 | tf_op jit(solution)/shard_map/ppermute | solution.py:268
  34.8 5.2 %collective-permute-start.7 = (f32[2,136,128]{2,1,0:T(8,128)S(1)}, f32[2,136,128]{2,1,0:T(8,128)S(1)}, u32[]{:S(2)}, u32[]{:S(2)}) collective-permute-start(f32[2,136,128]{2,1,0:T(8,128)S(1)} %get-tuple-element.92), channel_id=1, source_target_pairs={{0,8},{4,12},{8,16},{12,20},{16,24},{20,28},{24,0},{28,4},{32,40},... | collective-permute-start | bytes 417800 | tf_op jit(solution)/shard_map/ppermute | solution.py:274
  36.5 8.1 %collective-permute-start.8 = (f32[2,136,128]{2,1,0:T(8,128)S(1)}, f32[2,136,128]{2,1,0:T(8,128)S(1)}, u32[]{:S(2)}, u32[]{:S(2)}) collective-permute-start(f32[2,136,128]{2,1,0:T(8,128)S(1)} %get-tuple-element.93), channel_id=1, source_target_pairs={{0,16},{4,20},{8,24},{12,28},{16,0},{20,4},{24,8},{28,12},{32,48},... | collective-permute-start | bytes 417800 | tf_op jit(solution)/shard_map/ppermute | solution.py:274
  38.7 5.9 %collective-permute-start.9 = (f32[2,136,128]{2,1,0:T(8,128)S(1)}, f32[2,136,128]{2,1,0:T(8,128)S(1)}, u32[]{:S(2)}, u32[]{:S(2)}) collective-permute-start(f32[2,136,128]{2,1,0:T(8,128)S(1)} %get-tuple-element.94), channel_id=1, source_target_pairs={{0,24},{4,28},{8,0},{12,4},{16,8},{20,12},{24,16},{28,20},{32,56},... | collective-permute-start | bytes 417800 | tf_op jit(solution)/shard_map/ppermute | solution.py:274
  45.2 4.6 %collective-permute-start.10 = (f32[8,136,128]{2,1,0:T(8,128)S(1)}, f32[8,136,128]{2,1,0:T(8,128)S(1)}, u32[]{:S(2)}, u32[]{:S(2)}) collective-permute-start(f32[8,136,128]{2,1,0:T(8,128)S(1)} %get-tuple-element.96), channel_id=1, source_target_pairs={{0,4},{4,0},{8,12},{12,8},{16,20},{20,16},{24,28},{28,24},{32,36},... | collective-permute-start | bytes 1671176 | tf_op jit(solution)/shard_map/ppermute | solution.py:279
  47.2 2.6 %copy-start = (f32[2048]{0:T(1024)S(1)}, f32[2048]{0:T(1024)}, u32[]{:S(2)}) copy-start(f32[2048]{0:T(1024)} %param.10) | copy-start | bytes 24580
  55.1 3.8 %collective-permute-start.13 = (f32[2,768]{1,0:T(2,128)S(1)}, f32[2,768]{1,0:T(2,128)S(1)}, u32[]{:S(2)}, u32[]{:S(2)}) collective-permute-start(f32[2,768]{1,0:T(2,128)S(1)} %get-tuple-element.99.refs_0_), channel_id=1, source_target_pairs={{0,3},{1,0},{2,1},{3,2},{4,7},{5,4},{6,5},{7,6},{8,11},{9,8},{10,9... | collective-permute-start | bytes 18440 | tf_op jit(solution)/shard_map/ppermute | solution.py:710
  57.9 4.0 %collective-permute-start.12 = (f32[2,768]{1,0:T(2,128)S(1)}, f32[2,768]{1,0:T(2,128)S(1)}, u32[]{:S(2)}, u32[]{:S(2)}) collective-permute-start(f32[2,768]{1,0:T(2,128)S(1)} %get-tuple-element.99.refs_0_), channel_id=1, source_target_pairs={{0,2},{1,3},{2,0},{3,1},{4,6},{5,7},{6,4},{7,5},{8,10},{9,11},{10,... | collective-permute-start | bytes 18440 | tf_op jit(solution)/shard_map/ppermute | solution.py:710
  58.2 3.7 %collective-permute-start.11 = (f32[2,768]{1,0:T(2,128)S(1)}, f32[2,768]{1,0:T(2,128)S(1)}, u32[]{:S(2)}, u32[]{:S(2)}) collective-permute-start(f32[2,768]{1,0:T(2,128)S(1)} %get-tuple-element.99.refs_0_), channel_id=1, source_target_pairs={{0,1},{1,2},{2,3},{3,0},{4,5},{5,6},{6,7},{7,4},{8,9},{9,10},{10,1... | collective-permute-start | bytes 18440 | tf_op jit(solution)/shard_map/ppermute | solution.py:710
  67.0 3.4 %collective-permute-start.14 = (f32[8,136,128]{2,1,0:T(8,128)S(1)}, f32[8,136,128]{2,1,0:T(8,128)S(1)}, u32[]{:S(2)}, u32[]{:S(2)}) collective-permute-start(f32[8,136,128]{2,1,0:T(8,128)S(1)} %get-tuple-element.101), channel_id=1, source_target_pairs={{0,4},{4,0},{8,12},{12,8},{16,20},{20,16},{24,28},{28,24},{32,36},... | collective-permute-start | bytes 1671176 | tf_op jit(solution)/shard_map/ppermute | solution.py:260
  71.0 10.8 %collective-permute-start.15 = (f32[2,136,128]{2,1,0:T(8,128)S(1)}, f32[2,136,128]{2,1,0:T(8,128)S(1)}, u32[]{:S(2)}, u32[]{:S(2)}) collective-permute-start(f32[2,136,128]{2,1,0:T(8,128)S(1)} %get-tuple-element.103), channel_id=1, source_target_pairs={{0,8},{4,12},{8,16},{12,20},{16,24},{20,28},{24,0},{28,4},{32,40},... | collective-permute-start | bytes 417800 | tf_op jit(solution)/shard_map/ppermute | solution.py:262
  71.9 9.9 %collective-permute-start.16 = (f32[2,136,128]{2,1,0:T(8,128)S(1)}, f32[2,136,128]{2,1,0:T(8,128)S(1)}, u32[]{:S(2)}, u32[]{:S(2)}) collective-permute-start(f32[2,136,128]{2,1,0:T(8,128)S(1)} %get-tuple-element.104), channel_id=1, source_target_pairs={{0,16},{4,20},{8,24},{12,28},{16,0},{20,4},{24,8},{28,12},{32,48},... | collective-permute-start | bytes 417800 | tf_op jit(solution)/shard_map/ppermute | solution.py:262
  74.1 7.7 %collective-permute-start.17 = (f32[2,136,128]{2,1,0:T(8,128)S(1)}, f32[2,136,128]{2,1,0:T(8,128)S(1)}, u32[]{:S(2)}, u32[]{:S(2)}) collective-permute-start(f32[2,136,128]{2,1,0:T(8,128)S(1)} %get-tuple-element.105), channel_id=1, source_target_pairs={{0,24},{4,28},{8,0},{12,4},{16,8},{20,12},{24,16},{28,20},{32,56},... | collective-permute-start | bytes 417800 | tf_op jit(solution)/shard_map/ppermute | solution.py:262
  82.5 8.9 %collective-permute-start.20 = (f32[2,136,128]{2,1,0:T(8,128)S(1)}, f32[2,136,128]{2,1,0:T(8,128)S(1)}, u32[]{:S(2)}, u32[]{:S(2)}) collective-permute-start(f32[2,136,128]{2,1,0:T(8,128)S(1)} %get-tuple-element.111.refs_0_), channel_id=1, source_target_pairs={{0,96},{4,100},{8,104},{12,108},{16,112},{20,116},{24,120},{28,124... | collective-permute-start | bytes 417800 | tf_op jit(solution)/shard_map/ppermute | solution.py:268
  82.6 8.8 %collective-permute-start.19 = (f32[2,136,128]{2,1,0:T(8,128)S(1)}, f32[2,136,128]{2,1,0:T(8,128)S(1)}, u32[]{:S(2)}, u32[]{:S(2)}) collective-permute-start(f32[2,136,128]{2,1,0:T(8,128)S(1)} %get-tuple-element.111.refs_0_), channel_id=1, source_target_pairs={{0,64},{4,68},{8,72},{12,76},{16,80},{20,84},{24,88},{28,92},{32,9... | collective-permute-start | bytes 417800 | tf_op jit(solution)/shard_map/ppermute | solution.py:268
  82.8 9.4 %collective-permute-start.18 = (f32[2,136,128]{2,1,0:T(8,128)S(1)}, f32[2,136,128]{2,1,0:T(8,128)S(1)}, u32[]{:S(2)}, u32[]{:S(2)}) collective-permute-start(f32[2,136,128]{2,1,0:T(8,128)S(1)} %get-tuple-element.111.refs_0_), channel_id=1, source_target_pairs={{0,32},{4,36},{8,40},{12,44},{16,48},{20,52},{24,56},{28,60},{32,6... | collective-permute-start | bytes 417800 | tf_op jit(solution)/shard_map/ppermute | solution.py:268
  92.9 9.0 %collective-permute-start.21 = (f32[2,136,128]{2,1,0:T(8,128)S(1)}, f32[2,136,128]{2,1,0:T(8,128)S(1)}, u32[]{:S(2)}, u32[]{:S(2)}) collective-permute-start(f32[2,136,128]{2,1,0:T(8,128)S(1)} %get-tuple-element.125), channel_id=1, source_target_pairs={{0,8},{4,12},{8,16},{12,20},{16,24},{20,28},{24,0},{28,4},{32,40},... | collective-permute-start | bytes 417800 | tf_op jit(solution)/shard_map/ppermute | solution.py:274
  93.9 9.0 %collective-permute-start.22 = (f32[2,136,128]{2,1,0:T(8,128)S(1)}, f32[2,136,128]{2,1,0:T(8,128)S(1)}, u32[]{:S(2)}, u32[]{:S(2)}) collective-permute-start(f32[2,136,128]{2,1,0:T(8,128)S(1)} %get-tuple-element.126), channel_id=1, source_target_pairs={{0,16},{4,20},{8,24},{12,28},{16,0},{20,4},{24,8},{28,12},{32,48},... | collective-permute-start | bytes 417800 | tf_op jit(solution)/shard_map/ppermute | solution.py:274
  96.7 6.3 %collective-permute-start.23 = (f32[2,136,128]{2,1,0:T(8,128)S(1)}, f32[2,136,128]{2,1,0:T(8,128)S(1)}, u32[]{:S(2)}, u32[]{:S(2)}) collective-permute-start(f32[2,136,128]{2,1,0:T(8,128)S(1)} %get-tuple-element.127), channel_id=1, source_target_pairs={{0,24},{4,28},{8,0},{12,4},{16,8},{20,12},{24,16},{28,20},{32,56},... | collective-permute-start | bytes 417800 | tf_op jit(solution)/shard_map/ppermute | solution.py:274
  103.6 3.0 %collective-permute-start.24 = (f32[8,136,128]{2,1,0:T(8,128)S(1)}, f32[8,136,128]{2,1,0:T(8,128)S(1)}, u32[]{:S(2)}, u32[]{:S(2)}) collective-permute-start(f32[8,136,128]{2,1,0:T(8,128)S(1)} %get-tuple-element.129), channel_id=1, source_target_pairs={{0,4},{4,0},{8,12},{12,8},{16,20},{20,16},{24,28},{28,24},{32,36},... | collective-permute-start | bytes 1671176 | tf_op jit(solution)/shard_map/ppermute | solution.py:279

commit v3 on v2

v3 whole, which is shorter than its diff:
```python
import functools

import jax
import jax.numpy as jnp
from jax import lax
from jax.experimental import pallas as pl
from jax.experimental.pallas import tpu as pltpu
from jax.sharding import PartitionSpec as P

HEAD_TOTAL = 64
DH = 128
SPAN = 128
ROWS = 8
PIECE = DH + ROWS
GROUP = 4
PAIR = 2
ALONG_X, ALONG_Z = 4, 4
F32 = jnp.float32
BF16 = jnp.bfloat16
EXACT = lax.Precision.HIGHEST
VMEM = pl.BlockSpec(memory_space=pltpu.VMEM)
SMEM = pl.BlockSpec(memory_space=pltpu.SMEM)
HBM = pl.BlockSpec(memory_space=pltpu.HBM)
ANY = pl.BlockSpec(memory_space=pl.ANY)


def dot(a, b, contract, precision=None):
    return lax.dot_general(
        a, b, ((contract[:1], contract[1:]), ((), ())), precision=precision, preferred_element_type=F32
    )


def nn(a, b):
    return dot(a, b, (1, 0))


def nt(a, b):
    return dot(a, b, (1, 1))


def params(mib):
    return pltpu.CompilerParams(vmem_limit_bytes=mib * 1024 * 1024)


def cost(flops, nbytes):
    return pl.CostEstimate(flops=int(flops), bytes_accessed=int(nbytes), transcendentals=0)


def head_rows(ref, head):
    return ref[pl.ds(pl.multiple_of(head * ROWS, ROWS), ROWS), :]


def head_lanes(head, count=1):
    return pl.ds(pl.multiple_of(head * DH, DH), count * DH)


def span(n):
    return slice(n * SPAN, (n + 1) * SPAN)


def last_lane(rows):
    return jnp.broadcast_to(rows[:, SPAN - 1 :], rows.shape)


def middle_lane(rows):
    return jnp.broadcast_to(rows[:, SPAN // 2 - 1 : SPAN // 2], rows.shape)


def masks():
    i = lax.broadcasted_iota(jnp.int32, (SPAN, SPAN), 0)
    j = lax.broadcasted_iota(jnp.int32, (SPAN, SPAN), 1)
    return i >= j, i <= j


def join_rows(rows, blocks):
    return jnp.concatenate([rows[n : n + 1] for n in range(blocks)], axis=1)


def piece_store(ref, at, state, extra):
    ref[at, :DH, :] = state
    ref[at, DH:, :] = extra


def extra_rows(decay, gain_row=None):
    place = lax.broadcasted_iota(jnp.int32, (ROWS, DH), 0)
    rest = 0.0 if gain_row is None else jnp.where(place == 1, gain_row, 0.0)
    return jnp.where(place == 0, decay, rest)


def half_heads(position_ref, of_other, at, heads):
    half = heads // 2
    start = (1 - position_ref[0]) if of_other else position_ref[0]
    return start * half + at


def decay_tables(log_ref, cum_ref, before_ref, total_ref):
    heads, rows = log_ref.shape
    _, triangle = masks()
    triangle = triangle.astype(F32)
    cum_ref[...] = jnp.zeros_like(cum_ref)
    before_ref[...] = jnp.zeros_like(before_ref)
    before = jnp.zeros((heads, SPAN), F32)
    for n in range(rows // SPAN):
        cum = dot(log_ref[:, span(n)], triangle, (1, 0), EXACT)
        for h in range(heads):
            cum_ref[h * ROWS + n : h * ROWS + n + 1, :] = cum[h : h + 1]
            before_ref[h * ROWS + n : h * ROWS + n + 1, :] = before[h : h + 1]
        before = before + last_lane(cum)
    for h in range(heads):
        total_ref[h * ROWS : (h + 1) * ROWS, :] = jnp.broadcast_to(before[h : h + 1], (ROWS, SPAN))


def state_body(of_other, position_ref, *refs):
    if of_other:
        k_hbm, v_hbm, log_hbm, out_ref, k_ref, v_ref, cum_ref, before_ref, total_ref, sems, log_ref, log_sem = refs
    else:
        k_ref, v_ref, cum_ref, before_ref, total_ref, out_ref = refs
    rows, width = k_ref.shape
    heads, blocks = width // DH, rows // SPAN
    copies = []
    if of_other:
        log_copy = pltpu.make_async_copy(log_hbm, log_ref, log_sem)
        log_copy.start()
        for g in range(heads // GROUP):
            lanes = head_lanes(lax.rem(half_heads(position_ref, True, g * GROUP, heads), heads), GROUP)
            for which, (source, target) in enumerate(((k_hbm, k_ref), (v_hbm, v_ref))):
                copies.append(pltpu.make_async_copy(source.at[:, lanes], target.at[:, lanes], sems.at[which, g]))
                copies[-1].start()
        log_copy.wait()
        decay_tables(log_ref, cum_ref, before_ref, total_ref)

    for g in range(heads // 2 // GROUP):
        first = half_heads(position_ref, of_other, g * GROUP, heads)
        if of_other:
            copies[2 * g].wait()
            copies[2 * g + 1].wait()
        totals = [head_rows(total_ref, first + at) for at in range(GROUP)]
        scales = [
            jnp.exp(totals[at] - head_rows(before_ref, first + at) - head_rows(cum_ref, first + at)) for at in range(GROUP)
        ]
        decayed = [
            (k_ref[:, head_lanes(first + at)].T.astype(F32) * join_rows(scales[at], blocks)).astype(BF16)
            for at in range(GROUP)
        ]
        states = [nn(decayed[at], v_ref[:, head_lanes(first + at)]) for at in range(GROUP)]
        for at in range(GROUP):
            piece_store(out_ref, g * GROUP + at, states[at], extra_rows(jnp.exp(totals[at])))
    for copy in copies[heads // GROUP :]:
        copy.wait()


def local_state(of_other, position, keys, values, more):
    rows, width = keys.shape
    heads = width // DH
    pieces = jax.ShapeDtypeStruct((heads // 2, PIECE, DH), F32)
    table = jax.ShapeDtypeStruct((heads * ROWS, SPAN), F32)
    like = jax.ShapeDtypeStruct(keys.shape, BF16)
    if of_other:
        specs, outs = [HBM] * 3, [pieces, like, like, table, table, table]
        scratch = [
            pltpu.SemaphoreType.DMA((2, heads // GROUP)),
            pltpu.VMEM(more[0].shape, F32),
            pltpu.SemaphoreType.DMA,
        ]
    else:
        specs, outs, scratch = [VMEM] * 5, [pieces], []
    return pl.pallas_call(
        functools.partial(state_body, of_other),
        in_specs=[SMEM] + specs,
        out_specs=[VMEM] * len(outs),
        out_shape=outs,
        scratch_shapes=scratch,
        compiler_params=params(4),
        cost_estimate=cost(heads * rows * DH * DH, 2 * rows * heads * DH),
        name="state_given" if of_other else "state_kept",
    )(position, keys, values, *more)


def first_row():
    return lax.broadcasted_iota(jnp.int32, (ROWS, DH), 0) == 0


def join_extra(a, b):
    return jnp.where(first_row(), a * b, a + b)


def cores_body(reverse, position_ref, own_ref, got_ref, *out_refs):
    z = position_ref[1]
    near_here = (position_ref[0] == 0) != reverse
    each = own_ref.shape[0] // ALONG_Z
    for shift, out_ref in enumerate(out_refs):
        for j in range(each):
            head = lax.rem(z + shift, ALONG_Z) * each + j
            own, got = own_ref[head], got_ref[head]
            near, far = jnp.where(near_here, own, got), jnp.where(near_here, got, own)
            piece_store(out_ref, j, far[DH : DH + 1] * near[:DH] + far[:DH], join_extra(near[DH:], far[DH:]))


def along_z_body(reverse, position_ref, *refs):
    in_refs, (_, total_ref, prefix_ref, slots) = refs[:ALONG_Z], refs[ALONG_Z:]
    z = position_ref[1]
    for shift, ref in enumerate(in_refs):
        slots[lax.rem(z - shift + ALONG_Z, ALONG_Z)] = ref[...]
    for j in range(total_ref.shape[0]):
        state = jnp.zeros((DH, DH), F32)
        extra = jnp.where(first_row(), 1.0, 0.0)
        for lap in range(ALONG_Z):
            at = ALONG_Z - 1 - lap if reverse else lap
            prefix_ref[at, j, :DH, :] = state
            prefix_ref[at, j, DH:, :] = extra
            state = slots[at, j, DH : DH + 1, :] * state + slots[at, j, :DH, :]
            extra = join_extra(extra, slots[at, j, DH:, :])
        piece_store(total_ref, j, state, extra)


def along_x_body(reverse, position_ref, *refs):
    in_refs, prefix_ref, out_refs, slots = refs[:ALONG_X], refs[ALONG_X], refs[ALONG_X + 2 : -1], refs[-1]
    z, x = position_ref[1], position_ref[2]
    for shift, ref in enumerate(in_refs):
        slots[lax.rem(x - shift + ALONG_X, ALONG_X)] = ref[...]
    for j in range(prefix_ref.shape[1]):
        state = jnp.zeros((DH, DH), F32)
        extra = jnp.zeros((ROWS, DH), F32)
        for lap in range(ALONG_X):
            at = ALONG_X - 1 - lap if reverse else lap
            taken = (at > x) if reverse else (at < x)
            state = jnp.where(taken, slots[at, j, DH : DH + 1, :] * state + slots[at, j, :DH, :], state)
            extra = extra + slots[at, j, DH:, :]
        for shift, out_ref in enumerate(out_refs):
            at = lax.rem(z + shift, ALONG_Z)
            piece_store(out_ref, j, prefix_ref[at, j, :DH, :] + prefix_ref[at, j, DH : DH + 1, :] * state, extra)


def entering_body(reverse, position_ref, *refs):
    in_refs, (own_ref, got_ref, _, keep_ref, give_ref) = refs[:ALONG_Z], refs[ALONG_Z:]
    z = position_ref[1]
    near_here = (position_ref[0] == 0) != reverse
    each = own_ref.shape[0] // ALONG_Z
    for shift, ref in enumerate(in_refs):
        for j in range(each):
            head = lax.rem(z - shift + ALONG_Z, ALONG_Z) * each + j
            near = jnp.where(near_here, own_ref[head], got_ref[head])
            entering, extra = ref[j, :DH, :], ref[j, DH:, :]
            passed = near[DH : DH + 1] * entering + near[:DH]
            piece_store(keep_ref, head, jnp.where(near_here, entering, passed), extra)
            piece_store(give_ref, head, jnp.where(near_here, passed, entering), extra)


def scan_step(body, name, reverse, position, arrays, after, out_counts, scratch):
    shapes = [jax.ShapeDtypeStruct(shape, F32) for shape in out_counts]
    afters = [] if after is None else [after]
    return pl.pallas_call(
        functools.partial(body, reverse),
        in_specs=[SMEM] + [VMEM] * len(arrays) + [ANY] * len(afters),
        out_specs=[VMEM] * len(shapes),
        out_shape=shapes,
        scratch_shapes=scratch,
        compiler_params=params(3),
        cost_estimate=cost(10**6, 10**6),
        name=name,
    )(position, *arrays, *afters)


def scan_over_seq(send, own, position, reverse, works):
    count = lax.axis_size("seq")
    heads = own.shape[0]
    each = heads // ALONG_Z

    def index(x, z, c):
        return (x % ALONG_X * ALONG_Z + z % ALONG_Z) * 2 + c

    every = [(x, z, c) for x in range(ALONG_X) for z in range(ALONG_Z) for c in range(2)]
    across = [(i, i ^ 1) for i in range(count)]
    by_z = [[(index(x, z, c), index(x, z + s, c)) for x, z, c in every] for s in range(ALONG_Z)]
    by_x = [[(index(x, z, c), index(x + s, z, c)) for x, z, c in every] for s in range(ALONG_X)]
    piece = (each, PIECE, DH)

    got = lax.ppermute(send, "seq", across)
    parts = scan_step(cores_body, "join_cores", reverse, position, [own, got], None, [piece] * ALONG_Z, [])
    arrived = [parts[0]] + [lax.ppermute(parts[s], "seq", by_z[s]) for s in range(1, ALONG_Z)]
    done = works[0](parts[0], ())
    total, prefix = scan_step(
        along_z_body, "join_z", reverse, position, arrived, done[-1],
        [piece, (ALONG_Z,) + piece], [pltpu.VMEM((ALONG_Z,) + piece, F32)],
    )
    totals = [total] + [lax.ppermute(total, "seq", by_x[s]) for s in range(1, ALONG_X)]
    done = works[1](total, done)
    parts = scan_step(
        along_x_body, "join_x", reverse, position, totals + [prefix], done[-1],
        [piece] * ALONG_Z, [pltpu.VMEM((ALONG_X,) + piece, F32)],
    )
    arrived = [parts[0]] + [lax.ppermute(parts[s], "seq", by_z[s]) for s in range(1, ALONG_Z)]
    done = works[2](parts[0], done)
    keep, give = scan_step(
        entering_body, "entering", reverse, position, arrived + [own, got], done[-1], [own.shape] * 2, []
    )
    return keep, lax.ppermute(give, "seq", across), done


def attend_pair(heads, q_ref, k_ref, v_ref, cum_ref, outs, both_masks):
    local_ref, low_ref, turned_ref, qs_ref, ks_ref, vs_ref, weights_ref = outs
    mask, turned_mask = both_masks
    blocks = k_ref.shape[0] // SPAN
    each = range(len(heads))
    steps = [(a, n) for n in range(blocks) for a in each]
    lanes = [head_lanes(h) for h in heads]
    cums = [head_rows(cum_ref, h) for h in heads]
    mids = [middle_lane(c) for c in cums]
    ends = [last_lane(c) for c in cums]
    query_col = [jnp.exp(c - m).T for c, m in zip(cums, mids)]
    key_col = [jnp.exp(m - c).T for c, m in zip(cums, mids)]
    mid_scale, end_scale = [jnp.exp(m) for m in mids], [jnp.exp(e) for e in ends]
    rest_scale = [jnp.exp(e - m) for e, m in zip(ends, mids)]
    q_up = {(a, n): (q_ref[span(n), lanes[a]].astype(F32) * query_col[a][:, n : n + 1]).astype(BF16) for a, n in steps}
    k_up = {(a, n): (k_ref[span(n), lanes[a]].astype(F32) * key_col[a][:, n : n + 1]).astype(BF16) for a, n in steps}
    v_up = {(a, n): (v_ref[span(n), lanes[a]].astype(F32) * key_col[a][:, n : n + 1]).astype(BF16) for a, n in steps}
    scores = {s: nt(q_up[s], k_up[s]) for s in steps}
    updates = {(a, n): nn(k_up[a, n].T, v_ref[span(n), lanes[a]]) for a, n in steps if n < blocks - 1}
    weights = {s: jnp.where(mask, scores[s], 0.0).astype(BF16) for s in steps}
    lows = {}
    for a in each:
        state = jnp.zeros((DH, DH), F32)
        for n in range(blocks):
            lows[a, n] = (mid_scale[a][n : n + 1] * state).astype(BF16)
            low_ref[heads[a], n] = lows[a, n]
            if n < blocks - 1:
                state = end_scale[a][n : n + 1] * state + rest_scale[a][n : n + 1] * updates[a, n]
    totals = {
        (a, n): nn(
            jnp.concatenate([weights[a, n], q_up[a, n]], axis=1),
            jnp.concatenate([v_ref[span(n), lanes[a]], lows[a, n]], axis=0),
        )
        for a, n in steps
    }
    turned_weights = {s: nt(k_up[s], q_up[s]) for s in steps}
    for a, n in steps:
        local_ref[span(n), lanes[a]] = totals[a, n].astype(BF16)
        qs_ref[span(n), lanes[a]] = q_up[a, n]
        ks_ref[span(n), lanes[a]] = k_up[a, n]
        vs_ref[span(n), lanes[a]] = v_up[a, n]
        weights_ref[heads[a], n] = jnp.where(turned_mask, turned_weights[a, n], 0.0).astype(BF16)
    for a in each:
        turned_ref[heads[a]] = jnp.concatenate([q_up[a, n].T for n in range(blocks)], axis=1)


def attend_body(first, count, load, *refs):
    k_ref, v_ref, cum_ref = refs[1:4]
    refs = refs[4:]
    copies = []
    if load == "queries":
        q_hbm, outs, (q_ref, sems) = refs[0], refs[1:8], refs[8:]
        for g in range(q_hbm.shape[1] // (GROUP * DH)):
            lanes = slice(g * GROUP * DH, (g + 1) * GROUP * DH)
            copies.append(pltpu.make_async_copy(q_hbm.at[:, lanes], q_ref.at[:, lanes], sems.at[g]))
    elif load == "grad_out":
        q_ref, go_hbm, outs, (go_ref, sems) = refs[0], refs[1], refs[9:16], refs[16:]
        copies.append(pltpu.make_async_copy(go_hbm, go_ref, sems.at[0]))
    else:
        q_ref, outs = refs[0], refs[8:15]
    for copy in copies:
        copy.start()
    both_masks = masks()

    def pairs(start, stop):
        @pl.loop(start // PAIR, stop // PAIR)
        def _(at):
            heads = [at * PAIR + a for a in range(PAIR)]
            attend_pair(heads, q_ref, k_ref, v_ref, cum_ref, outs, both_masks)

    if load == "queries":
        for g, copy in enumerate(copies):
            copy.wait()
            if g * GROUP < count:
                pairs(g * GROUP, min((g + 1) * GROUP, count))
    else:
        pairs(first, first + count)
        for copy in copies:
            copy.wait()


def attend(after, first, count, load, keys, values, cum, queries, grad_out, done):
    rows, width = keys.shape
    heads, blocks = width // DH, rows // SPAN
    like = jax.ShapeDtypeStruct((rows, width), BF16)
    squares = jax.ShapeDtypeStruct((heads, blocks, DH, DH), BF16)
    outs = [like, squares, jax.ShapeDtypeStruct((heads, DH, rows), BF16), like, like, like, squares]
    arrays, specs = [after, keys, values, cum, queries], [ANY, VMEM, VMEM, VMEM]
    specs.append(HBM if load == "queries" else VMEM)
    if load == "grad_out":
        arrays.append(grad_out)
        specs.append(HBM)
    aliases = {len(arrays) + i: i for i in range(len(done))}
    if load is not None:
        outs.append(like)
    return pl.pallas_call(
        functools.partial(attend_body, first, count, load),
        in_specs=specs + [VMEM] * len(done),
        out_specs=[VMEM] * len(outs),
        out_shape=outs,
        input_output_aliases=aliases,
        scratch_shapes=[] if load is None else [pltpu.SemaphoreType.DMA((heads // GROUP,))],
        compiler_params=params(6),
        cost_estimate=cost(10 * rows * count * DH * DH, 12 * rows * count * DH),
        name=f"attend_{first}",
    )(*arrays, *done)


def enter_body(of_other, position_ref, q_ref, local_ref, go_ref, gain_ref, state_ref, cum_ref, before_ref, *refs):
    if of_other:
        attn_ref, low_ref, stats_ref, square_ref, inner_ref = refs[4:]
    else:
        attn_ref, low_ref, square_ref, inner_ref = refs
    rows, width = q_ref.shape
    heads, blocks = width // DH, rows // SPAN
    if not of_other:
        square_ref[...] = jnp.zeros_like(square_ref)
        inner_ref[...] = jnp.zeros_like(inner_ref)

    @pl.loop(0, heads // 2 // GROUP)
    def _(g):
        first = half_heads(position_ref, of_other, g * GROUP, heads)
        lanes = [head_lanes(first + at) for at in range(GROUP)]
        carried, scales, gains = [], [], []
        for at in range(GROUP):
            low = state_ref[g * GROUP + at, :DH, :].astype(BF16)
            low_ref[first + at] = low
            carried.append(nn(q_ref[:, lanes[at]], low))
            scales.append(jnp.exp(middle_lane(head_rows(cum_ref, first + at)) + head_rows(before_ref, first + at)))
            gains.append(gain_ref[:, lanes[at]])
        for n in range(blocks):
            square = square_ref[span(n), :]
            inner = inner_ref[span(n), :]
            for at in range(GROUP):
                entered = carried[at][span(n)] * scales[at][n : n + 1]
                attn = (local_ref[span(n), lanes[at]].astype(F32) + entered).astype(BF16)
                attn_ref[span(n), lanes[at]] = attn
                attn = attn.astype(F32)
                square += attn * attn
                inner += go_ref[span(n), lanes[at]].astype(F32) * gains[at] * attn
            square_ref[span(n), :] = square
            inner_ref[span(n), :] = inner

    if of_other:
        ones = jnp.ones((8, DH), F32)
        stats_ref[0:1, :] = dot(ones, square_ref[...], (1, 1), EXACT)[0:1]
        stats_ref[1:2, :] = dot(ones, inner_ref[...], (1, 1), EXACT)[0:1]


def attend_entering(of_other, position, queries, local, grad_out, gain, state, cum, before, done):
    rows, width = queries.shape
    heads = width // DH
    sums = jax.ShapeDtypeStruct((rows, DH), F32)
    outs = [jax.ShapeDtypeStruct((rows, width), BF16), jax.ShapeDtypeStruct((heads, DH, DH), BF16)]
    if of_other:
        outs, aliases = outs + [jax.ShapeDtypeStruct((2, rows), F32), sums, sums], {8: 0, 9: 1, 10: 3, 11: 4}
    else:
        outs, aliases = outs + [sums, sums], {}
    return pl.pallas_call(
        functools.partial(enter_body, of_other),
        in_specs=[SMEM] + [VMEM] * (7 + len(done)),
        out_specs=[VMEM] * len(outs),
        out_shape=outs,
        input_output_aliases=aliases,
        compiler_params=params(4),
        cost_estimate=cost(rows * width * DH, 4 * rows * width),
        name="enter_taken" if of_other else "enter_kept",
    )(position, queries, local, grad_out, gain, state, cum, before, *done)


def columns(row, ref, blocks):
    for n in range(blocks):
        ref[span(n), :] = jnp.broadcast_to(row[:, span(n)], (SPAN, SPAN)).T


def norm_body(of_other, position_ref, turned_ref, attn_ref, go_ref, gain_ref, cum_ref, before_ref, total_ref, *refs):
    rows, width = attn_ref.shape
    heads, blocks = width // DH, rows // SPAN
    if of_other:
        stats_refs, (ga_ref, out_ref, inverse_ref, factor_ref) = refs[:-4], refs[-4:]
        stats = functools.reduce(jnp.add, [ref[...] for ref in stats_refs]) / (HEAD_TOTAL * DH)
        inverse = lax.rsqrt(stats[0:1] + 1e-06)
        columns(inverse, inverse_ref, blocks)
        columns(inverse * inverse * inverse * stats[1:2], factor_ref, blocks)
    else:
        inverse_ref, factor_ref, _, ga_ref, out_ref = refs

    @pl.loop(0, heads // 2 // GROUP)
    def _(g):
        places = [g * GROUP + at for at in range(GROUP)]
        heads_now = [half_heads(position_ref, of_other, place, heads) for place in places]
        lanes = [head_lanes(head) for head in heads_now]
        gains = [gain_ref[:, lane] for lane in lanes]
        gain_sums = [jnp.zeros((8, DH), F32) for _ in places]
        grads = [[] for _ in places]
        for n in range(blocks):
            for at in range(GROUP):
                attn = attn_ref[span(n), lanes[at]].astype(F32)
                scaled = go_ref[span(n), lanes[at]].astype(F32) * inverse_ref[span(n), :]
                gain_sums[at] += jnp.sum((scaled * attn).reshape(SPAN // 8, 8, DH), axis=0)
                grad = (scaled * gains[at] - attn * factor_ref[span(n), :]).astype(BF16)
                ga_ref[span(n), lanes[at]] = grad
                grads[at].append(grad)
        updates = [
            [nn(turned_ref[heads_now[at], :, span(n)], grads[at][n]) for n in range(blocks)] for at in range(GROUP)
        ]
        scales = [jnp.exp(middle_lane(head_rows(cum_ref, h)) + head_rows(before_ref, h)) for h in heads_now]
        states = [sum(scales[at][n : n + 1] * updates[at][n] for n in range(blocks)) for at in range(GROUP)]
        for at in range(GROUP):
            decay = jnp.exp(head_rows(total_ref, heads_now[at]))
            piece_store(out_ref, places[at], states[at], extra_rows(decay, jnp.sum(gain_sums[at], axis=0, keepdims=True)))


def norm_backward(of_other, position, turned, attn, grad_out, gain, cum, before, total, more):
    rows, width = attn.shape
    heads = width // DH
    pieces = jax.ShapeDtypeStruct((heads // 2, PIECE, DH), F32)
    cols = jax.ShapeDtypeStruct((rows, DH), F32)
    outs = [jax.ShapeDtypeStruct((rows, width), BF16), pieces] + ([cols, cols] if of_other else [])
    return pl.pallas_call(
        functools.partial(norm_body, of_other),
        in_specs=[SMEM] + [VMEM] * (7 + len(more)),
        out_specs=[VMEM] * len(outs),
        out_shape=outs,
        input_output_aliases={} if of_other else {10: 0},
        compiler_params=params(5),
        cost_estimate=cost(rows * width * DH, 4 * rows * width),
        name="norm_given" if of_other else "norm_kept",
    )(position, turned, attn, grad_out, gain, cum, before, total, *more)


def grads_pair(heads, places, refs, out_ref, gq_ref, lk_ref, lv_ref, both_masks):
    q_ref, k_ref, turned_ref, ks_ref, vs_ref, weights_ref, ga_ref, attn_ref = refs[:8]
    gain_ref, inverse_ref, low_ref, enter_ref, cum_ref, before_ref = refs[8:]
    mask, _ = both_masks
    blocks = k_ref.shape[0] // SPAN
    each = range(len(heads))
    steps = [(a, n) for n in range(blocks) for a in each]
    lanes = [head_lanes(h) for h in heads]
    here = [head_lanes(p) for p in places]
    cums = [head_rows(cum_ref, h) for h in heads]
    mids = [middle_lane(c) for c in cums]
    ends = [last_lane(c) for c in cums]
    query_col = [jnp.exp(c - m).T for c, m in zip(cums, mids)]
    mid_scale, end_scale = [jnp.exp(m) for m in mids], [jnp.exp(e) for e in ends]
    rest_scale = [jnp.exp(e - m) for e, m in zip(ends, mids)]
    enter_scale = [jnp.exp(m + head_rows(before_ref, h)) for m, h in zip(mids, heads)]
    entering = [enter_ref[h].astype(F32) for h in heads]

    def at(ref, a, n):
        return ref[span(n), lanes[a]]

    updates = {(a, n): nn(turned_ref[heads[a], :, span(n)], at(ga_ref, a, n)) for a, n in steps if n > 0}
    ga_up = {(a, n): (at(ga_ref, a, n).astype(F32) * query_col[a][:, n : n + 1]).astype(BF16) for a, n in steps}
    states = {
        (a, n): (low_ref[heads[a], n].astype(F32) + enter_scale[a][n : n + 1] * entering[a]).astype(BF16)
        for a, n in steps
    }
    from_query = {
        (a, n): nt(ga_up[a, n], jnp.concatenate([at(vs_ref, a, n), states[a, n]], axis=0)) for a, n in steps
    }
    lows = {}
    for a in each:
        back = jnp.zeros((DH, DH), F32)
        for n in reversed(range(blocks)):
            lows[a, n] = (rest_scale[a][n : n + 1] * back).astype(BF16)
            if n > 0:
                back = end_scale[a][n : n + 1] * back + mid_scale[a][n : n + 1] * updates[a, n]
    scores = {s: jnp.where(mask, from_query[s][:, :SPAN], 0.0).astype(BF16) for s in steps}
    from_key = {(a, n): nt(at(vs_ref, a, n), lows[a, n]) for a, n in steps}
    grad_v = {
        (a, n): nn(
            jnp.concatenate([weights_ref[heads[a], n], at(ks_ref, a, n)], axis=1),
            jnp.concatenate([at(ga_ref, a, n), lows[a, n]], axis=0),
        )
        for a, n in steps
    }
    grad_q = {(a, n): nn(scores[a, n], at(k_ref, a, n)) + from_query[a, n][:, SPAN:] for a, n in steps}
    grad_k = {(a, n): nn(scores[a, n].T, at(q_ref, a, n)) + from_key[a, n] for a, n in steps}
    for a, n in steps:
        gq_ref[span(n), here[a]] = grad_q[a, n].astype(BF16)
        lv_ref[span(n), lanes[a]] = grad_v[a, n].astype(BF16)
        lk_ref[span(n), lanes[a]] = grad_k[a, n].astype(BF16)
        normed = at(attn_ref, a, n).astype(F32) * inverse_ref[span(n), :]
        out_ref[span(n), here[a]] = (normed * gain_ref[:, lanes[a]]).astype(BF16)


def grads_body(first, count, chained, *refs):
    inputs = refs[1:15]
    refs = refs[15 + (4 if chained else 0) :]
    out_hbm, gq_hbm, lk_ref, lv_ref, out_ref, gq_ref, sems = refs
    both_masks = masks()

    def copies(at):
        here, there = head_lanes(at * PAIR, PAIR), head_lanes(first + at * PAIR, PAIR)
        return [
            pltpu.make_async_copy(out_ref.at[:, here], out_hbm.at[:, there], sems.at[0, at]),
            pltpu.make_async_copy(gq_ref.at[:, here], gq_hbm.at[:, there], sems.at[1, at]),
        ]

    @pl.loop(0, count // PAIR)
    def _(at):
        places = [at * PAIR + a for a in range(PAIR)]
        heads = [first + p for p in places]
        grads_pair(heads, places, inputs, out_ref, gq_ref, lk_ref, lv_ref, both_masks)
        for copy in copies(at):
            copy.start()

    @pl.loop(0, count // PAIR)
    def _(at):
        for copy in copies(at):
            copy.wait()


def grads_local(after, first, count, inputs, done):
    rows, width = inputs[0].shape
    like = jax.ShapeDtypeStruct((rows, width), BF16)
    kinds = [HBM, HBM, VMEM, VMEM]
    return pl.pallas_call(
        functools.partial(grads_body, first, count, bool(done)),
        in_specs=[ANY] + [VMEM] * 14 + (kinds if done else []),
        out_specs=kinds,
        out_shape=[like] * 4,
        input_output_aliases={15 + i: i for i in range(4)} if done else {},
        scratch_shapes=[
            pltpu.VMEM((rows, count * DH), BF16),
            pltpu.VMEM((rows, count * DH), BF16),
            pltpu.SemaphoreType.DMA((2, count // PAIR)),
        ],
        compiler_params=params(8),
        cost_estimate=cost(22 * rows * count * DH * DH, 24 * rows * count * DH),
        name=f"grads_{first}",
    )(after, *inputs, *done)


def leave_body(of_other, position_ref, k_ref, v_ref, lk_ref, lv_ref, state_ref, cum_ref, before_ref, total_ref, *refs):
    rows, width = k_ref.shape
    heads, blocks = width // DH, rows // SPAN
    half = heads // 2
    copies = []
    if of_other:
        kept_k_ref, kept_v_ref, kept_gain_ref, gk_hbm, gv_hbm, gg_ref, gk_ref, gv_ref, sems, kept_sems = refs
        there = head_lanes(half_heads(position_ref, False, 0, heads), half)
        for which, (source, target) in enumerate(((kept_k_ref, gk_hbm), (kept_v_ref, gv_hbm))):
            copies.append(pltpu.make_async_copy(source, target.at[:, there], kept_sems.at[which]))
            copies[-1].start()
        gg_ref[...] = kept_gain_ref[...]
    else:
        gk_ref, gv_ref, gg_ref = refs
    for g in range(half // GROUP):

        @pl.loop(g * GROUP // PAIR, (g + 1) * GROUP // PAIR)
        def _(at):
            first = half_heads(position_ref, of_other, at * PAIR, heads)
            lanes = [head_lanes(first + a) for a in range(PAIR)]
            here = [head_lanes(at * PAIR + a) for a in range(PAIR)]
            lows = [state_ref[at * PAIR + a, :DH, :].astype(BF16) for a in range(PAIR)]
            from_v = [nt(v_ref[:, lanes[a]], lows[a]) for a in range(PAIR)]
            from_k = [nn(k_ref[:, lanes[a]], lows[a]) for a in range(PAIR)]
            scales = [
                jnp.exp(
                    head_rows(total_ref, first + a)
                    - head_rows(before_ref, first + a)
                    - middle_lane(head_rows(cum_ref, first + a))
                )
                for a in range(PAIR)
            ]
            for n in range(blocks):
                for a in range(PAIR):
                    factor = scales[a][n : n + 1]
                    grad_k = lk_ref[span(n), lanes[a]].astype(F32) + factor * from_v[a][span(n)]
                    grad_v = lv_ref[span(n), lanes[a]].astype(F32) + factor * from_k[a][span(n)]
                    gk_ref[span(n), here[a]] = grad_k.astype(BF16)
                    gv_ref[span(n), here[a]] = grad_v.astype(BF16)
            for a in range(PAIR):
                gg_ref[:, lanes[a]] = state_ref[at * PAIR + a, DH + 1 : DH + 2, :]

        if of_other:
            here = slice(g * GROUP * DH, (g + 1) * GROUP * DH)
            there = head_lanes(half_heads(position_ref, True, g * GROUP, heads), GROUP)
            for which, (source, target) in enumerate(((gk_ref, gk_hbm), (gv_ref, gv_hbm))):
                copies.append(pltpu.make_async_copy(source.at[:, here], target.at[:, there], sems.at[which, g]))
                copies[-1].start()
    for copy in copies:
        copy.wait()


def grads_leaving(of_other, position, keys, values, local_k, local_v, state, cum, before, total, done):
    rows, width = keys.shape
    heads = width // DH
    like = jax.ShapeDtypeStruct((rows, width if of_other else width // 2), BF16)
    kept = pltpu.VMEM((rows, width // 2), BF16)
    sems = [pltpu.SemaphoreType.DMA((2, heads // 2 // GROUP)), pltpu.SemaphoreType.DMA((2,))]
    return pl.pallas_call(
        functools.partial(leave_body, of_other),
        in_specs=[SMEM] + [VMEM] * (8 + len(done)),
        out_specs=[HBM, HBM, VMEM] if of_other else [VMEM] * 3,
        out_shape=[like, like, jax.ShapeDtypeStruct((1, width), F32)],
        scratch_shapes=[kept, kept] + sems if of_other else [],
        compiler_params=params(6),
        cost_estimate=cost(2 * rows * width * DH, 6 * rows * width),
        name="leave_taken" if of_other else "leave_kept",
    )(position, keys, values, local_k, local_v, state, cum, before, total, *done)


def per_device(queries, keys, values, log_decay, gain, grad_out):
    place = lax.axis_index("seq")
    position = jnp.stack([place % 2, place // 2 % ALONG_Z, place // (2 * ALONG_Z)]).astype(jnp.int32)
    gain_row = gain.reshape(1, -1)
    keys, values, queries, grad_out, log_decay = (
        pltpu.with_memory_space_constraint(a, pltpu.HBM) for a in (keys, values, queries, grad_out, log_decay)
    )
    send, keys, values, cum, before, total = local_state(True, position, keys, values, (log_decay,))
    (own,) = local_state(False, position, keys, values, (cum, before, total))

    def attend_part(first, count, load):
        def run(after, done):
            held = done[7] if done else queries
            outs = attend(after, first, count, load, keys, values, cum, held, grad_out, done[:7])
            if load == "queries":
                return (*outs[:7], outs[7], outs[0])
            if load == "grad_out":
                return (*outs[:7], held, outs[7], outs[0])
            return (*outs[:7], held, done[8], outs[0])

        return run

    keep, taken, (local, lows, turned, q_up, k_up, v_up, weights, queries, grad_out, _) = scan_over_seq(
        send, own, position, False, [attend_part(0, 4, "queries"), attend_part(4, 6, "grad_out"), attend_part(10, 6, None)]
    )
    table = (cum, before)
    done = attend_entering(False, position, q_up, local, grad_out, gain_row, keep, *table, ())
    attn, entering, stats = attend_entering(True, position, q_up, local, grad_out, gain_row, taken, *table, done)[:3]
    count = lax.axis_size("head")
    stats = [stats] + [
        lax.ppermute(stats, "head", [(i, (i + s) % count) for i in range(count)]) for s in range(1, count)
    ]
    shared = (position, turned, attn, grad_out, gain_row, cum, before, total)
    grad_attn, send, inverse, factor = norm_backward(True, *shared, stats)
    grad_attn, own = norm_backward(False, *shared, (inverse, factor, grad_attn))
    inputs = (queries, keys, turned, k_up, v_up, weights, grad_attn, attn, gain_row, inverse, lows, entering, cum, before)

    def grads_part(first, count):
        return lambda after, done: grads_local(after, first, count, inputs, done)

    keep, taken, (output, grad_q, local_k, local_v) = scan_over_seq(
        send, own, position, True, [grads_part(0, 6), grads_part(6, 6), grads_part(12, 4)]
    )
    shared = (position, k_up, v_up, local_k, local_v)
    done = grads_leaving(False, *shared, keep, cum, before, total, ())
    grad_k, grad_v, grad_gain = grads_leaving(True, *shared, taken, cum, before, total, done)
    return output, grad_q, grad_k, grad_v, grad_gain.reshape(-1)


def solution(mesh):
    tokens, heads = P("seq", "head"), P("head")
    return jax.shard_map(
        per_device,
        mesh=mesh,
        in_specs=(tokens, tokens, tokens, P("head", "seq"), heads, tokens),
        out_specs=(tokens, tokens, tokens, tokens, heads),
        check_vma=False,
    )
```

time: 114 us -> 105 us (0.921)
  waiting for transfers between devices: 20 us -> 4.69 us
  starting transfers between devices: 33 us -> 39.8 us
    ppermute x6, waiting for transfers between devices: 5.04 us -> 0.02 us  [scan_over_seq(): lax.ppermute(total, 'seq', by_x[s])]
    pallas_call x3, Pallas kernels: 19.8 us -> 15.7 us  [grads_local(): pl.pallas_call(functools.partial(grads_body, first, count, bool(done)), i...]
    ppermute x12, waiting for transfers between devices: 7.24 us -> 3.26 us  [scan_over_seq(): lax.ppermute(parts[s], 'seq', by_z[s])]
    ppermute x6, starting transfers between devices: 5.2 us -> 8.76 us  [scan_over_seq(): lax.ppermute(total, 'seq', by_x[s])]
    ppermute x2, waiting for transfers between devices: 3.17 us -> 0.01 us  [scan_over_seq(): got = lax.ppermute(send, 'seq', across)]
    pallas_call x3, Pallas kernels: 11.7 us -> 14.4 us  [attend(): pl.pallas_call(functools.partial(attend_body, first, count, load), in_spe...]
    ppermute x2, starting transfers between devices: 3.39 us -> 5.82 us  [scan_over_seq(): return (keep, lax.ppermute(give, 'seq', across), done)]
    ppermute x3, waiting for transfers between devices: 3.01 us -> 1.41 us  [per_device(): lax.ppermute(stats, 'head', [(i, (i + s) % count) for i in range(count)])]
  transfers between devices with their start and end apart: 25 -> 25, of which waited for: 12 -> 7; matrix products, arithmetic and copies ran while one was open for 0% -> 0% of each run, Pallas kernels for 28% -> 38%
where the time goes in v3:
time: 105 us
  Pallas kernels  59.5 us (57%)
  starting transfers between devices  39.8 us (38%)
  waiting for transfers between devices  4.69 us (4%)
  between operations  1.13 us (1%)
    ppermute x12, starting transfers between devices, scan_over_seq(): lax.ppermute(parts[s], 'seq', by_z[s])  16.9 us
    pallas_call x3, Pallas kernels, grads_local(): pl.pallas_call(functools.partial(grads_body, first, count, bool(done)), i...  15.7 us
    pallas_call x3, Pallas kernels, attend(): pl.pallas_call(functools.partial(attend_body, first, count, load), in_spe...  14.4 us
    ppermute x6, starting transfers between devices, scan_over_seq(): lax.ppermute(total, 'seq', by_x[s])  8.76 us
    pallas_call x2, Pallas kernels, grads_leaving(): pl.pallas_call(functools.partial(leave_body, of_other), in_specs=[SMEM] +...  7.24 us
    pallas_call x2, Pallas kernels, attend_entering(): pl.pallas_call(functools.partial(enter_body, of_other), in_specs=[SMEM] +...  5.92 us
    ppermute x2, starting transfers between devices, scan_over_seq(): return (keep, lax.ppermute(give, 'seq', across), done)  5.82 us
    pallas_call x2, Pallas kernels, norm_backward(): pl.pallas_call(functools.partial(norm_body, of_other), in_specs=[SMEM] +...  5.68 us
  transfers between devices with their start and end apart: 25, of which 7 were waited for; matrix products, arithmetic and copies ran while one was open for 0% of the time, Pallas kernels for 38%

profile of v3, /device:TPU:1, one launch (start us, length us, event | category | flops | bytes accessed | tf_op | source)
XLA Modules:
  0.0 105.2 jit_solution(10201015228438485207)
XLA Ops:
  0.7 3.5 %state_given.1 = (f32[8,136,128]{2,1,0:T(8,128)S(1)}, bf16[768,2048]{1,0:T(8,128)(2,1)S(1)}, bf16[768,2048]{1,0:T(8,128)(2,1)S(1)}, f32[128,128]{1,0:T(8,128)S(1...) custom-call(s32[3]{0:T(128)S(1)} %pad_add_fusion.position_ref, bf16[768,2048]{1,0:T(8,128)(2,1)} %refs_0_.1, ...), custom_call_target="tpu_custom_call" | custom-call | flops 201326592 | bytes 3145728 | tf_op jit(solution)/shard_map/state_given/pallas_call | solution.py:167
  4.2 1.5 %collective-permute-start = (f32[8,136,128]{2,1,0:T(8,128)S(1)}, f32[8,136,128]{2,1,0:T(8,128)S(1)}, u32[]{:S(2)}, u32[]{:S(2)}) collective-permute-start(f32[8,136,128]{2,1,0:T(8,128)S(1)} %get-tuple-element.94), channel_id=1, source_target_pairs={{0,4},{4,0},{8,12},{12,8},{16,20},{20,16},{24,28},{28,24},{32,36},... | collective-permute-start | bytes 1671176 | tf_op jit(solution)/shard_map/ppermute | solution.py:278
  5.7 1.7 %state_kept.1.own_ref.refs_4_ = f32[8,136,128]{2,1,0:T(8,128)S(1)} custom-call(s32[3]{0:T(128)S(1)} %pad_add_fusion.position_ref, bf16[768,2048]{1,0:T(8,128)(2,1)S(1)} %get-tuple-element.89.refs_0_.refs_1_.refs_2_, bf16[768,2048]{1,0:T(8,128)(2,1)S(1)} %get-tuple-element.90.refs_1_.refs_2_, ...), custom_call_target="tpu_custom_call" | custom-call | flops 201326592 | bytes 3145728 | tf_op jit(solution)/shard_map/state_kept/pallas_call | solution.py:167
  7.5 0.6 join_cores.2
  8.1 1.8 %collective-permute-start.1 = (f32[2,136,128]{2,1,0:T(8,128)S(1)}, f32[2,136,128]{2,1,0:T(8,128)S(1)}, u32[]{:S(2)}, u32[]{:S(2)}) collective-permute-start(f32[2,136,128]{2,1,0:T(8,128)S(1)} %get-tuple-element.96), channel_id=1, source_target_pairs={{0,8},{4,12},{8,16},{12,20},{16,24},{20,28},{24,0},{28,4},{32,40},... | collective-permute-start | bytes 417800 | tf_op jit(solution)/shard_map/ppermute | solution.py:280
  9.9 3.3 %collective-permute-start.2 = (f32[2,136,128]{2,1,0:T(8,128)S(1)}, f32[2,136,128]{2,1,0:T(8,128)S(1)}, u32[]{:S(2)}, u32[]{:S(2)}) collective-permute-start(f32[2,136,128]{2,1,0:T(8,128)S(1)} %get-tuple-element.97), channel_id=1, source_target_pairs={{0,16},{4,20},{8,24},{12,28},{16,0},{20,4},{24,8},{28,12},{32,48},... | collective-permute-start | bytes 417800 | tf_op jit(solution)/shard_map/ppermute | solution.py:280
  13.2 0.7 collective-permute-start.3
  13.9 4.5 %attend_0.1 = (bf16[768,2048]{1,0:T(8,128)(2,1)S(1)}, bf16[16,6,128,128]{3,2,1,0:T(8,128)(2,1)S(1)}, bf16[16,128,768]{2,1,0:T(8,128)(2,1)S(1)}, bf16[768,2048]{1...) custom-call(f32[2,136,128]{2,1,0:T(8,128)S(1)} %get-tuple-element.95, ...), custom_call_target="tpu_custom_call" | custom-call | flops 503316480 | bytes 4718592 | tf_op jit(solution)/shard_map/attend_0/pallas_call | solution.py:395
  18.4 1.4 %collective-permute-done.2.refs_2_ = f32[2,136,128]{2,1,0:T(8,128)S(1)} collective-permute-done((f32[2,136,128]{2,1,0:T(8,128)S(1)}, f32[2,136,128]{2,1,0:T(8,128)S(1)}, u32[]{:S(2)}, u32[]{:S(2)}) %collective-permute-start.2) | collective-permute-done | bytes 139296 | tf_op jit(solution)/shard_map/ppermute | solution.py:280
  19.8 0.6 join_z.2
  20.4 1.3 %collective-permute-start.4 = (f32[2,136,128]{2,1,0:T(8,128)S(1)}, f32[2,136,128]{2,1,0:T(8,128)S(1)}, u32[]{:S(2)}, u32[]{:S(2)}) collective-permute-start(f32[2,136,128]{2,1,0:T(8,128)S(1)} %get-tuple-element.100.refs_0_), channel_id=1, source_target_pairs={{0,32},{4,36},{8,40},{12,44},{16,48},{20,52},{24,56},{28,60},{32,6... | collective-permute-start | bytes 417800 | tf_op jit(solution)/shard_map/ppermute | solution.py:286
  21.7 2.5 %collective-permute-start.5 = (f32[2,136,128]{2,1,0:T(8,128)S(1)}, f32[2,136,128]{2,1,0:T(8,128)S(1)}, u32[]{:S(2)}, u32[]{:S(2)}) collective-permute-start(f32[2,136,128]{2,1,0:T(8,128)S(1)} %get-tuple-element.100.refs_0_), channel_id=1, source_target_pairs={{0,64},{4,68},{8,72},{12,76},{16,80},{20,84},{24,88},{28,92},{32,9... | collective-permute-start | bytes 417800 | tf_op jit(solution)/shard_map/ppermute | solution.py:286
  24.2 1.2 %collective-permute-start.6 = (f32[2,136,128]{2,1,0:T(8,128)S(1)}, f32[2,136,128]{2,1,0:T(8,128)S(1)}, u32[]{:S(2)}, u32[]{:S(2)}) collective-permute-start(f32[2,136,128]{2,1,0:T(8,128)S(1)} %get-tuple-element.100.refs_0_), channel_id=1, source_target_pairs={{0,96},{4,100},{8,104},{12,108},{16,112},{20,116},{24,120},{28,124... | collective-permute-start | bytes 417800 | tf_op jit(solution)/shard_map/ppermute | solution.py:286
  25.3 5.0 %attend_4.1 = (bf16[768,2048]{1,0:T(8,128)(2,1)S(1)}, bf16[16,6,128,128]{3,2,1,0:T(8,128)(2,1)S(1)}, bf16[16,128,768]{2,1,0:T(8,128)(2,1)S(1)}, bf16[768,2048]{1...) custom-call(f32[2,136,128]{2,1,0:T(8,128)S(1)} %get-tuple-element.10, ...), custom_call_target="tpu_custom_call", output_to_operand_aliasing={{0}: (6, {}), {1}: (7, {}), {2}: (8, {}), {3}: (9, {}), {4}... | custom-call | flops 754974720 | bytes 7077888 | tf_op jit(solution)/shard_map/attend_4/pallas_call | solution.py:395
  30.4 0.7 join_x.2
  31.1 1.2 %collective-permute-start.7 = (f32[2,136,128]{2,1,0:T(8,128)S(1)}, f32[2,136,128]{2,1,0:T(8,128)S(1)}, u32[]{:S(2)}, u32[]{:S(2)}) collective-permute-start(f32[2,136,128]{2,1,0:T(8,128)S(1)} %get-tuple-element.121), channel_id=1, source_target_pairs={{0,8},{4,12},{8,16},{12,20},{16,24},{20,28},{24,0},{28,4},{32,40},... | collective-permute-start | bytes 417800 | tf_op jit(solution)/shard_map/ppermute | solution.py:292
  32.3 2.3 %collective-permute-start.8 = (f32[2,136,128]{2,1,0:T(8,128)S(1)}, f32[2,136,128]{2,1,0:T(8,128)S(1)}, u32[]{:S(2)}, u32[]{:S(2)}) collective-permute-start(f32[2,136,128]{2,1,0:T(8,128)S(1)} %get-tuple-element.122), channel_id=1, source_target_pairs={{0,16},{4,20},{8,24},{12,28},{16,0},{20,4},{24,8},{28,12},{32,48},... | collective-permute-start | bytes 417800 | tf_op jit(solution)/shard_map/ppermute | solution.py:292
  34.8 5.0 %attend_10.1 = (bf16[768,2048]{1,0:T(8,128)(2,1)S(1)}, bf16[16,6,128,128]{3,2,1,0:T(8,128)(2,1)S(1)}, bf16[16,128,768]{2,1,0:T(8,128)(2,1)S(1)}, bf16[768,2048]{...) custom-call(f32[2,136,128]{2,1,0:T(8,128)S(1)} %get-tuple-element.11, ...), custom_call_target="tpu_custom_call", output_to_operand_aliasing={{0}: (5, {}), {1}: (6, {}), {2}: (7, {}), {3}: (8, {}), {4}... | custom-call | flops 754974720 | bytes 7077888 | tf_op jit(solution)/shard_map/attend_10/pallas_call | solution.py:395
  39.9 0.7 entering.2
  40.6 3.3 %collective-permute-start.10 = (f32[8,136,128]{2,1,0:T(8,128)S(1)}, f32[8,136,128]{2,1,0:T(8,128)S(1)}, u32[]{:S(2)}, u32[]{:S(2)}) collective-permute-start(f32[8,136,128]{2,1,0:T(8,128)S(1)} %get-tuple-element.124), channel_id=1, source_target_pairs={{0,4},{4,0},{8,12},{12,8},{16,20},{20,16},{24,28},{28,24},{32,36},... | collective-permute-start | bytes 1671176 | tf_op jit(solution)/shard_map/ppermute | solution.py:297
  43.9 2.6 %enter_kept.1 = (bf16[768,2048]{1,0:T(8,128)(2,1)S(1)}, bf16[16,128,128]{2,1,0:T(8,128)(2,1)S(1)}, f32[768,128]{1,0:T(8,128)S(1)}, f32[768,128]{1,0:T(8,128)S(1)}) custom-call(s32[3]{0:T(128)S(1)} %pad_add_fusion.position_ref, bf16[768,2048]{1,0:T(8,128)(2,1)S(1)} %get-tuple-element.118.q_ref, bf16[768,2048]{1,0:T(8,128)(2,1)S(1)} %get-tuple-element.119.refs_6_.local_ref, ...), custom_call_target="tpu_custom_call" | custom-call | flops 201326592 | bytes 6291456 | tf_op jit(solution)/shard_map/enter_kept/pallas_call | solution.py:458
  46.5 3.3 %enter_taken.1 = (bf16[768,2048]{1,0:T(8,128)(2,1)S(1)}, bf16[16,128,128]{2,1,0:T(8,128)(2,1)S(1)}, f32[2,768]{1,0:T(2,128)S(1)}, f32[768,128]{1,0:T(8,128)S(1)}, f32[768,128]{1,0:T(8,128)S(1)}) custom-call(s32[3]{0:T(128)S(1)} %pad_add_fusion.position_ref, ...), custom_call_target="tpu_custom_call", output_to_operand_aliasing={{0}: (8, {}), {1}: (9, {}), {3}: (10, {}), {4}: (11, {})} | custom-call | flops 201326592 | bytes 6291456 | tf_op jit(solution)/shard_map/enter_taken/pallas_call | solution.py:458
  49.8 1.3 %collective-permute-start.11 = (f32[2,768]{1,0:T(2,128)S(1)}, f32[2,768]{1,0:T(2,128)S(1)}, u32[]{:S(2)}, u32[]{:S(2)}) collective-permute-start(f32[2,768]{1,0:T(2,128)S(1)} %get-tuple-element.131.refs_0_), channel_id=1, source_target_pairs={{0,1},{1,2},{2,3},{3,0},{4,5},{5,6},{6,7},{7,4},{8,9},{9,10},{10,1... | collective-permute-start | bytes 18440 | tf_op jit(solution)/shard_map/ppermute | solution.py:735
  51.1 2.6 %collective-permute-start.12 = (f32[2,768]{1,0:T(2,128)S(1)}, f32[2,768]{1,0:T(2,128)S(1)}, u32[]{:S(2)}, u32[]{:S(2)}) collective-permute-start(f32[2,768]{1,0:T(2,128)S(1)} %get-tuple-element.131.refs_0_), channel_id=1, source_target_pairs={{0,2},{1,3},{2,0},{3,1},{4,6},{5,7},{6,4},{7,5},{8,10},{9,11},{10,... | collective-permute-start | bytes 18440 | tf_op jit(solution)/shard_map/ppermute | solution.py:735
  53.7 1.1 %collective-permute-start.13 = (f32[2,768]{1,0:T(2,128)S(1)}, f32[2,768]{1,0:T(2,128)S(1)}, u32[]{:S(2)}, u32[]{:S(2)}) collective-permute-start(f32[2,768]{1,0:T(2,128)S(1)} %get-tuple-element.131.refs_0_), channel_id=1, source_target_pairs={{0,3},{1,0},{2,1},{3,2},{4,7},{5,4},{6,5},{7,6},{8,11},{9,8},{10,9... | collective-permute-start | bytes 18440 | tf_op jit(solution)/shard_map/ppermute | solution.py:735
  55.1 1.1 %collective-permute-done.13.refs_3_ = f32[2,768]{1,0:T(2,128)S(1)} collective-permute-done((f32[2,768]{1,0:T(2,128)S(1)}, f32[2,768]{1,0:T(2,128)S(1)}, u32[]{:S(2)}, u32[]{:S(2)}) %collective-permute-start.13) | collective-permute-done | bytes 6176 | tf_op jit(solution)/shard_map/ppermute | solution.py:735
  56.2 3.0 %norm_given.1 = (bf16[768,2048]{1,0:T(8,128)(2,1)S(1)}, f32[8,136,128]{2,1,0:T(8,128)S(1)}, f32[768,128]{1,0:T(8,128)S(1)}, f32[768,128]{1,0:T(8,128)S(1)}) custom-call(s32[3]{0:T(128)S(1)} %pad_add_fusion.position_ref, bf16[16,128,768]{2,1,0:T(8,128)(2,1)S(1)} %get-tuple-element.117.turned_ref.refs_3_, ...), custom_call_target="tpu_custom_call" | custom-call | flops 201326592 | bytes 6291456 | tf_op jit(solution)/shard_map/norm_given/pallas_call | solution.py:519
  59.2 1.8 %collective-permute-start.14 = (f32[8,136,128]{2,1,0:T(8,128)S(1)}, f32[8,136,128]{2,1,0:T(8,128)S(1)}, u32[]{:S(2)}, u32[]{:S(2)}) collective-permute-start(f32[8,136,128]{2,1,0:T(8,128)S(1)} %get-tuple-element.136), channel_id=1, source_target_pairs={{0,4},{4,0},{8,12},{12,8},{16,20},{20,16},{24,28},{28,24},{32,36},... | collective-permute-start | bytes 1671176 | tf_op jit(solution)/shard_map/ppermute | solution.py:278
  61.0 2.7 %norm_kept.1 = (bf16[768,2048]{1,0:T(8,128)(2,1)S(1)}, f32[8,136,128]{2,1,0:T(8,128)S(1)}) custom-call(s32[3]{0:T(128)S(1)} %pad_add_fusion.position_ref, bf16[16,128,768]{2,1,0:T(8,128)(2,1)S(1)} %get-tuple-element.117.turned_ref.refs_3_, bf16[768,2048]{1,0:T(8,128)(2,1)S(1)} %get-tuple-element.130.attn_ref.refs_8_, ...), custom_call_target="tpu_custom_call", output_to_operand_aliasing={{0}: (10, {})} | custom-call | flops 201326592 | bytes 6291456 | tf_op jit(solution)/shard_map/norm_kept/pallas_call | solution.py:519
  63.7 0.6 join_cores.3
  64.3 0.6 collective-permute-start.15
  64.9 2.4 %collective-permute-start.16 = (f32[2,136,128]{2,1,0:T(8,128)S(1)}, f32[2,136,128]{2,1,0:T(8,128)S(1)}, u32[]{:S(2)}, u32[]{:S(2)}) collective-permute-start(f32[2,136,128]{2,1,0:T(8,128)S(1)} %get-tuple-element.139), channel_id=1, source_target_pairs={{0,16},{4,20},{8,24},{12,28},{16,0},{20,4},{24,8},{28,12},{32,48},... | collective-permute-start | bytes 417800 | tf_op jit(solution)/shard_map/ppermute | solution.py:280
  67.5 5.8 %grads_0.1 = (bf16[768,2048]{1,0:T(8,128)(2,1)}, bf16[768,2048]{1,0:T(8,128)(2,1)}, bf16[768,2048]{1,0:T(8,128)(2,1)S(1)}, bf16[768,2048]{1,0:T(8,128)(2,1)S(1)}) custom-call(f32[2,136,128]{2,1,0:T(8,128)S(1)} %get-tuple-element.137.refs_0_, bf16[768,2048]{1,0:T(8,128)(2,1)S(1)} %get-tuple-element.102.refs_4_.refs_1_, ...), custom_call_target="tpu_custom_call" | custom-call | flops 1660944384 | bytes 14155776 | tf_op jit(solution)/shard_map/grads_0/pallas_call | solution.py:618
  73.3 0.8 collective-permute-done.16.refs_2_
  74.2 0.6 join_z.3
  74.8 0.7 collective-permute-start.18
  75.5 2.4 %collective-permute-start.19 = (f32[2,136,128]{2,1,0:T(8,128)S(1)}, f32[2,136,128]{2,1,0:T(8,128)S(1)}, u32[]{:S(2)}, u32[]{:S(2)}) collective-permute-start(f32[2,136,128]{2,1,0:T(8,128)S(1)} %get-tuple-element.148.refs_0_), channel_id=1, source_target_pairs={{0,64},{4,68},{8,72},{12,76},{16,80},{20,84},{24,88},{28,92},{32,9... | collective-permute-start | bytes 417800 | tf_op jit(solution)/shard_map/ppermute | solution.py:286
  78.0 0.7 collective-permute-start.20
  78.7 5.8 %grads_6.1 = (bf16[768,2048]{1,0:T(8,128)(2,1)}, bf16[768,2048]{1,0:T(8,128)(2,1)}, bf16[768,2048]{1,0:T(8,128)(2,1)S(1)}, bf16[768,2048]{1,0:T(8,128)(2,1)S(1)}) custom-call(f32[2,136,128]{2,1,0:T(8,128)S(1)} %get-tuple-element.148.refs_0_, ...), custom_call_target="tpu_custom_call", output_to_operand_aliasing={{0}: (15, {}), {1}: (16, {}), {2}: (17, {}), {3}: (18, {})} | custom-call | flops 1660944384 | bytes 14155776 | tf_op jit(solution)/shard_map/grads_6/pallas_call | solution.py:618
  84.6 0.7 join_x.3
  85.2 1.6 %collective-permute-start.21 = (f32[2,136,128]{2,1,0:T(8,128)S(1)}, f32[2,136,128]{2,1,0:T(8,128)S(1)}, u32[]{:S(2)}, u32[]{:S(2)}) collective-permute-start(f32[2,136,128]{2,1,0:T(8,128)S(1)} %get-tuple-element.162), channel_id=1, source_target_pairs={{0,8},{4,12},{8,16},{12,20},{16,24},{20,28},{24,0},{28,4},{32,40},... | collective-permute-start | bytes 417800 | tf_op jit(solution)/shard_map/ppermute | solution.py:292
  86.9 2.5 %collective-permute-start.22 = (f32[2,136,128]{2,1,0:T(8,128)S(1)}, f32[2,136,128]{2,1,0:T(8,128)S(1)}, u32[]{:S(2)}, u32[]{:S(2)}) collective-permute-start(f32[2,136,128]{2,1,0:T(8,128)S(1)} %get-tuple-element.163), channel_id=1, source_target_pairs={{0,16},{4,20},{8,24},{12,28},{16,0},{20,4},{24,8},{28,12},{32,48},... | collective-permute-start | bytes 417800 | tf_op jit(solution)/shard_map/ppermute | solution.py:292
  89.4 4.1 %grads_12.1 = (bf16[768,2048]{1,0:T(8,128)(2,1)}, bf16[768,2048]{1,0:T(8,128)(2,1)}, bf16[768,2048]{1,0:T(8,128)(2,1)S(1)}, bf16[768,2048]{1,0:T(8,128)(2,1)S(1)}) custom-call(f32[2,136,128]{2,1,0:T(8,128)S(1)} %get-tuple-element.154.refs_0_, ...), custom_call_target="tpu_custom_call", output_to_operand_aliasing={{0}: (15, {}), {1}: (16, {}), {2}: (17, {}), {3}: (18, {})} | custom-call | flops 1107296256 | bytes 9437184 | tf_op jit(solution)/shard_map/grads_12/pallas_call | solution.py:618
  93.6 0.9 collective-permute-done.22.refs_2_
  94.5 0.7 entering.3
  95.2 2.5 %collective-permute-start.24 = (f32[8,136,128]{2,1,0:T(8,128)S(1)}, f32[8,136,128]{2,1,0:T(8,128)S(1)}, u32[]{:S(2)}, u32[]{:S(2)}) collective-permute-start(f32[8,136,128]{2,1,0:T(8,128)S(1)} %get-tuple-element.165), channel_id=1, source_target_pairs={{0,4},{4,0},{8,12},{12,8},{16,20},{20,16},{24,28},{28,24},{32,36},... | collective-permute-start | bytes 1671176 | tf_op jit(solution)/shard_map/ppermute | solution.py:297
  97.7 2.8 %leave_kept.1 = (bf16[768,1024]{1,0:T(8,128)(2,1)S(1)}, bf16[768,1024]{1,0:T(8,128)(2,1)S(1)}, f32[1,2048]{1,0:T(1,128)S(1)}) custom-call(s32[3]{0:T(128)S(1)} %pad_add_fusion.position_ref, bf16[768,2048]{1,0:T(8,128)(2,1)S(1)} %get-tuple-element.141.refs_4_.k_ref, bf16[768,2048]{1,0:T(8,128)(2,1)S(1)} %get-tuple-element.142.refs_5_.v_ref, ...), custom_call_target="tpu_custom_call" | custom-call | flops 402653184 | bytes 9437184 | tf_op jit(solution)/shard_map/leave_kept/pallas_call | solution.py:693
  100.6 4.4 %leave_taken.1 = (bf16[768,2048]{1,0:T(8,128)(2,1)}, bf16[768,2048]{1,0:T(8,128)(2,1)}, f32[1,2048]{1,0:T(1,128)}) custom-call(s32[3]{0:T(128)S(1)} %pad_add_fusion.position_ref, bf16[768,2048]{1,0:T(8,128)(2,1)S(1)} %get-tuple-element.141.refs_4_.k_ref, bf16[768,2048]{1,0:T(8,128)(2,1)S(1)} %get-tuple-element.142.refs_5_.v_ref, ...), custom_call_target="tpu_custom_call" | custom-call | flops 402653184 | bytes 9437184 | tf_op jit(solution)/shard_map/leave_taken/pallas_call | solution.py:693
  (31 shorter events, 1.1 us)
Async XLA Ops:
  4.2 3.2 %collective-permute-start = (f32[8,136,128]{2,1,0:T(8,128)S(1)}, f32[8,136,128]{2,1,0:T(8,128)S(1)}, u32[]{:S(2)}, u32[]{:S(2)}) collective-permute-start(f32[8,136,128]{2,1,0:T(8,128)S(1)} %get-tuple-element.94), channel_id=1, source_target_pairs={{0,4},{4,0},{8,12},{12,8},{16,20},{20,16},{24,28},{28,24},{32,36},... | collective-permute-start | bytes 1671176 | tf_op jit(solution)/shard_map/ppermute | solution.py:278
  8.1 10.3 %collective-permute-start.1 = (f32[2,136,128]{2,1,0:T(8,128)S(1)}, f32[2,136,128]{2,1,0:T(8,128)S(1)}, u32[]{:S(2)}, u32[]{:S(2)}) collective-permute-start(f32[2,136,128]{2,1,0:T(8,128)S(1)} %get-tuple-element.96), channel_id=1, source_target_pairs={{0,8},{4,12},{8,16},{12,20},{16,24},{20,28},{24,0},{28,4},{32,40},... | collective-permute-start | bytes 417800 | tf_op jit(solution)/shard_map/ppermute | solution.py:280
  9.9 9.9 %collective-permute-start.2 = (f32[2,136,128]{2,1,0:T(8,128)S(1)}, f32[2,136,128]{2,1,0:T(8,128)S(1)}, u32[]{:S(2)}, u32[]{:S(2)}) collective-permute-start(f32[2,136,128]{2,1,0:T(8,128)S(1)} %get-tuple-element.97), channel_id=1, source_target_pairs={{0,16},{4,20},{8,24},{12,28},{16,0},{20,4},{24,8},{28,12},{32,48},... | collective-permute-start | bytes 417800 | tf_op jit(solution)/shard_map/ppermute | solution.py:280
  13.2 6.6 %collective-permute-start.3 = (f32[2,136,128]{2,1,0:T(8,128)S(1)}, f32[2,136,128]{2,1,0:T(8,128)S(1)}, u32[]{:S(2)}, u32[]{:S(2)}) collective-permute-start(f32[2,136,128]{2,1,0:T(8,128)S(1)} %get-tuple-element.98), channel_id=1, source_target_pairs={{0,24},{4,28},{8,0},{12,4},{16,8},{20,12},{24,16},{28,20},{32,56},... | collective-permute-start | bytes 417800 | tf_op jit(solution)/shard_map/ppermute | solution.py:280
  20.4 9.9 %collective-permute-start.4 = (f32[2,136,128]{2,1,0:T(8,128)S(1)}, f32[2,136,128]{2,1,0:T(8,128)S(1)}, u32[]{:S(2)}, u32[]{:S(2)}) collective-permute-start(f32[2,136,128]{2,1,0:T(8,128)S(1)} %get-tuple-element.100.refs_0_), channel_id=1, source_target_pairs={{0,32},{4,36},{8,40},{12,44},{16,48},{20,52},{24,56},{28,60},{32,6... | collective-permute-start | bytes 417800 | tf_op jit(solution)/shard_map/ppermute | solution.py:286
  21.7 8.6 %collective-permute-start.5 = (f32[2,136,128]{2,1,0:T(8,128)S(1)}, f32[2,136,128]{2,1,0:T(8,128)S(1)}, u32[]{:S(2)}, u32[]{:S(2)}) collective-permute-start(f32[2,136,128]{2,1,0:T(8,128)S(1)} %get-tuple-element.100.refs_0_), channel_id=1, source_target_pairs={{0,64},{4,68},{8,72},{12,76},{16,80},{20,84},{24,88},{28,92},{32,9... | collective-permute-start | bytes 417800 | tf_op jit(solution)/shard_map/ppermute | solution.py:286
  24.2 6.2 %collective-permute-start.6 = (f32[2,136,128]{2,1,0:T(8,128)S(1)}, f32[2,136,128]{2,1,0:T(8,128)S(1)}, u32[]{:S(2)}, u32[]{:S(2)}) collective-permute-start(f32[2,136,128]{2,1,0:T(8,128)S(1)} %get-tuple-element.100.refs_0_), channel_id=1, source_target_pairs={{0,96},{4,100},{8,104},{12,108},{16,112},{20,116},{24,120},{28,124... | collective-permute-start | bytes 417800 | tf_op jit(solution)/shard_map/ppermute | solution.py:286
  31.1 8.8 %collective-permute-start.7 = (f32[2,136,128]{2,1,0:T(8,128)S(1)}, f32[2,136,128]{2,1,0:T(8,128)S(1)}, u32[]{:S(2)}, u32[]{:S(2)}) collective-permute-start(f32[2,136,128]{2,1,0:T(8,128)S(1)} %get-tuple-element.121), channel_id=1, source_target_pairs={{0,8},{4,12},{8,16},{12,20},{16,24},{20,28},{24,0},{28,4},{32,40},... | collective-permute-start | bytes 417800 | tf_op jit(solution)/shard_map/ppermute | solution.py:292
  32.3 7.6 %collective-permute-start.8 = (f32[2,136,128]{2,1,0:T(8,128)S(1)}, f32[2,136,128]{2,1,0:T(8,128)S(1)}, u32[]{:S(2)}, u32[]{:S(2)}) collective-permute-start(f32[2,136,128]{2,1,0:T(8,128)S(1)} %get-tuple-element.122), channel_id=1, source_target_pairs={{0,16},{4,20},{8,24},{12,28},{16,0},{20,4},{24,8},{28,12},{32,48},... | collective-permute-start | bytes 417800 | tf_op jit(solution)/shard_map/ppermute | solution.py:292
  34.6 5.3 %collective-permute-start.9 = (f32[2,136,128]{2,1,0:T(8,128)S(1)}, f32[2,136,128]{2,1,0:T(8,128)S(1)}, u32[]{:S(2)}, u32[]{:S(2)}) collective-permute-start(f32[2,136,128]{2,1,0:T(8,128)S(1)} %get-tuple-element.123), channel_id=1, source_target_pairs={{0,24},{4,28},{8,0},{12,4},{16,8},{20,12},{24,16},{28,20},{32,56},... | collective-permute-start | bytes 417800 | tf_op jit(solution)/shard_map/ppermute | solution.py:292
  39.8 6.6 %copy-start = (bf16[16,6,128,128]{3,2,1,0:T(8,128)(2,1)}, bf16[16,6,128,128]{3,2,1,0:T(8,128)(2,1)S(1)}, u32[]{:S(2)}) copy-start(bf16[16,6,128,128]{3,2,1,0:T(8,128)(2,1)S(1)} %get-tuple-element.143.refs_6_) | copy-start | bytes 9437188
  39.8 4.0 %copy-start.2 = (f32[2048]{0:T(1024)S(1)}, f32[2048]{0:T(1024)}, u32[]{:S(2)}) copy-start(f32[2048]{0:T(1024)} %param.10) | copy-start | bytes 24580
  40.6 5.9 %collective-permute-start.10 = (f32[8,136,128]{2,1,0:T(8,128)S(1)}, f32[8,136,128]{2,1,0:T(8,128)S(1)}, u32[]{:S(2)}, u32[]{:S(2)}) collective-permute-start(f32[8,136,128]{2,1,0:T(8,128)S(1)} %get-tuple-element.124), channel_id=1, source_target_pairs={{0,4},{4,0},{8,12},{12,8},{16,20},{20,16},{24,28},{28,24},{32,36},... | collective-permute-start | bytes 1671176 | tf_op jit(solution)/shard_map/ppermute | solution.py:297
  49.8 5.0 %collective-permute-start.11 = (f32[2,768]{1,0:T(2,128)S(1)}, f32[2,768]{1,0:T(2,128)S(1)}, u32[]{:S(2)}, u32[]{:S(2)}) collective-permute-start(f32[2,768]{1,0:T(2,128)S(1)} %get-tuple-element.131.refs_0_), channel_id=1, source_target_pairs={{0,1},{1,2},{2,3},{3,0},{4,5},{5,6},{6,7},{7,4},{8,9},{9,10},{10,1... | collective-permute-start | bytes 18440 | tf_op jit(solution)/shard_map/ppermute | solution.py:735
  51.1 4.0 %collective-permute-start.12 = (f32[2,768]{1,0:T(2,128)S(1)}, f32[2,768]{1,0:T(2,128)S(1)}, u32[]{:S(2)}, u32[]{:S(2)}) collective-permute-start(f32[2,768]{1,0:T(2,128)S(1)} %get-tuple-element.131.refs_0_), channel_id=1, source_target_pairs={{0,2},{1,3},{2,0},{3,1},{4,6},{5,7},{6,4},{7,5},{8,10},{9,11},{10,... | collective-permute-start | bytes 18440 | tf_op jit(solution)/shard_map/ppermute | solution.py:735
  53.7 2.5 %collective-permute-start.13 = (f32[2,768]{1,0:T(2,128)S(1)}, f32[2,768]{1,0:T(2,128)S(1)}, u32[]{:S(2)}, u32[]{:S(2)}) collective-permute-start(f32[2,768]{1,0:T(2,128)S(1)} %get-tuple-element.131.refs_0_), channel_id=1, source_target_pairs={{0,3},{1,0},{2,1},{3,2},{4,7},{5,4},{6,5},{7,6},{8,11},{9,8},{10,9... | collective-permute-start | bytes 18440 | tf_op jit(solution)/shard_map/ppermute | solution.py:735
  59.2 4.5 %collective-permute-start.14 = (f32[8,136,128]{2,1,0:T(8,128)S(1)}, f32[8,136,128]{2,1,0:T(8,128)S(1)}, u32[]{:S(2)}, u32[]{:S(2)}) collective-permute-start(f32[8,136,128]{2,1,0:T(8,128)S(1)} %get-tuple-element.136), channel_id=1, source_target_pairs={{0,4},{4,0},{8,12},{12,8},{16,20},{20,16},{24,28},{28,24},{32,36},... | collective-permute-start | bytes 1671176 | tf_op jit(solution)/shard_map/ppermute | solution.py:278
  61.0 6.5 %copy-start.1 = (bf16[16,6,128,128]{3,2,1,0:T(8,128)(2,1)S(1)}, bf16[16,6,128,128]{3,2,1,0:T(8,128)(2,1)}, u32[]{:S(2)}) copy-start(bf16[16,6,128,128]{3,2,1,0:T(8,128)(2,1)} %copy-done) | copy-start | bytes 9437188
  64.3 9.0 %collective-permute-start.15 = (f32[2,136,128]{2,1,0:T(8,128)S(1)}, f32[2,136,128]{2,1,0:T(8,128)S(1)}, u32[]{:S(2)}, u32[]{:S(2)}) collective-permute-start(f32[2,136,128]{2,1,0:T(8,128)S(1)} %get-tuple-element.138), channel_id=1, source_target_pairs={{0,8},{4,12},{8,16},{12,20},{16,24},{20,28},{24,0},{28,4},{32,40},... | collective-permute-start | bytes 417800 | tf_op jit(solution)/shard_map/ppermute | solution.py:280
  64.9 9.2 %collective-permute-start.16 = (f32[2,136,128]{2,1,0:T(8,128)S(1)}, f32[2,136,128]{2,1,0:T(8,128)S(1)}, u32[]{:S(2)}, u32[]{:S(2)}) collective-permute-start(f32[2,136,128]{2,1,0:T(8,128)S(1)} %get-tuple-element.139), channel_id=1, source_target_pairs={{0,16},{4,20},{8,24},{12,28},{16,0},{20,4},{24,8},{28,12},{32,48},... | collective-permute-start | bytes 417800 | tf_op jit(solution)/shard_map/ppermute | solution.py:280
  67.3 6.9 %collective-permute-start.17 = (f32[2,136,128]{2,1,0:T(8,128)S(1)}, f32[2,136,128]{2,1,0:T(8,128)S(1)}, u32[]{:S(2)}, u32[]{:S(2)}) collective-permute-start(f32[2,136,128]{2,1,0:T(8,128)S(1)} %get-tuple-element.140), channel_id=1, source_target_pairs={{0,24},{4,28},{8,0},{12,4},{16,8},{20,12},{24,16},{28,20},{32,56},... | collective-permute-start | bytes 417800 | tf_op jit(solution)/shard_map/ppermute | solution.py:280
  74.8 9.7 %collective-permute-start.18 = (f32[2,136,128]{2,1,0:T(8,128)S(1)}, f32[2,136,128]{2,1,0:T(8,128)S(1)}, u32[]{:S(2)}, u32[]{:S(2)}) collective-permute-start(f32[2,136,128]{2,1,0:T(8,128)S(1)} %get-tuple-element.148.refs_0_), channel_id=1, source_target_pairs={{0,32},{4,36},{8,40},{12,44},{16,48},{20,52},{24,56},{28,60},{32,6... | collective-permute-start | bytes 417800 | tf_op jit(solution)/shard_map/ppermute | solution.py:286
  75.5 9.0 %collective-permute-start.19 = (f32[2,136,128]{2,1,0:T(8,128)S(1)}, f32[2,136,128]{2,1,0:T(8,128)S(1)}, u32[]{:S(2)}, u32[]{:S(2)}) collective-permute-start(f32[2,136,128]{2,1,0:T(8,128)S(1)} %get-tuple-element.148.refs_0_), channel_id=1, source_target_pairs={{0,64},{4,68},{8,72},{12,76},{16,80},{20,84},{24,88},{28,92},{32,9... | collective-permute-start | bytes 417800 | tf_op jit(solution)/shard_map/ppermute | solution.py:286
  78.0 6.6 %collective-permute-start.20 = (f32[2,136,128]{2,1,0:T(8,128)S(1)}, f32[2,136,128]{2,1,0:T(8,128)S(1)}, u32[]{:S(2)}, u32[]{:S(2)}) collective-permute-start(f32[2,136,128]{2,1,0:T(8,128)S(1)} %get-tuple-element.148.refs_0_), channel_id=1, source_target_pairs={{0,96},{4,100},{8,104},{12,108},{16,112},{20,116},{24,120},{28,124... | collective-permute-start | bytes 417800 | tf_op jit(solution)/shard_map/ppermute | solution.py:286
  85.2 8.3 %collective-permute-start.21 = (f32[2,136,128]{2,1,0:T(8,128)S(1)}, f32[2,136,128]{2,1,0:T(8,128)S(1)}, u32[]{:S(2)}, u32[]{:S(2)}) collective-permute-start(f32[2,136,128]{2,1,0:T(8,128)S(1)} %get-tuple-element.162), channel_id=1, source_target_pairs={{0,8},{4,12},{8,16},{12,20},{16,24},{20,28},{24,0},{28,4},{32,40},... | collective-permute-start | bytes 417800 | tf_op jit(solution)/shard_map/ppermute | solution.py:292
  86.9 7.6 %collective-permute-start.22 = (f32[2,136,128]{2,1,0:T(8,128)S(1)}, f32[2,136,128]{2,1,0:T(8,128)S(1)}, u32[]{:S(2)}, u32[]{:S(2)}) collective-permute-start(f32[2,136,128]{2,1,0:T(8,128)S(1)} %get-tuple-element.163), channel_id=1, source_target_pairs={{0,16},{4,20},{8,24},{12,28},{16,0},{20,4},{24,8},{28,12},{32,48},... | collective-permute-start | bytes 417800 | tf_op jit(solution)/shard_map/ppermute | solution.py:292
  89.4 5.1 %collective-permute-start.23 = (f32[2,136,128]{2,1,0:T(8,128)S(1)}, f32[2,136,128]{2,1,0:T(8,128)S(1)}, u32[]{:S(2)}, u32[]{:S(2)}) collective-permute-start(f32[2,136,128]{2,1,0:T(8,128)S(1)} %get-tuple-element.164), channel_id=1, source_target_pairs={{0,24},{4,28},{8,0},{12,4},{16,8},{20,12},{24,16},{28,20},{32,56},... | collective-permute-start | bytes 417800 | tf_op jit(solution)/shard_map/ppermute | solution.py:292
  95.2 5.4 %collective-permute-start.24 = (f32[8,136,128]{2,1,0:T(8,128)S(1)}, f32[8,136,128]{2,1,0:T(8,128)S(1)}, u32[]{:S(2)}, u32[]{:S(2)}) collective-permute-start(f32[8,136,128]{2,1,0:T(8,128)S(1)} %get-tuple-element.165), channel_id=1, source_target_pairs={{0,4},{4,0},{8,12},{12,8},{16,20},{20,16},{24,28},{28,24},{32,36},... | collective-permute-start | bytes 1671176 | tf_op jit(solution)/shard_map/ppermute | solution.py:297
